TPU v7x, 32 devices: a whole 2x2x4 slice. The times are simulated.
32 devices in a mesh: cfg: 2 (over core), vox: 8 (over z, x), head: 2 (over y).
Axes of the slice: x: 2, y: 2, z: 4, core: 2. Of those that a mesh axis runs over, the one named last changes fastest.
Arguments:
- x_latent: bfloat16 [6144, 1024], P(('cfg', 'vox')), may hold values from -6 to 6
- windows: int32 [6144], P(('cfg', 'vox')), may hold values from 0 to 15, as said below
- coords: int32 [3, 6144], P(None, ('cfg', 'vox')), may hold values from 0 to 63
- modulation: float32 [3, 3, 1024], replicated, may hold values from -3 to 3
- w_qkv: bfloat16 [1024, 3, 1024], P(None, None, 'head'), may hold values from -0.1875 to 0.1875
- w_out: bfloat16 [1024, 1024], P('head'), may hold values from -0.1875 to 0.1875
- qk_gain: float32 [2, 1024], P(None, 'head'), may hold values from 0.5 to 8
- guidance: float32 [2], replicated, may hold values from 1.5 to 7.5
Outputs:
- guided: bfloat16 [6144, 1024], P(('cfg', 'vox'), 'head')
Inputs may be any that keep to these rules, and one draw needn't show every extreme that they name: `windows`: the voxels of one device (aligned blocks of 384) name each window at most 32 times; in every draw one window is named exactly 32 times by every block, so it fills all 512 slots.
All inputs are finite; a program needn't handle non-finite values.
Results may differ from a plain program's by a relative error of at most 0.0045.
The roundings to bfloat16 on the way count: a program that leaves them out, or rounds other values in their place, can miss the bound.
Values may be sent and summed in bfloat16 or wider, within the bound.
No kernel may reach another device: no remote copies, remote signals or barrier semaphores. Data moves between devices by JAX's collectives and lax.ppermute only.
A program may use at most 384 MiB of HBM per device.

v0:
```python
import math

import jax
import jax.numpy as jnp
from jax import lax
from jax.sharding import PartitionSpec as P

HEADS = 16
SLOTS = 512


def position_table(coords, model_width):
    freq_count = model_width // 3 // 2
    frequency = 1.0 / 10000.0 ** (jnp.arange(freq_count, dtype=jnp.float32) / freq_count)
    angles = coords.astype(jnp.float32)[:, :, None] * frequency[None, None, :]
    embedding = jnp.concatenate([jnp.sin(angles), jnp.cos(angles)], axis=2)
    embedding = jnp.transpose(embedding, (1, 0, 2)).reshape(coords.shape[1], 6 * freq_count)
    padding = jnp.zeros((coords.shape[1], model_width - 6 * freq_count), jnp.float32)
    return jnp.concatenate([embedding, padding], axis=1)


def modulate(hidden, modulation):
    centred = hidden - jnp.mean(hidden, axis=1, keepdims=True)
    spread = jnp.mean(centred * centred, axis=1, keepdims=True)
    normal = centred * lax.rsqrt(spread + 1e-06)
    return (normal[None] * (1.0 + modulation[:, 1, None, :]) + modulation[:, 0, None, :]).astype(
        jnp.bfloat16
    )


def head_norm(projected, gain_row, head_size):
    shaped = projected.reshape(projected.shape[:-1] + (projected.shape[-1] // head_size, head_size))
    scale_rms = lax.rsqrt(jnp.mean(shaped * shaped, axis=-1, keepdims=True) + 1e-06)
    return (shaped * scale_rms).reshape(projected.shape) * gain_row


def on_device(x_latent, windows, coords, modulation, w_qkv, w_out, qk_gain, guidance):
    voxels, model_width = x_latent.shape
    group = w_qkv.shape[2]
    head_size = model_width // HEADS
    head_count = group // head_size
    branches = modulation.shape[0]
    senders = lax.axis_size(("cfg", "vox"))
    capacity = SLOTS // senders
    hidden = x_latent.astype(jnp.float32) + position_table(coords, model_width)
    normed = modulate(hidden, modulation)
    projected = jnp.einsum(
        "bvd,dk->vbk",
        normed,
        w_qkv.reshape(model_width, 3 * group),
        preferred_element_type=jnp.float32,
    )
    query_rows = head_norm(projected[:, :, :group], qk_gain[0], head_size).astype(jnp.bfloat16)
    key_rows = head_norm(projected[:, :, group : 2 * group], qk_gain[1], head_size).astype(
        jnp.bfloat16
    )
    value_rows = projected[:, :, 2 * group :].astype(jnp.bfloat16)
    payload = jnp.concatenate([query_rows, key_rows, value_rows], axis=2).reshape(
        voxels, branches * 3 * group
    )
    onehot = (windows[:, None] == jnp.arange(senders, dtype=jnp.int32)[None, :]).astype(jnp.int32)
    rank_in = jnp.sum((jnp.cumsum(onehot, axis=0) - onehot) * onehot, axis=1)
    placed = windows * capacity + rank_in
    placing = (placed[None, :] == jnp.arange(SLOTS, dtype=jnp.int32)[:, None]).astype(jnp.bfloat16)
    outgoing = jnp.dot(placing, payload, preferred_element_type=jnp.float32).astype(jnp.bfloat16)
    outgoing = outgoing.reshape(senders, capacity, branches * 3 * group)
    counts = jnp.sum(onehot, axis=0).astype(jnp.bfloat16).reshape(senders, 1)
    direct_rows, direct_counts = (
        lax.all_to_all(outgoing, ("cfg", "vox"), split_axis=0, concat_axis=0, tiled=True),
        lax.all_to_all(counts, ("cfg", "vox"), split_axis=0, concat_axis=0, tiled=True),
    )
    incoming = direct_rows.reshape(SLOTS, branches, 3 * group)
    arrived = direct_counts.reshape(senders)
    slot_number = jnp.arange(SLOTS, dtype=jnp.int32)
    owner_table = (
        (slot_number // capacity)[:, None] == jnp.arange(senders, dtype=jnp.int32)[None, :]
    ).astype(jnp.float32)
    slot_limit = jnp.sum(owner_table * arrived.astype(jnp.float32)[None, :], axis=1)
    live_slot = (slot_number % capacity).astype(jnp.float32) < slot_limit
    query_win = incoming[:, :, :group].reshape(SLOTS, branches, head_count, head_size)
    key_win = incoming[:, :, group : 2 * group].reshape(SLOTS, branches, head_count, head_size)
    value_win = incoming[:, :, 2 * group :].reshape(SLOTS, branches, head_count, head_size)
    scores = jnp.einsum(
        "qbhd,kbhd->bhqk", query_win, key_win, preferred_element_type=jnp.float32
    ) * (1.0 / math.sqrt(head_size))
    scores = jnp.where(live_slot[None, None, None, :], scores, -1e30)
    highest = jnp.max(scores, axis=3, keepdims=True)
    weights = jnp.exp(scores - highest)
    attend = (weights / jnp.sum(weights, axis=3, keepdims=True)).astype(jnp.bfloat16)
    mixed = jnp.einsum(
        "bhqk,kbhd->qbhd", attend, value_win, preferred_element_type=jnp.float32
    ).astype(jnp.bfloat16)
    mixed = mixed.reshape(senders, capacity, branches * group)
    back_rows = lax.all_to_all(mixed, ("cfg", "vox"), split_axis=0, concat_axis=0, tiled=True)
    back_rows = back_rows.reshape(SLOTS, branches, group)
    returned = jnp.einsum(
        "sv,sbg->vbg", placing, back_rows, preferred_element_type=jnp.float32
    ).astype(jnp.bfloat16)
    partial_value = jnp.einsum("vbg,gd->bvd", returned, w_out, preferred_element_type=jnp.float32)
    image_scale = guidance[0]
    text_scale = guidance[1]
    coefficients = jnp.stack([1.0 - image_scale, image_scale - text_scale, text_scale])
    branch_weights = coefficients[:, None] * modulation[:, 2, :]
    column_share = model_width // lax.axis_size("head")
    head_slot = lax.axis_index("head")
    residual = lax.dynamic_slice_in_dim(hidden, head_slot * column_share, column_share, 1)
    residual = residual * jnp.sum(coefficients)
    guided_term = jnp.einsum("bvd,bd->vd", partial_value, branch_weights)
    summed = lax.psum_scatter(guided_term, "head", scatter_dimension=1, tiled=True)
    guided = residual + summed
    return guided.astype(jnp.bfloat16)


def solution(mesh):
    placed = (
        P(("cfg", "vox"), None),
        P(("cfg", "vox")),
        P(None, ("cfg", "vox")),
        P(),
        P(None, None, "head"),
        P("head", None),
        P(None, "head"),
        P(),
    )
    return jax.shard_map(
        on_device, mesh=mesh, in_specs=placed, out_specs=P(("cfg", "vox"), "head"), check_vma=False
    )
```

profile of v0, /device:TPU:0, one launch (start us, length us, event | category | flops | bytes accessed | tf_op | source)
XLA Modules:
  0.0 351.5 jit_solution(2051910473007351559)
XLA Ops:
  6.5 0.0 copy-start
  6.5 0.8 fusion.35
  7.3 0.9 reduce-window.6
  8.2 0.2 slice_reduce_fusion
  8.4 0.9 convert_reduce_fusion
  9.3 0.7 copy.77
  10.0 7.4 %all-to-all-start.1 = ((bf16[16,1,1]{2,1,0:T(2,128)(2,1)}), bf16[16,1,1]{2,1,0:T(2,128)(2,1)S(1)}, u32[]{:S(2)}, u32[]{:S(2)}) async-start(bf16[16,1,1]{2,1,0:T(2,128)(2,1)} %copy.77), calls=%async_computation.1 | async-start | bytes 16384 | tf_op jit(solution)/shard_map/all_to_all | solution.py:70
  17.4 0.7 convert_element_type.75
  18.1 2.9 multiply_sine_fusion
  21.0 1.3 maximum_bitcast_fusion
  22.2 2.6 reshape.148
  24.8 0.0 copy-done.3
  24.8 0.4 copy.66
  25.2 1.6 fusion.51
  26.8 0.2 multiply_reduce_fusion.1
  27.1 1.3 subtract_multiply_fusion
  28.4 3.0 copy.68
  31.4 0.0 copy-done.4
  31.4 4.7 %copy.69 = bf16[1024,3,512]{0,2,1:T(8,128)(2,1)} copy(bf16[1024,3,512]{2,0,1:T(8,128)(2,1)} %param.12) | data formatting | bytes 6291456 | tf_op args[4]
  36.1 6.3 %convolution_bitcast_fusion = f32[384,3,1536]{2,0,1:T(8,128)S(1)} fusion(bf16[1024,1536,1]{0,1,2:T(8,128)(2,1)} %bitcast.81, f32[3,1024]{1,0:T(4,128)S(1)} %get-tuple-element.25, f32[3,1024]{1,0:T(4,128)S(1)} %get-tuple-element.26, f32[384,1024]{1,0:T(8,128)} %copy.68), kind=kOutput, calls=%fused_computation.12 | convolution fusion | flops 3627417600 | bytes 11821056 | tf_op jit(solution)/shard_map/bvd,dk->vbk/dot_general | solution.py:47
  42.4 3.1 slice_multiply_fusion.1
  45.5 1.3 copy-done.1
  46.8 1.2 slice.75
  48.0 3.1 copy.71
  51.1 1.9 bitcast_reduce_fusion.1
  53.0 1.7 mul.153
  54.7 3.1 copy.72
  57.8 3.1 copy.73
  61.0 1.9 bitcast_reduce_fusion
  62.8 1.7 mul.161
  64.5 3.1 copy.74
  67.7 0.0 copy-done.6
  67.7 5.1 %multiply_convert_fusion.1 = (bf16[384,3,512]{2,0,1:T(8,128)(2,1)S(1)}, bf16[384,3,512]{2,0,1:T(8,128)(2,1)S(1)}) fusion(f32[384,3,512]{2,0,1:T(8,128)} %copy.72, f32[384,3,1536]{2,0,1:T(8,128)} %copy-done.1, f32[512]{0:T(512)S(1)} %bitcast.89, f32[512]{0:T(512)S(1)} %bitcast.90, f32[384,3,512]{2,0,1:T(8,128)} %copy.74), kind=kLoop, calls=%fused_computation.19 | loop fusion | flops 3538944 | bytes 11800576 | tf_op jit(solution)/shard_map/convert_element_type | solution.py:53
  72.8 0.0 copy-done.2
  72.8 1.9 pad_maximum_fusion
  74.7 6.0 %copy.75 = bf16[384,3,1536]{0,2,1:T(8,128)(2,1)} copy(bf16[384,3,1536]{2,0,1:T(8,128)(2,1)} %pad_maximum_fusion) | data formatting | bytes 7077888 | tf_op jit(solution)/shard_map/concatenate | solution.py:58
  80.7 6.5 %convolution_convert_fusion = bf16[512,4608]{1,0:T(8,128)(2,1)} fusion(bf16[384,4608]{0,1:T(8,128)(2,1)} %bitcast.80, s32[384]{0:T(512)S(1)} %multiply_add_fusion), kind=kOutput, calls=%fused_computation.9 | convolution fusion | flops 1814691840 | bytes 8259072 | tf_op jit(solution)/shard_map/dot_general | solution.py:65
  87.2 0.0 all-to-all-done.1
  87.2 6.0 %all-to-all-start = ((bf16[16,32,4608]{2,1,0:T(8,128)(2,1)}), bf16[16,32,4608]{2,1,0:T(8,128)(2,1)}, u32[]{:S(2)}, u32[]{:S(2)}) async-start(bf16[16,32,4608]{2,1,0:T(8,128)(2,1)} %bitcast.79), calls=%async_computation | async-start | bytes 9437184 | tf_op jit(solution)/shard_map/all_to_all | solution.py:69
  93.3 0.2 convert_reduce_fusion.1
  93.5 0.1 select_reduce_fusion
  93.6 100.0 %all-to-all-done = bf16[16,32,4608]{2,1,0:T(8,128)(2,1)} async-done(((bf16[16,32,4608]{2,1,0:T(8,128)(2,1)}), bf16[16,32,4608]{2,1,0:T(8,128)(2,1)}, u32[]{:S(2)}, u32[]{:S(2)}) %all-to-all-start) | async-done | bytes 4718624 | tf_op jit(solution)/shard_map/all_to_all | solution.py:69
  193.6 11.8 %reshape.153 = bf16[512,3,1536]{2,1,0:T(4,128)(2,1)} reshape(bf16[16,32,4608]{2,1,0:T(8,128)(2,1)} %all-to-all-done) | data formatting | bytes 9437184 | tf_op jit(solution)/shard_map/reshape | solution.py:72
  205.5 5.4 %fusion.52 = (bf16[512,3,512]{2,1,0:T(4,128)(2,1)}, bf16[512,3,512]{2,1,0:T(4,128)(2,1)}, bf16[512,3,512]{2,1,0:T(4,128)(2,1)}) fusion(bf16[512,3,1536]{2,1,0:T(4,128)(2,1)} %reshape.153), kind=kLoop, calls=%fused_computation.87 | loop fusion | bytes 9437184 | tf_op jit(solution)/shard_map/slice | solution.py:81
  210.9 4.1 %copy.78 = bf16[512,3,512]{0,2,1:T(8,128)(2,1)} copy(bf16[512,3,512]{2,1,0:T(4,128)(2,1)} %get-tuple-element.14) | data formatting | bytes 3145728 | tf_op jit(solution)/shard_map/slice | solution.py:80
  215.0 4.1 %copy.79 = bf16[512,3,512]{0,2,1:T(8,128)(2,1)} copy(bf16[512,3,512]{2,1,0:T(4,128)(2,1)} %get-tuple-element.13) | data formatting | bytes 3145728 | tf_op jit(solution)/shard_map/slice | solution.py:81
  219.1 4.1 %copy.76 = bf16[512,3,512]{0,2,1:T(8,128)(2,1)} copy(bf16[512,3,512]{2,1,0:T(4,128)(2,1)} %get-tuple-element.15) | data formatting | bytes 3145728 | tf_op jit(solution)/shard_map/slice | solution.py:82
  223.2 10.2 %fusion.55 = f32[3,8,512]{2,1,0:T(8,128)S(1)} fusion(pred[512]{0:T(512)(128)(4,1)S(1)} %fusion.38, bf16[512,3,8,64]{0,3,2,1:T(8,128)(2,1)} %bitcast.82, bf16[512,3,8,64]{0,3,2,1:T(8,128)(2,1)} %bitcast.84), kind=kOutput, calls=%fused_computation.90 | convolution fusion | flops 830472704 | bytes 3195392 | tf_op jit(solution)/shard_map/sub | solution.py:88
  233.3 13.6 %fusion.17 = bf16[512,3,8,64]{0,3,2,1:T(8,128)(2,1)} fusion(bf16[512,3,8,64]{0,3,2,1:T(8,128)(2,1)} %bitcast.86, f32[3,8,512]{2,1,0:T(8,128)S(1)} %fusion.55, pred[512]{0:T(512)(128)(4,1)S(1)} %fusion.38, bf16[512,3,8,64]{0,3,2,1:T(8,128)(2,1)} %bitcast.83, bf16[512,3,8,64]{0,3,2,1:T(8,128)(2,1)} %bitcast.85), kind=kOutput, calls=%fused_computation.32 | convolution fusion | flops 1642869248 | bytes 6341120 | tf_op jit(solution)/shard_map/bhqk,kbhd->qbhd/dot_general | solution.py:90
  246.9 5.0 %copy.81 = bf16[512,3,8,64]{3,2,1,0:T(8,128)(2,1)} copy(bf16[512,3,8,64]{0,3,2,1:T(8,128)(2,1)} %fusion.17) | data formatting | bytes 3145728 | tf_op jit(solution)/shard_map/convert_element_type | solution.py:92
  251.9 5.3 %reshape.157 = bf16[16,32,1536]{2,1,0:T(8,128)(2,1)} reshape(bf16[512,3,8,64]{3,2,1,0:T(8,128)(2,1)} %copy.81) | data formatting | bytes 3145728 | tf_op jit(solution)/shard_map/reshape | solution.py:93
  257.3 8.7 %all-to-all-start.2 = ((bf16[16,32,1536]{2,1,0:T(8,128)(2,1)}), bf16[16,32,1536]{2,1,0:T(8,128)(2,1)}, u32[]{:S(2)}, u32[]{:S(2)}) async-start(bf16[16,32,1536]{2,1,0:T(8,128)(2,1)} %reshape.157), calls=%async_computation.2 | async-start | bytes 3145728 | tf_op jit(solution)/shard_map/all_to_all | solution.py:94
  265.9 0.0 reduce-scatter.2.cloned.1.call-start
  266.0 0.6 fusion.54
  268.5 0.7 pad_maximum_fusion.1
  269.2 0.1 fusion.36
  269.3 33.7 %all-to-all-done.2 = bf16[16,32,1536]{2,1,0:T(8,128)(2,1)} async-done(((bf16[16,32,1536]{2,1,0:T(8,128)(2,1)}), bf16[16,32,1536]{2,1,0:T(8,128)(2,1)}, u32[]{:S(2)}, u32[]{:S(2)}) %all-to-all-start.2) | async-done | bytes 1572896 | tf_op jit(solution)/shard_map/all_to_all | solution.py:94
  303.0 5.6 %reshape.158 = bf16[512,3,512]{2,1,0:T(4,128)(2,1)} reshape(bf16[16,32,1536]{2,1,0:T(8,128)(2,1)} %all-to-all-done.2) | data formatting | bytes 3145728 | tf_op jit(solution)/shard_map/reshape | solution.py:95
  308.6 5.0 %multiply_reduce_fusion = f32[1024,384]{0,1:T(8,128)} fusion(f32[1024,3]{0,1:T(4,128)S(1)} %fusion.36, bf16[512,1024]{1,0:T(8,128)(2,1)S(1)} %copy-done, bf16[512,3,512]{2,1,0:T(4,128)(2,1)} %reshape.158, s32[384]{0:T(512)S(1)} %multiply_add_fusion), kind=kOutput, calls=%fused_computation.10 | convolution fusion | flops 1814691840 | bytes 4208128 | tf_op jit(solution)/shard_map/vbg,gd->bvd/dot_general | solution.py:99
  313.6 3.0 copy.92
  316.7 0.0 reduce-scatter.2.cloned.1.call-update
  317.3 25.1 %reduce-scatter.2.cloned.1.call-done = f32[384,512]{0,1:T(8,128)} async-done(((f32[384,1024]{0,1:T(8,128)}), f32[384,512]{0,1:T(8,128)}) %reduce-scatter.2.cloned.1.call-update) | async-done | bytes 786448 | tf_op jit(solution)/shard_map/reduce_scatter | solution.py:109
  342.5 1.2 add_convert_fusion.2
  343.7 0.9 copy.83
  (23 shorter events, 0.2 us)
Async XLA Ops:
  6.5 302.1 %copy-start = (bf16[512,1024]{1,0:T(8,128)(2,1)S(1)}, bf16[512,1024]{1,0:T(8,128)(2,1)}, u32[]{:S(2)}) copy-start(bf16[512,1024]{1,0:T(8,128)(2,1)} %param.13) | copy-start | bytes 3145732
  10.0 77.2 %all-to-all-start.1 = ((bf16[16,1,1]{2,1,0:T(2,128)(2,1)}), bf16[16,1,1]{2,1,0:T(2,128)(2,1)S(1)}, u32[]{:S(2)}, u32[]{:S(2)}) async-start(bf16[16,1,1]{2,1,0:T(2,128)(2,1)} %copy.77), calls=%async_computation.1 | async-start | bytes 16384 | tf_op jit(solution)/shard_map/all_to_all | solution.py:70
  22.2 2.6 copy-start.3
  28.4 3.0 copy-start.4
  42.4 4.4 %copy-start.1 = (f32[384,3,1536]{2,0,1:T(8,128)}, f32[384,3,1536]{2,0,1:T(8,128)S(1)}, u32[]{:S(2)}) copy-start(f32[384,3,1536]{2,0,1:T(8,128)S(1)} %convolution_bitcast_fusion) | copy-start | bytes 21233668
  64.5 3.2 copy-start.6
  67.7 5.2 %copy-start.2 = (bf16[384,3,512]{2,0,1:T(8,128)(2,1)S(1)}, bf16[384,3,512]{2,0,1:T(8,128)(2,1)}, u32[]{:S(2)}) copy-start(bf16[384,3,512]{2,0,1:T(8,128)(2,1)} %slice.75) | copy-start | bytes 3538948
  74.7 6.0 %copy-start.5 = (s32[384]{0:T(512)S(1)}, s32[384]{0:T(512)}, u32[]{:S(2)}) copy-start(s32[384]{0:T(512)} %param.9) | copy-start | bytes 4612
  87.2 106.4 %all-to-all-start = ((bf16[16,32,4608]{2,1,0:T(8,128)(2,1)}), bf16[16,32,4608]{2,1,0:T(8,128)(2,1)}, u32[]{:S(2)}, u32[]{:S(2)}) async-start(bf16[16,32,4608]{2,1,0:T(8,128)(2,1)} %bitcast.79), calls=%async_computation | async-start | bytes 9437184 | tf_op jit(solution)/shard_map/all_to_all | solution.py:69
  257.3 8.7 %copy-start.7 = (f32[2]{0:T(128)S(1)}, f32[2]{0:T(128)}, u32[]{:S(2)}) copy-start(f32[2]{0:T(128)} %param.15) | copy-start | bytes 28
  257.3 45.8 %all-to-all-start.2 = ((bf16[16,32,1536]{2,1,0:T(8,128)(2,1)}), bf16[16,32,1536]{2,1,0:T(8,128)(2,1)}, u32[]{:S(2)}, u32[]{:S(2)}) async-start(bf16[16,32,1536]{2,1,0:T(8,128)(2,1)} %reshape.157), calls=%async_computation.2 | async-start | bytes 3145728 | tf_op jit(solution)/shard_map/all_to_all | solution.py:94
  265.9 76.5 %reduce-scatter.2.cloned.1.call-start = ((), (), s32[]{:S(2)}) async-start(), calls=%async_computation.4 | async-start | bytes 2359296 | tf_op jit(solution)/shard_map/reduce_scatter | solution.py:109
Sparse Core Ops, SparseCore 0:
  316.8 25.5 reduce-scatter.1
where the time goes:
time: 353 us; the launch traced here: 351 us
  waiting for transfers between devices  159 us (45%)
  local copies, waits for them, and re-layouts  86 us (24%)
  matrix products  41.5 us (12%)
  other arithmetic  26.8 us (8%)
  starting transfers between devices  22.1 us (6%)
  between operations  16.1 us (5%)
    all_to_all x1, waiting for transfers between devices, on_device(): lax.all_to_all(outgoing, ('cfg', 'vox'), split_axis=0, concat_axis=0, til...  100 us
    all_to_all x1, waiting for transfers between devices, on_device(): lax.all_to_all(mixed, ('cfg', 'vox'), split_axis=0, concat_axis=0, tiled=...  33.7 us
    reduce_scatter x1, waiting for transfers between devices, on_device(): lax.psum_scatter(guided_term, 'head', scatter_dimension=1, tiled=True)  25.1 us
    dot_general x1, matrix products, on_device(): jnp.einsum('bhqk,kbhd->qbhd', attend, value_win, preferred_element_type=j...  13.6 us
    reshape x1, local copies, waits for them, and re-layouts, on_device(): incoming = direct_rows.reshape(SLOTS, branches, 3 * group)  11.8 us
    sub x1, matrix products, on_device(): weights = jnp.exp(scores - highest)  10.2 us
    mul x4, local copies, waits for them, and re-layouts, head_norm(): return (shaped * scale_rms).reshape(projected.shape) * gain_row  9.59 us
    slice x2, local copies, waits for them, and re-layouts, on_device(): incoming[:, :, group:2 * group]  9.48 us
  transfers between devices with their start and end apart: 4, of which 3 were waited for; matrix products, arithmetic and copies ran while one was open for 20% of the time, Pallas kernels for 0%

commit v1 on v0

v1 whole, which is shorter than its diff:
```python
import functools

import jax
import jax.numpy as jnp
from jax import lax
from jax.experimental import pallas as pl
from jax.experimental.pallas import tpu as pltpu
from jax.sharding import PartitionSpec as P

HEADS = 16
SLOTS = 512
GRID = 64
EXTRA = 128
BF16 = jnp.bfloat16
F32 = jnp.float32
VMEM = pl.BlockSpec(memory_space=pltpu.VMEM)
SMEM = pl.BlockSpec(memory_space=pltpu.SMEM)
NT = (((1,), (1,)), ((), ()))
TN = (((0,), (0,)), ((), ()))


def params(megabytes):
    return pltpu.CompilerParams(vmem_limit_bytes=megabytes * 1024 * 1024)


def iota(shape, dim):
    return lax.broadcasted_iota(jnp.int32, shape, dim)


def dot(a, b):
    return jnp.dot(a, b, preferred_element_type=F32)


def position_parts(model_width):
    freq_count = model_width // 3 // 2
    frequency = 1.0 / 10000.0 ** (jnp.arange(freq_count, dtype=F32) / freq_count)
    angles = jnp.arange(GRID, dtype=F32)[:, None] * frequency[None, :]
    block = jnp.concatenate([jnp.sin(angles), jnp.cos(angles)], axis=1)
    width = 2 * freq_count
    rows = [
        jnp.pad(block, ((0, 0), (c * width, model_width - (c + 1) * width))) for c in range(3)
    ]
    table = jnp.concatenate(rows, axis=0)
    top = lax.reduce_precision(table, 8, 7)
    rest = table - top
    middle = lax.reduce_precision(rest, 8, 7)
    low = rest - middle
    return jnp.concatenate([top, middle, low], axis=0).astype(BF16)


def place_kernel(senders, capacity, windows_ref, coords_ref, x_ref, out_ref, placing_ref):
    windows = windows_ref[...]
    voxels = windows.shape[1]
    width = x_ref.shape[1]
    member = windows == iota((senders, voxels), 0)
    earlier = (iota((voxels, voxels), 0) < iota((voxels, voxels), 1)).astype(F32).astype(BF16)
    member_f = member.astype(F32)
    before = dot(member_f.astype(BF16), earlier)
    rank = jnp.sum(before * member_f, axis=0, keepdims=True).astype(jnp.int32)
    placed = windows * capacity + rank
    placing = (placed == iota((SLOTS, voxels), 0)).astype(F32).astype(BF16)
    placing_ref[...] = placing
    row = iota((EXTRA, voxels), 0)
    extra = jnp.where(row == 3, 1.0, 0.0).astype(F32)
    for c in range(3):
        extra = jnp.where(row == c, coords_ref[c : c + 1, :].astype(F32), extra)
    out_ref[:, :width] = dot(placing, x_ref[...]).astype(BF16)
    out_ref[:, width:] = lax.dot_general(
        placing, extra.astype(BF16), NT, preferred_element_type=F32
    ).astype(BF16)


def attend_branch(normed, normed_q, weight, gain_ref, bias, head_size, att_ref):
    slots, queries = bias.shape[1], att_ref.shape[0]
    group = att_ref.shape[1]
    tile = min(256, group)
    square = (iota((tile, tile), 0) // head_size) == (iota((tile, tile), 1) // head_size)
    same_head = square.astype(F32).astype(BF16)

    def head_norm(rows, gain):
        squares = rows * rows
        top = squares.astype(BF16)
        low = (squares - top.astype(F32)).astype(BF16)
        mean = (dot(top, same_head) + dot(low, same_head)) * (1.0 / head_size)
        return rows * lax.rsqrt(mean + 1e-06) * gain

    lane_head = iota((queries, tile), 1) // head_size
    for start in range(0, group, tile):
        columns = slice(start, start + tile)
        query = head_norm(weight(0, columns, True), gain_ref[0:1, columns])
        key = head_norm(weight(1, columns, False), gain_ref[1:2, columns]).astype(BF16)
        value = weight(2, columns, False).astype(BF16)
        query = query.astype(BF16).astype(F32) * (1.0 / head_size**0.5)
        count = tile // head_size

        def score(head):
            one = jnp.where(lane_head == head, query, 0.0).astype(BF16)
            return lax.dot_general(one, key, NT, preferred_element_type=F32)

        scores = score(0)
        mixed = jnp.zeros((queries, tile), F32)
        for head in range(count):
            following = score(head + 1) if head + 1 < count else None
            step = min(32, queries)
            pieces = []
            for r in range(0, queries, step):
                piece = scores[r : r + step] + bias
                weights = jnp.exp(piece - jnp.max(piece, axis=1, keepdims=True))
                total = jnp.sum(weights, axis=1, keepdims=True)
                pieces.append((weights * (1.0 / total)).astype(BF16))
            attend = jnp.concatenate(pieces, axis=0)
            mixed = jnp.where(lane_head == head, dot(attend, value), mixed)
            scores = following
        att_ref[:, columns] = mixed.astype(BF16)


def own_kernel(
    senders,
    head_size,
    guidance_ref,
    rows_ref,
    table_ref,
    modulation_ref,
    w_ref,
    gain_ref,
    w_out_ref,
    normed_ref,
    normed_q_ref,
    acc_ref,
    bias_ref,
    hidden_ref,
    att_ref,
):
    branches, slots, width = normed_ref.shape
    queries = normed_q_ref.shape[1]
    group = att_ref.shape[1]
    capacity = slots // senders
    share = queries // senders
    first = lax.axis_index("head") * share
    g0, g1 = guidance_ref[0], guidance_ref[1]
    coefficients = (1.0 - g0, g0 - g1, g1)
    total = (coefficients[0] + coefficients[1]) + coefficients[2]

    extra = rows_ref[:, width:]
    pick = ((iota((8, EXTRA), 1) == 3)).astype(F32).astype(BF16)
    live = lax.dot_general(pick, extra, NT, preferred_element_type=F32)
    bias_ref[...] = jnp.where(live > 0.5, 0.0, -1e30)

    spots = extra.astype(F32)
    lane = iota((slots, 3 * GRID), 1)
    wanted = jnp.where(
        lane < GRID,
        spots[:, 0:1],
        jnp.where(lane < 2 * GRID, spots[:, 1:2], spots[:, 2:3]),
    )
    chosen = (wanted == (lane % GRID).astype(F32)).astype(F32).astype(BF16)
    chosen = jnp.concatenate([chosen, chosen, chosen], axis=1)
    hidden_ref[...] = dot(chosen, table_ref[...]) + rows_ref[:, :width].astype(F32)

    chunk = 32

    def normalise(i, carry):
        rows = pl.ds(pl.multiple_of(i * chunk, chunk), chunk)
        hidden = hidden_ref[rows, :]
        centred = hidden - jnp.mean(hidden, axis=1, keepdims=True)
        spread = jnp.mean(centred * centred, axis=1, keepdims=True)
        normal = centred * lax.rsqrt(spread + 1e-06)
        for b in range(branches):
            normed_ref[b, rows, :] = (
                normal * (1.0 + modulation_ref[b, 1:2, :]) + modulation_ref[b, 0:1, :]
            ).astype(BF16)
        return carry

    lax.fori_loop(0, slots // chunk, normalise, 0)

    if share % 16 == 0:
        for s in range(senders):
            source = pl.ds(pl.multiple_of(s * capacity + first, 16), share)
            target = slice(s * share, (s + 1) * share)
            acc_ref[target, :] = hidden_ref[source, :] * total
            for b in range(branches):
                normed_q_ref[b, target, :] = normed_ref[b, source, :]
    else:
        row = iota((queries, slots), 0)
        wanted_slot = (row // share) * capacity + first + row % share
        chooser = (wanted_slot == iota((queries, slots), 1)).astype(F32)
        picked = jnp.dot(
            chooser, hidden_ref[...], preferred_element_type=F32, precision=lax.Precision.HIGHEST
        )
        acc_ref[...] = picked * total
        for b in range(branches):
            normed_q_ref[b] = dot(chooser.astype(BF16), normed_ref[b]).astype(BF16)

    bias = bias_ref[0:1, :]
    g_coefficients = coefficients

    def branch(b, carry):
        def weight(part, columns, is_query):
            source = normed_q_ref[b] if is_query else normed_ref[b]
            place = slice(part * group + columns.start, part * group + columns.stop)
            return dot(source, w_ref[:, place])

        attend_branch(None, None, weight, gain_ref, bias, head_size, att_ref)
        scale = jnp.where(
            b == 0, g_coefficients[0], jnp.where(b == 1, g_coefficients[1], g_coefficients[2])
        )
        acc_ref[...] += dot(att_ref[...], w_out_ref[...]) * (scale * modulation_ref[b, 2:3, :])
        return carry

    lax.fori_loop(0, branches, branch, 0)


def other_kernel(
    head_size,
    out_parts,
    guidance_ref,
    normed_ref,
    normed_q_ref,
    acc_ref,
    bias_ref,
    modulation_ref,
    mine_ref,
    theirs_ref,
    gain_ref,
    out_mine_ref,
    out_theirs_ref,
    out_ref,
    att_ref,
    sum_ref,
):
    branches, slots, width = normed_ref.shape
    group = att_ref.shape[1]
    half = mine_ref.shape[0]
    wide = out_mine_ref.shape[1]
    cfg = lax.axis_index("cfg")
    here = pl.ds(pl.multiple_of(cfg * half, 128), half)
    there = pl.ds(pl.multiple_of((1 - cfg) * half, 128), half)
    out_here = pl.ds(pl.multiple_of(cfg * wide, 128), wide)
    out_there = pl.ds(pl.multiple_of((1 - cfg) * wide, 128), wide)
    g0, g1 = guidance_ref[0], guidance_ref[1]
    bias = bias_ref[0:1, :]
    sum_ref[...] = acc_ref[...]

    def branch(b, carry):
        def weight(part, columns, is_query):
            source = normed_q_ref if is_query else normed_ref
            place = slice(part * group + columns.start, part * group + columns.stop)
            return dot(source[b, :, here], mine_ref[:, place]) + dot(
                source[b, :, there], theirs_ref[:, place]
            )

        attend_branch(None, None, weight, gain_ref, bias, head_size, att_ref)
        scale = jnp.where(b == 0, 1.0 - g0, jnp.where(b == 1, g0 - g1, g1))
        sum_ref[:, out_here] += dot(att_ref[...], out_mine_ref[...]) * (
            scale * modulation_ref[b, 2:3, out_here]
        )
        sum_ref[:, out_there] += dot(att_ref[...], out_theirs_ref[...]) * (
            scale * modulation_ref[b, 2:3, out_there]
        )
        return carry

    lax.fori_loop(0, branches, branch, 0)
    if out_parts is None:
        out_ref[...] = sum_ref[...].astype(out_ref.dtype)
    else:
        senders, heads, share, columns = out_parts
        for h in range(heads):
            piece = sum_ref[:, h * columns : (h + 1) * columns].astype(BF16)
            out_ref[:, h] = piece.reshape(senders, share, columns)


def return_kernel(placing_ref, rows_ref, out_ref):
    out_ref[...] = dot(placing_ref[...], rows_ref[...]).astype(BF16)


def on_device(x_latent, windows, coords, modulation, w_qkv, w_out, qk_gain, guidance):
    voxels, width = x_latent.shape
    group = w_qkv.shape[2]
    head_size = width // HEADS
    branches = modulation.shape[0]
    senders = lax.axis_size(("cfg", "vox"))
    heads = lax.axis_size("head")
    cores = lax.axis_size("cfg")
    capacity = SLOTS // senders
    queries = SLOTS // heads
    share = capacity // heads

    outgoing, placing = pl.pallas_call(
        functools.partial(place_kernel, senders, capacity),
        out_shape=(
            jax.ShapeDtypeStruct((SLOTS, width + EXTRA), BF16),
            jax.ShapeDtypeStruct((SLOTS, voxels), BF16),
        ),
        in_specs=[VMEM] * 3,
        out_specs=(VMEM, VMEM),
        compiler_params=params(24),
        name="place",
    )(windows.reshape(1, voxels), coords, x_latent)
    arrived = lax.all_to_all(
        outgoing.reshape(senders, capacity, width + EXTRA),
        ("cfg", "vox"),
        split_axis=0,
        concat_axis=0,
        tiled=True,
    ).reshape(SLOTS, width + EXTRA)

    core = lax.axis_index("cfg")
    flat = w_qkv.reshape(width, 3 * group)
    half = lax.dynamic_slice_in_dim(flat, core * (width // cores), width // cores, 0)
    out_half = lax.dynamic_slice_in_dim(w_out, core * (width // cores), width // cores, 1)
    swap = [(c, (c + 1) % cores) for c in range(cores)]
    others = []
    for distance in range(1, heads):
        turn = [(h, (h + distance) % heads) for h in range(heads)]
        mine = lax.ppermute(half, "head", turn)
        gain = lax.ppermute(qk_gain, "head", turn)
        out_mine = lax.ppermute(out_half, "head", turn)
        theirs = lax.ppermute(mine, "cfg", swap)
        out_theirs = lax.ppermute(out_mine, "cfg", swap)
        others.append((mine, theirs, gain, out_mine, out_theirs))

    table = position_parts(width)
    normed, normed_q, acc, bias = pl.pallas_call(
        functools.partial(own_kernel, senders, head_size),
        out_shape=(
            jax.ShapeDtypeStruct((branches, SLOTS, width), BF16),
            jax.ShapeDtypeStruct((branches, queries, width), BF16),
            jax.ShapeDtypeStruct((queries, width), F32),
            jax.ShapeDtypeStruct((8, SLOTS), F32),
        ),
        in_specs=[SMEM] + [VMEM] * 6,
        out_specs=(VMEM,) * 4,
        scratch_shapes=[pltpu.VMEM((SLOTS, width), F32), pltpu.VMEM((queries, group), BF16)],
        compiler_params=params(44),
        name="own_heads",
    )(guidance, arrived, table, modulation, flat, qk_gain, w_out)

    for number, (mine, theirs, gain, out_mine, out_theirs) in enumerate(others):
        last = number == len(others) - 1
        parts = None
        shape = jax.ShapeDtypeStruct((queries, width), BF16 if last else F32)
        if last and share % 16 == 0:
            parts = (senders, heads, share, width // heads)
            shape = jax.ShapeDtypeStruct(parts, BF16)
        acc = pl.pallas_call(
            functools.partial(other_kernel, head_size, parts),
            out_shape=shape,
            in_specs=[SMEM] + [VMEM] * 10,
            out_specs=VMEM,
            scratch_shapes=[pltpu.VMEM((queries, group), BF16), pltpu.VMEM((queries, width), F32)],
            compiler_params=params(44),
            name="other_heads",
        )(
            guidance,
            normed,
            normed_q,
            acc,
            bias,
            modulation,
            mine,
            theirs,
            gain,
            out_mine,
            out_theirs,
        )
    if share % 16 != 0:
        acc = acc.reshape(senders, share, heads, width // heads).transpose(0, 2, 1, 3)
    back = lax.all_to_all(
        acc.reshape(senders * heads, share, width // heads),
        ("cfg", "vox", "head"),
        split_axis=0,
        concat_axis=0,
        tiled=True,
    )
    return pl.pallas_call(
        return_kernel,
        out_shape=jax.ShapeDtypeStruct((voxels, width // heads), BF16),
        in_specs=[VMEM] * 2,
        out_specs=VMEM,
        compiler_params=params(24),
        name="return_rows",
    )(placing.T, back.reshape(SLOTS, width // heads))


def solution(mesh):
    placed = (
        P(("cfg", "vox"), None),
        P(("cfg", "vox")),
        P(None, ("cfg", "vox")),
        P(),
        P(None, None, "head"),
        P("head", None),
        P(None, "head"),
        P(),
    )
    return jax.shard_map(
        on_device, mesh=mesh, in_specs=placed, out_specs=P(("cfg", "vox"), "head"), check_vma=False
    )
```

time: 353 us -> 134 us (0.38)
  waiting for transfers between devices: 159 us -> 54.9 us
  local copies, waits for them, and re-layouts: 86 us -> 13.1 us
  Pallas kernels: 0 us -> 47.4 us
  matrix products: 41.5 us -> 0 us
  other arithmetic: 26.8 us -> 0.62 us
  between operations: 16.1 us -> 0.18 us
  starting transfers between devices: 22.1 us -> 17.3 us
    all_to_all x3 -> x2, waiting for transfers between devices: 134 us -> 16.6 us  [the longest x1 16.6 us: on_device(): lax.all_to_all(acc.reshape(senders * heads, share, width // heads), ('cfg...]
    pallas_call x0 -> x4, Pallas kernels: none -> 47.4 us  [the longest x1 23.5 us: on_device(): pl.pallas_call(functools.partial(own_kernel, senders, head_size), out_sha...]
    ppermute x0 -> x5, waiting for transfers between devices: none -> 38.3 us  [the longest x1 25.9 us: on_device(): mine = lax.ppermute(half, 'head', turn)]
    dot_general x4 -> x0, matrix products: 31.4 us -> none  [the longest x1 13.6 us: on_device(): jnp.einsum('bhqk,kbhd->qbhd', attend, value_win, preferred_element_type=j...]
    reduce_scatter x1 -> x0, waiting for transfers between devices: 25.1 us -> none  [on_device(): lax.psum_scatter(guided_term, 'head', scatter_dimension=1, tiled=True)]
    reshape x4 -> x2, local copies, waits for them, and re-layouts: 25.3 us -> 3.18 us  [the longest x1 3.18 us: on_device(): flat = w_qkv.reshape(width, 3 * group)]
    slice x8 -> x0, local copies, waits for them, and re-layouts: 19.7 us -> none  [the longest x2 9.48 us: on_device(): incoming[:, :, group:2 * group]]
    mul x7 -> x0, local copies, waits for them, and re-layouts: 18.9 us -> none  [the longest x4 9.59 us: head_norm(): return (shaped * scale_rms).reshape(projected.shape) * gain_row]
  transfers between devices with their start and end apart: 4 -> 7, of which waited for: 3 -> 3; matrix products, arithmetic and copies ran while one was open for 20% -> 1% of each run, Pallas kernels for 0% -> 19%
where the time goes in v1:
time: 134 us
  waiting for transfers between devices  54.9 us (41%)
  Pallas kernels  47.4 us (35%)
  starting transfers between devices  17.3 us (13%)
  local copies, waits for them, and re-layouts  13.1 us (10%)
    ppermute x1, waiting for transfers between devices, on_device(): mine = lax.ppermute(half, 'head', turn)  25.9 us
    pallas_call x1, Pallas kernels, on_device(): pl.pallas_call(functools.partial(own_kernel, senders, head_size), out_sha...  23.5 us
    pallas_call x1, Pallas kernels, on_device(): pl.pallas_call(functools.partial(other_kernel, head_size, parts), out_sha...  20.8 us
    all_to_all x1, waiting for transfers between devices, on_device(): lax.all_to_all(acc.reshape(senders * heads, share, width // heads), ('cfg...  16.6 us
    ppermute x1, waiting for transfers between devices, on_device(): out_mine = lax.ppermute(out_half, 'head', turn)  12.4 us
    unnamed x23, local copies, waits for them, and re-layouts  8.36 us
    all_to_all x1, starting transfers between devices, on_device(): lax.all_to_all(acc.reshape(senders * heads, share, width // heads), ('cfg...  6.19 us
    all_to_all x1, starting transfers between devices, on_device(): lax.all_to_all(outgoing.reshape(senders, capacity, width + EXTRA), ('cfg'...  6.04 us
  transfers between devices with their start and end apart: 7, of which 3 were waited for; matrix products, arithmetic and copies ran while one was open for 1% of the time, Pallas kernels for 19%

profile of v1, /device:TPU:0, one launch (start us, length us, event | category | flops | bytes accessed | tf_op | source)
XLA Modules:
  0.0 133.5 jit_solution(10584646307699920742)
XLA Ops:
  0.0 4.6 %copy.12 = bf16[1024,3,512]{0,2,1:T(8,128)(2,1)} copy(bf16[1024,3,512]{2,0,1:T(8,128)(2,1)} %param.12) | data formatting | bytes 6291456 | tf_op args[4]
  4.6 3.2 %copy.13.w_ref = bf16[1024,1536]{1,0:T(8,128)(2,1)S(1)} copy(bf16[1024,1536]{0,1:T(8,128)(2,1)} %bitcast.9) | data formatting | bytes 6291456 | tf_op jit(solution)/shard_map/reshape | solution.py:308
  7.8 0.0 copy-start.9
  7.8 0.0 copy-start.10
  7.9 0.0 copy-start.2
  7.9 0.0 copy-start.6
  7.9 1.3 constant_dynamic-slice_fusion.1
  9.2 0.8 copy-done.9
  10.0 3.0 %collective-permute-start = (bf16[512,1536]{1,0:T(8,128)(2,1)}, bf16[512,1536]{1,0:T(8,128)(2,1)}, u32[]{:S(2)}, u32[]{:S(2)}) collective-permute-start(bf16[512,1536]{1,0:T(8,128)(2,1)} %constant_dynamic-slice_fusion.1), channel_id=1, source_target_pairs={{0,1},{1,0},{2,3},{3,2},{4,5},{5,4},{6,7},{7,6},{8,9},{9,8},{10,11... | collective-permute-start | bytes 4718600 | tf_op jit(solution)/shard_map/ppermute | solution.py:315
  13.0 0.0 copy-done.10
  13.0 0.0 copy-done.2
  13.0 0.0 copy-done.6
  13.0 0.0 copy-start.1
  13.0 2.0 %place.1 = (bf16[512,1152]{1,0:T(8,128)(2,1)}, bf16[512,384]{1,0:T(8,128)(2,1)S(1)}) custom-call(s32[1,384]{1,0:T(1,128)S(1)} %reshape.24.windows_ref, s32[3,384]{1,0:T(4,128)S(1)} %copy-done.6, bf16[384,1024]{1,0:T(8,128)(2,1)S(1)} %copy-done.2), custom_call_target="tpu_custom_call" | custom-call | tf_op jit(solution)/shard_map/place/pallas_call | solution.py:288
  15.0 0.0 copy-start.3
  15.0 0.7 copy-done.3
  15.8 0.0 copy-start.7
  15.8 6.0 %all-to-all-start = ((bf16[16,32,1152]{2,1,0:T(8,128)(2,1)}), bf16[16,32,1152]{2,1,0:T(8,128)(2,1)S(1)}, u32[]{:S(2)}, u32[]{:S(2)}) async-start(bf16[16,32,1152]{2,1,0:T(8,128)(2,1)} %bitcast.1), calls=%async_computation | async-start | bytes 2359296 | tf_op jit(solution)/shard_map/all_to_all | solution.py:299
  21.8 25.9 %collective-permute-done.mine_ref = bf16[512,1536]{1,0:T(8,128)(2,1)} collective-permute-done((bf16[512,1536]{1,0:T(8,128)(2,1)}, bf16[512,1536]{1,0:T(8,128)(2,1)}, u32[]{:S(2)}, u32[]{:S(2)}) %collective-permute-start) | collective-permute-done | bytes 1572896 | tf_op jit(solution)/shard_map/ppermute | solution.py:315
  47.7 0.0 collective-permute-start.1
  47.7 0.0 copy-done.1
  47.7 1.8 %collective-permute-start.3 = (bf16[512,512]{1,0:T(8,128)(2,1)S(1)}, bf16[512,512]{1,0:T(8,128)(2,1)}, u32[]{:S(2)}, u32[]{:S(2)}) collective-permute-start(bf16[512,512]{1,0:T(8,128)(2,1)S(1)} %constant_dynamic-slice_fusion), channel_id=1, source_target_pairs={{0,1},{1,0},{2,3},{3,2},{4,5},{5,4},{6,7},{7,6},{8,9},{9,8},{10,11... | collective-permute-start | bytes 1572872 | tf_op jit(solution)/shard_map/ppermute | solution.py:317
  49.5 0.0 copy-done.7
  49.5 0.3 collective-permute-start.2
  49.8 12.4 %collective-permute-done.3.out_mine_ref = bf16[512,512]{1,0:T(8,128)(2,1)} collective-permute-done((bf16[512,512]{1,0:T(8,128)(2,1)S(1)}, bf16[512,512]{1,0:T(8,128)(2,1)}, u32[]{:S(2)}, u32[]{:S(2)}) %collective-permute-start.3) | collective-permute-done | bytes 524320 | tf_op jit(solution)/shard_map/ppermute | solution.py:317
  62.3 0.0 collective-permute-start.4
  62.3 0.3 fusion.3
  62.5 0.1 pad_maximum_fusion.1
  62.6 0.0 copy-start.5
  62.6 0.0 copy-start.8
  62.6 0.2 reduce-precision_convert_fusion.1
  62.8 0.1 pad_maximum_fusion.table_ref
  62.9 0.0 all-to-all-done
  62.9 0.5 copy-done.5
  63.4 0.0 copy-done.8
  63.4 23.5 %own_heads.1 = (bf16[3,512,1024]{2,1,0:T(8,128)(2,1)S(1)}, bf16[3,256,1024]{2,1,0:T(8,128)(2,1)S(1)}, f32[256,1024]{1,0:T(8,128)S(1)}, f32[8,512]{1,0:T(8,128)S(1)}) custom-call(f32[2]{0:T(128)S(1)} %copy-done.8, bf16[512,1152]{1,0:T(8,128)(2,1)S(1)} %bitcast.6, bf16[576,1024]{1,0:T(8,128)(2,1)S(1)} %pad_maximum_fusion.table_ref, ...), custom_call_target="tpu_custom_call" | custom-call | tf_op jit(solution)/shard_map/own_heads/pallas_call | solution.py:323
  87.0 0.0 copy-start
  87.0 1.6 %copy-done = bf16[3,512,1024]{2,1,0:T(8,128)(2,1)} copy-done((bf16[3,512,1024]{2,1,0:T(8,128)(2,1)}, bf16[3,512,1024]{2,1,0:T(8,128)(2,1)S(1)}, u32[]{:S(2)}) %copy-start) | copy-done | bytes 3145752
  88.6 0.0 collective-permute-done.2.gain_ref
  88.6 0.0 collective-permute-done.4.out_theirs_ref
  88.6 0.0 collective-permute-done.1.theirs_ref
  88.6 0.0 copy-start.4
  88.6 20.8 %other_heads.1 = bf16[16,2,16,512]{3,2,1,0:T(8,128)(2,1)} custom-call(f32[2]{0:T(128)S(1)} %copy-done.8, bf16[3,512,1024]{2,1,0:T(8,128)(2,1)} %copy-done, bf16[3,256,1024]{2,1,0:T(8,128)(2,1)S(1)} %get-tuple-element.14.normed_q_ref, f32[256,1024]{1,0:T(8,128)S(1)} %get-tuple-element.15.acc_ref, f32[8,512]{1,0:T(8,128)S(1)} %get-tuple-element.16.bias_ref, ...), custom_call_target="tpu_custom_call" | custom-call | tf_op jit(solution)/shard_map/other_heads/pallas_call | solution.py:345
  109.4 6.2 %all-to-all-start.1 = ((bf16[32,16,512]{2,1,0:T(8,128)(2,1)}), bf16[32,16,512]{2,1,0:T(8,128)(2,1)S(1)}, u32[]{:S(2)}, u32[]{:S(2)}) async-start(bf16[32,16,512]{2,1,0:T(8,128)(2,1)} %bitcast.4), calls=%async_computation.1 | async-start | bytes 1048576 | tf_op jit(solution)/shard_map/all_to_all | solution.py:368
  115.6 0.0 copy-done.4
  115.6 0.2 copy.11
  115.8 16.6 %all-to-all-done.1 = bf16[32,16,512]{2,1,0:T(8,128)(2,1)S(1)} async-done(((bf16[32,16,512]{2,1,0:T(8,128)(2,1)}), bf16[32,16,512]{2,1,0:T(8,128)(2,1)S(1)}, u32[]{:S(2)}, u32[]{:S(2)}) %all-to-all-start.1) | async-done | bytes 524320 | tf_op jit(solution)/shard_map/all_to_all | solution.py:368
  132.4 1.1 return_rows.1
  (3 shorter events, 0.0 us)
Async XLA Ops:
  7.8 2.2 %copy-start.9 = (bf16[1024,1536]{1,0:T(8,128)(2,1)}, bf16[1024,1536]{1,0:T(8,128)(2,1)S(1)}, u32[]{:S(2)}) copy-start(bf16[1024,1536]{1,0:T(8,128)(2,1)S(1)} %copy.13.w_ref) | copy-start | bytes 9437188
  7.8 5.1 %copy-start.10 = (s32[384]{0:T(512)S(1)}, s32[384]{0:T(512)}, u32[]{:S(2)}) copy-start(s32[384]{0:T(512)} %param.9) | copy-start | bytes 4612
  7.9 5.1 %copy-start.2 = (bf16[384,1024]{1,0:T(8,128)(2,1)S(1)}, bf16[384,1024]{1,0:T(8,128)(2,1)}, u32[]{:S(2)}) copy-start(bf16[384,1024]{1,0:T(8,128)(2,1)} %x_ref.1) | copy-start | bytes 2359300
  7.9 5.1 %copy-start.6 = (s32[3,384]{1,0:T(4,128)S(1)}, s32[3,384]{1,0:T(4,128)}, u32[]{:S(2)}) copy-start(s32[3,384]{1,0:T(4,128)} %coords_ref.1) | copy-start | bytes 13828
  10.0 37.7 %collective-permute-start = (bf16[512,1536]{1,0:T(8,128)(2,1)}, bf16[512,1536]{1,0:T(8,128)(2,1)}, u32[]{:S(2)}, u32[]{:S(2)}) collective-permute-start(bf16[512,1536]{1,0:T(8,128)(2,1)} %constant_dynamic-slice_fusion.1), channel_id=1, source_target_pairs={{0,1},{1,0},{2,3},{3,2},{4,5},{5,4},{6,7},{7,6},{8,9},{9,8},{10,11... | collective-permute-start | bytes 4718600 | tf_op jit(solution)/shard_map/ppermute | solution.py:315
  13.0 34.7 %copy-start.1 = (bf16[512,1024]{1,0:T(8,128)(2,1)S(1)}, bf16[512,1024]{1,0:T(8,128)(2,1)}, u32[]{:S(2)}) copy-start(bf16[512,1024]{1,0:T(8,128)(2,1)} %w_out_ref.1) | copy-start | bytes 3145732
  15.0 0.7 copy-start.3
  15.8 33.8 %copy-start.7 = (f32[2,512]{1,0:T(2,128)S(1)}, f32[2,512]{1,0:T(2,128)}, u32[]{:S(2)}) copy-start(f32[2,512]{1,0:T(2,128)} %gain_ref.1) | copy-start | bytes 12292
  15.8 47.2 %all-to-all-start = ((bf16[16,32,1152]{2,1,0:T(8,128)(2,1)}), bf16[16,32,1152]{2,1,0:T(8,128)(2,1)S(1)}, u32[]{:S(2)}, u32[]{:S(2)}) async-start(bf16[16,32,1152]{2,1,0:T(8,128)(2,1)} %bitcast.1), calls=%async_computation | async-start | bytes 2359296 | tf_op jit(solution)/shard_map/all_to_all | solution.py:299
  47.7 41.0 %collective-permute-start.1 = (bf16[512,1536]{1,0:T(8,128)(2,1)}, bf16[512,1536]{1,0:T(8,128)(2,1)}, u32[]{:S(2)}, u32[]{:S(2)}) collective-permute-start(bf16[512,1536]{1,0:T(8,128)(2,1)} %collective-permute-done.mine_ref), channel_id=1, source_target_pairs={{0,16},{16,0},{1,17},{17,1},{2,18},{18,2},{3,19},{19,3},{4,20},{20... | collective-permute-start | bytes 4718600 | tf_op jit(solution)/shard_map/ppermute | solution.py:318
  47.7 14.6 %collective-permute-start.3 = (bf16[512,512]{1,0:T(8,128)(2,1)S(1)}, bf16[512,512]{1,0:T(8,128)(2,1)}, u32[]{:S(2)}, u32[]{:S(2)}) collective-permute-start(bf16[512,512]{1,0:T(8,128)(2,1)S(1)} %constant_dynamic-slice_fusion), channel_id=1, source_target_pairs={{0,1},{1,0},{2,3},{3,2},{4,5},{5,4},{6,7},{7,6},{8,9},{9,8},{10,11... | collective-permute-start | bytes 1572872 | tf_op jit(solution)/shard_map/ppermute | solution.py:317
  49.5 39.1 %collective-permute-start.2 = (f32[2,512]{1,0:T(2,128)S(1)}, f32[2,512]{1,0:T(2,128)S(1)}, u32[]{:S(2)}, u32[]{:S(2)}) collective-permute-start(f32[2,512]{1,0:T(2,128)S(1)} %copy-done.7), channel_id=1, source_target_pairs={{0,1},{1,0},{2,3},{3,2},{4,5},{5,4},{6,7},{7,6},{8,9},{9,8},{10,11... | collective-permute-start | bytes 12296 | tf_op jit(solution)/shard_map/ppermute | solution.py:316
  62.3 26.3 %collective-permute-start.4 = (bf16[512,512]{1,0:T(8,128)(2,1)}, bf16[512,512]{1,0:T(8,128)(2,1)}, u32[]{:S(2)}, u32[]{:S(2)}) collective-permute-start(bf16[512,512]{1,0:T(8,128)(2,1)} %collective-permute-done.3.out_mine_ref), channel_id=1, source_target_pairs={{0,16},{16,0},{1,17},{17,1},{2,18},{18,2},{3,19},{19,3},{4,20},{20... | collective-permute-start | bytes 1572872 | tf_op jit(solution)/shard_map/ppermute | solution.py:319
  62.6 0.8 copy-start.5
  62.6 0.8 copy-start.8
  87.0 1.6 %copy-start = (bf16[3,512,1024]{2,1,0:T(8,128)(2,1)}, bf16[3,512,1024]{2,1,0:T(8,128)(2,1)S(1)}, u32[]{:S(2)}) copy-start(bf16[3,512,1024]{2,1,0:T(8,128)(2,1)S(1)} %get-tuple-element.13.normed_ref) | copy-start | bytes 9437188
  88.6 27.0 %copy-start.4 = (bf16[512,384]{1,0:T(8,128)(2,1)S(1)}, bf16[512,384]{1,0:T(8,128)(2,1)}, u32[]{:S(2)}) copy-start(bf16[512,384]{1,0:T(8,128)(2,1)} %copy-done.3) | copy-start | bytes 1179652
  109.4 23.0 %all-to-all-start.1 = ((bf16[32,16,512]{2,1,0:T(8,128)(2,1)}), bf16[32,16,512]{2,1,0:T(8,128)(2,1)S(1)}, u32[]{:S(2)}, u32[]{:S(2)}) async-start(bf16[32,16,512]{2,1,0:T(8,128)(2,1)} %bitcast.4), calls=%async_computation.1 | async-start | bytes 1048576 | tf_op jit(solution)/shard_map/all_to_all | solution.py:368

commit v2 on v1

v2 whole, which is shorter than its diff:
```python
import functools

import jax
import jax.numpy as jnp
from jax import lax
from jax.experimental import pallas as pl
from jax.experimental.pallas import tpu as pltpu
from jax.sharding import PartitionSpec as P

HEADS = 16
SLOTS = 512
GRID = 64
EXTRA = 128
BF16 = jnp.bfloat16
F32 = jnp.float32
VMEM = pl.BlockSpec(memory_space=pltpu.VMEM)
SMEM = pl.BlockSpec(memory_space=pltpu.SMEM)
NT = (((1,), (1,)), ((), ()))
TN = (((0,), (0,)), ((), ()))


def params(megabytes):
    return pltpu.CompilerParams(vmem_limit_bytes=megabytes * 1024 * 1024)


def iota(shape, dim):
    return lax.broadcasted_iota(jnp.int32, shape, dim)


def dot(a, b):
    return jnp.dot(a, b, preferred_element_type=F32)


def position_parts(model_width):
    freq_count = model_width // 3 // 2
    frequency = 1.0 / 10000.0 ** (jnp.arange(freq_count, dtype=F32) / freq_count)
    angles = jnp.arange(GRID, dtype=F32)[:, None] * frequency[None, :]
    block = jnp.concatenate([jnp.sin(angles), jnp.cos(angles)], axis=1)
    width = 2 * freq_count
    rows = [
        jnp.pad(block, ((0, 0), (c * width, model_width - (c + 1) * width))) for c in range(3)
    ]
    table = jnp.concatenate(rows, axis=0)
    top = lax.reduce_precision(table, 8, 7)
    rest = table - top
    middle = lax.reduce_precision(rest, 8, 7)
    low = rest - middle
    return jnp.concatenate([top, middle, low], axis=0).astype(BF16)


def place_kernel(senders, capacity, windows_ref, coords_ref, x_ref, out_ref, placing_ref):
    windows = windows_ref[...]
    voxels = windows.shape[1]
    width = x_ref.shape[1]
    member = windows == iota((senders, voxels), 0)
    earlier = (iota((voxels, voxels), 0) < iota((voxels, voxels), 1)).astype(F32).astype(BF16)
    member_f = member.astype(F32)
    before = dot(member_f.astype(BF16), earlier)
    rank = jnp.sum(before * member_f, axis=0, keepdims=True).astype(jnp.int32)
    placed = windows * capacity + rank
    placing = (placed == iota((SLOTS, voxels), 0)).astype(F32).astype(BF16)
    placing_ref[...] = placing
    row = iota((EXTRA, voxels), 0)
    extra = jnp.where(row == 3, 1.0, 0.0).astype(F32)
    for c in range(3):
        extra = jnp.where(row == c, coords_ref[c : c + 1, :].astype(F32), extra)
    out_ref[:, :width] = dot(placing, x_ref[...]).astype(BF16)
    out_ref[:, width:] = lax.dot_general(
        placing, extra.astype(BF16), NT, preferred_element_type=F32
    ).astype(BF16)


def column_norm(rows, gain, head_size):
    blocks = []
    for start in range(0, rows.shape[0], head_size):
        block = rows[start : start + head_size]
        mean = jnp.sum(block * block, axis=0, keepdims=True) * (1.0 / head_size)
        blocks.append(block * lax.rsqrt(mean + 1e-06) * gain[start : start + head_size])
    return jnp.concatenate(blocks, axis=0).astype(BF16)


def attend_tile(normed, normed_q, w_query, w_key, w_value, gain_ref, features, bias, head_size):
    queries, tile = normed_q.shape[0], w_query.shape[0]
    query = lax.dot_general(w_query, normed_q, NT, preferred_element_type=F32)
    query = column_norm(query, gain_ref[0, features, :], head_size)
    key = lax.dot_general(w_key, normed, NT, preferred_element_type=F32)
    key = column_norm(key, gain_ref[1, features, :], head_size)
    value = lax.dot_general(normed, w_value, NT, preferred_element_type=F32).astype(BF16)
    query = (query.astype(F32) * (1.0 / head_size**0.5)).T
    lane_head = iota((queries, tile), 1) // head_size
    count = tile // head_size

    def score(head):
        return dot(jnp.where(lane_head == head, query, 0.0).astype(BF16), key)

    scores = score(0)
    mixed = jnp.zeros((queries, tile), F32)
    step = min(32, queries)
    for head in range(count):
        following = score(head + 1) if head + 1 < count else None
        pieces = []
        for r in range(0, queries, step):
            piece = scores[r : r + step] + bias
            weights = jnp.exp(piece - jnp.max(piece, axis=1, keepdims=True))
            total = jnp.sum(weights, axis=1, keepdims=True)
            pieces.append((weights * (1.0 / total)).astype(BF16))
        attend = jnp.concatenate(pieces, axis=0)
        mixed = jnp.where(lane_head == head, dot(attend, value), mixed)
        scores = following
    return mixed.astype(BF16)


def branch_scales(guidance_ref):
    g0, g1 = guidance_ref[0], guidance_ref[1]
    return 1.0 - g0, g0 - g1, g1


def pick_scale(b, scales):
    return jnp.where(b == 0, scales[0], jnp.where(b == 1, scales[1], scales[2]))


def own_kernel(
    senders,
    head_size,
    guidance_ref,
    rows_ref,
    table_ref,
    modulation_ref,
    w_ref,
    gain_ref,
    w_out_ref,
    normed_ref,
    normed_q_ref,
    acc_ref,
    bias_ref,
    hidden_ref,
    att_ref,
):
    branches, slots, width = normed_ref.shape
    queries = normed_q_ref.shape[1]
    group = att_ref.shape[1]
    capacity = slots // senders
    share = queries // senders
    first = lax.axis_index("head") * share
    scales = branch_scales(guidance_ref)
    total = (scales[0] + scales[1]) + scales[2]

    extra = rows_ref[:, width:]
    pick = ((iota((8, EXTRA), 1) == 3)).astype(F32).astype(BF16)
    live = lax.dot_general(pick, extra, NT, preferred_element_type=F32)
    bias_ref[...] = jnp.where(live > 0.5, 0.0, -1e30)

    spots = extra.astype(F32)
    lane = iota((slots, 3 * GRID), 1)
    wanted = jnp.where(
        lane < GRID,
        spots[:, 0:1],
        jnp.where(lane < 2 * GRID, spots[:, 1:2], spots[:, 2:3]),
    )
    chosen = (wanted == (lane % GRID).astype(F32)).astype(F32).astype(BF16)
    chosen = jnp.concatenate([chosen, chosen, chosen], axis=1)
    hidden_ref[...] = dot(chosen, table_ref[...]) + rows_ref[:, :width].astype(F32)

    chunk = 32

    def normalise(i, carry):
        rows = pl.ds(pl.multiple_of(i * chunk, chunk), chunk)
        hidden = hidden_ref[rows, :]
        centred = hidden - jnp.mean(hidden, axis=1, keepdims=True)
        spread = jnp.mean(centred * centred, axis=1, keepdims=True)
        normal = centred * lax.rsqrt(spread + 1e-06)
        for b in range(branches):
            normed_ref[b, rows, :] = (
                normal * (1.0 + modulation_ref[b, 1:2, :]) + modulation_ref[b, 0:1, :]
            ).astype(BF16)
        return carry

    lax.fori_loop(0, slots // chunk, normalise, 0, unroll=2)

    if share % 16 == 0:
        for s in range(senders):
            source = pl.ds(pl.multiple_of(s * capacity + first, 16), share)
            target = slice(s * share, (s + 1) * share)
            acc_ref[target, :] = hidden_ref[source, :] * total
            for b in range(branches):
                normed_q_ref[b, target, :] = normed_ref[b, source, :]
    else:
        row = iota((queries, slots), 0)
        wanted_slot = (row // share) * capacity + first + row % share
        chooser = (wanted_slot == iota((queries, slots), 1)).astype(F32)
        picked = jnp.dot(
            chooser, hidden_ref[...], preferred_element_type=F32, precision=lax.Precision.HIGHEST
        )
        acc_ref[...] = picked * total
        for b in range(branches):
            normed_q_ref[b] = dot(chooser.astype(BF16), normed_ref[b]).astype(BF16)

    bias = bias_ref[0:1, :]
    tile = min(256, group)

    def branch(b, carry):
        for start in range(0, group, tile):
            features = slice(start, start + tile)
            att_ref[:, features] = attend_tile(
                normed_ref[b],
                normed_q_ref[b],
                w_ref[0, features, :],
                w_ref[1, features, :],
                w_ref[2, features, :],
                gain_ref,
                features,
                bias,
                head_size,
            )
        acc_ref[...] += dot(att_ref[...], w_out_ref[...]) * (
            pick_scale(b, scales) * modulation_ref[b, 2:3, :]
        )
        return carry

    lax.fori_loop(0, branches, branch, 0)


def other_kernel(head_size, normed_ref, normed_q_ref, bias_ref, w_ref, gain_ref, att_ref):
    branches, tile = att_ref.shape[0], att_ref.shape[2]
    bias = bias_ref[0:1, :]

    def branch(b, carry):
        att_ref[b] = attend_tile(
            normed_ref[b],
            normed_q_ref[b],
            w_ref[0],
            w_ref[1],
            w_ref[2],
            gain_ref,
            slice(0, tile),
            bias,
            head_size,
        )
        return carry

    lax.fori_loop(0, branches, branch, 0)


def finish_kernel(out_parts, guidance_ref, acc_ref, modulation_ref, *refs):
    out_ref, pairs = refs[-1], refs[:-1]
    half = len(pairs) // 2
    scales = branch_scales(guidance_ref)
    total = acc_ref[...]
    for b in range(modulation_ref.shape[0]):
        part = dot(pairs[0][b], pairs[half][...])
        for n in range(1, half):
            part = part + dot(pairs[n][b], pairs[half + n][...])
        total = total + part * (scales[b] * modulation_ref[b, 2:3, :])
    if out_parts is None:
        out_ref[...] = total.astype(BF16)
    else:
        senders, heads, share, columns = out_parts
        for h in range(heads):
            piece = total[:, h * columns : (h + 1) * columns].astype(BF16)
            out_ref[:, h] = piece.reshape(senders, share, columns)


def return_kernel(placing_ref, rows_ref, out_ref):
    out_ref[...] = dot(placing_ref[...], rows_ref[...]).astype(BF16)


def on_device(x_latent, windows, coords, modulation, w_qkv, w_out, qk_gain, guidance):
    voxels, width = x_latent.shape
    group = w_qkv.shape[2]
    head_size = width // HEADS
    branches = modulation.shape[0]
    senders = lax.axis_size(("cfg", "vox"))
    heads = lax.axis_size("head")
    cores = lax.axis_size("cfg")
    capacity = SLOTS // senders
    queries = SLOTS // heads
    share = capacity // heads

    outgoing, placing = pl.pallas_call(
        functools.partial(place_kernel, senders, capacity),
        out_shape=(
            jax.ShapeDtypeStruct((SLOTS, width + EXTRA), BF16),
            jax.ShapeDtypeStruct((SLOTS, voxels), BF16),
        ),
        in_specs=[VMEM] * 3,
        out_specs=(VMEM, VMEM),
        compiler_params=params(16),
        name="place",
    )(windows.reshape(1, voxels), coords, x_latent)
    arrived = lax.all_to_all(
        outgoing.reshape(senders, capacity, width + EXTRA),
        ("cfg", "vox"),
        split_axis=0,
        concat_axis=0,
        tiled=True,
    ).reshape(SLOTS, width + EXTRA)

    w_qkv, w_out_sent, qk_gain, outgoing_done = lax.optimization_barrier(
        (w_qkv, w_out, qk_gain, outgoing)
    )
    del outgoing_done
    tile = group // cores
    start = lax.axis_index("cfg") * tile
    half = jnp.transpose(lax.dynamic_slice_in_dim(w_qkv, start, tile, 2), (1, 2, 0))
    out_half = lax.dynamic_slice_in_dim(w_out_sent, start, tile, 0)
    gain_half = lax.dynamic_slice_in_dim(qk_gain, start, tile, 1)
    swap = [(c, (c + 1) % cores) for c in range(cores)]
    fetched = []
    for distance in range(1, heads):
        turn = [(h, (h + distance) % heads) for h in range(heads)]
        fetched.append(tuple(lax.ppermute(a, "head", turn) for a in (half, gain_half, out_half)))

    table = position_parts(width)
    normed, normed_q, acc, bias = pl.pallas_call(
        functools.partial(own_kernel, senders, head_size),
        out_shape=(
            jax.ShapeDtypeStruct((branches, SLOTS, width), BF16),
            jax.ShapeDtypeStruct((branches, queries, width), BF16),
            jax.ShapeDtypeStruct((queries, width), F32),
            jax.ShapeDtypeStruct((8, SLOTS), F32),
        ),
        in_specs=[SMEM] + [VMEM] * 6,
        out_specs=(VMEM,) * 4,
        scratch_shapes=[pltpu.VMEM((SLOTS, width), F32), pltpu.VMEM((queries, group), BF16)],
        compiler_params=params(26),
        name="own_heads",
    )(
        guidance,
        arrived,
        table,
        modulation,
        jnp.transpose(w_qkv, (1, 2, 0)),
        qk_gain[:, :, None],
        w_out,
    )

    def attend(weights, gain):
        return pl.pallas_call(
            functools.partial(other_kernel, head_size),
            out_shape=jax.ShapeDtypeStruct((branches, queries, tile), BF16),
            in_specs=[VMEM] * 5,
            out_specs=VMEM,
            compiler_params=params(20),
            name="other_heads",
        )(normed, normed_q, bias, weights, gain[:, :, None])

    attended, outs = [], []
    ahead = bias
    for weights, gain, out_rows in fetched:
        weights, gain, ahead = lax.optimization_barrier((weights, gain, ahead))
        swapped = lax.ppermute(weights, "cfg", swap), lax.ppermute(gain, "cfg", swap)
        mine = attend(weights, gain)
        out_rows, mine = lax.optimization_barrier((out_rows, mine))
        out_swapped = lax.ppermute(out_rows, "cfg", swap)
        theirs = attend(*swapped)
        ahead = theirs
        attended += [mine, theirs]
        outs += [out_rows, out_swapped]

    parts = None
    shape = jax.ShapeDtypeStruct((queries, width), BF16)
    if share % 16 == 0:
        parts = (senders, heads, share, width // heads)
        shape = jax.ShapeDtypeStruct(parts, BF16)
    acc = pl.pallas_call(
        functools.partial(finish_kernel, parts),
        out_shape=shape,
        in_specs=[SMEM] + [VMEM] * (2 + 2 * len(outs)),
        out_specs=VMEM,
        compiler_params=params(20),
        name="finish",
    )(guidance, acc, modulation, *attended, *outs)
    if share % 16 != 0:
        acc = acc.reshape(senders, share, heads, width // heads).transpose(0, 2, 1, 3)
    back = lax.all_to_all(
        acc.reshape(senders * heads, share, width // heads),
        ("cfg", "vox", "head"),
        split_axis=0,
        concat_axis=0,
        tiled=True,
    )
    return pl.pallas_call(
        return_kernel,
        out_shape=jax.ShapeDtypeStruct((voxels, width // heads), BF16),
        in_specs=[VMEM] * 2,
        out_specs=VMEM,
        compiler_params=params(16),
        name="return_rows",
    )(placing.T, back.reshape(SLOTS, width // heads))


def solution(mesh):
    placed = (
        P(("cfg", "vox"), None),
        P(("cfg", "vox")),
        P(None, ("cfg", "vox")),
        P(),
        P(None, None, "head"),
        P("head", None),
        P(None, "head"),
        P(),
    )
    return jax.shard_map(
        on_device, mesh=mesh, in_specs=placed, out_specs=P(("cfg", "vox"), "head"), check_vma=False
    )
```

time: 134 us -> 119 us (0.89)
  waiting for transfers between devices: 54.9 us -> 38.1 us
  local copies, waits for them, and re-layouts: 13.1 us -> 25.4 us
  Pallas kernels: 47.4 us -> 37.6 us
  starting transfers between devices: 17.3 us -> 14.8 us
    ppermute x5 -> x6, waiting for transfers between devices: 38.3 us -> 1.52 us  [the longest x1 1.16 us: on_device(): lax.ppermute(gain, 'cfg', swap)]
    all_to_all x1, waiting for transfers between devices: 0.01 us -> 19.9 us  [on_device(): lax.all_to_all(outgoing.reshape(senders, capacity, width + EXTRA), ('cfg'...]
    unnamed x23 -> x48, local copies, waits for them, and re-layouts: 8.36 us -> 15.7 us
    pallas_call x1, Pallas kernels: 23.5 us -> 16.6 us  [on_device(): pl.pallas_call(functools.partial(own_kernel, senders, head_size), out_sha...]
    broadcast_in_dim x0 -> x3, local copies, waits for them, and re-layouts: none -> 3.4 us  [the longest x2 2.37 us: attend(): gain[:, :, None]]
    optimization_barrier x0 -> x1, local copies, waits for them, and re-layouts: none -> 3.18 us  [on_device(): lax.optimization_barrier((w_qkv, w_out, qk_gain, outgoing))]
    reshape x1 -> x0, local copies, waits for them, and re-layouts: 3.18 us -> none  [on_device(): flat = w_qkv.reshape(width, 3 * group)]
    pallas_call x1 -> x3, Pallas kernels: 20.8 us -> 17.8 us  [the longest x2 14.7 us: attend(): pl.pallas_call(functools.partial(other_kernel, head_size), out_shape=jax....]
  transfers between devices with their start and end apart: 7 -> 8, of which waited for: 3 -> 4; matrix products, arithmetic and copies ran while one was open for 1% -> 9% of each run, Pallas kernels for 19% -> 27%
where the time goes in v2:
time: 119 us; the launch traced here: 118 us
  waiting for transfers between devices  38.1 us (32%)
  Pallas kernels  37.6 us (32%)
  local copies, waits for them, and re-layouts  25.4 us (21%)
  starting transfers between devices  14.8 us (12%)
  other arithmetic  1.64 us (1%)
    all_to_all x1, waiting for transfers between devices, on_device(): lax.all_to_all(outgoing.reshape(senders, capacity, width + EXTRA), ('cfg'...  19.9 us
    all_to_all x1, waiting for transfers between devices, on_device(): lax.all_to_all(acc.reshape(senders * heads, share, width // heads), ('cfg...  16.6 us
    pallas_call x1, Pallas kernels, on_device(): pl.pallas_call(functools.partial(own_kernel, senders, head_size), out_sha...  16.6 us
    unnamed x48, local copies, waits for them, and re-layouts  15.7 us
    pallas_call x2, Pallas kernels, attend(): pl.pallas_call(functools.partial(other_kernel, head_size), out_shape=jax....  14.7 us
    all_to_all x1, starting transfers between devices, on_device(): lax.all_to_all(outgoing.reshape(senders, capacity, width + EXTRA), ('cfg'...  7.4 us
    ppermute x3, starting transfers between devices, on_device(): lax.ppermute(a, 'head', turn)  3.56 us
    all_to_all x1, starting transfers between devices, on_device(): lax.all_to_all(acc.reshape(senders * heads, share, width // heads), ('cfg...  3.26 us
  transfers between devices with their start and end apart: 8, of which 4 were waited for; matrix products, arithmetic and copies ran while one was open for 9% of the time, Pallas kernels for 27%

profile of v2, /device:TPU:0, one launch (start us, length us, event | category | flops | bytes accessed | tf_op | source)
XLA Modules:
  0.0 117.7 jit_solution(10907883438537839137)
XLA Ops:
  0.0 0.7 reshape.21.windows_ref
  0.7 0.0 copy-start.13
  0.7 1.1 copy-done.13
  1.8 0.7 copy-done.18
  2.5 2.1 %place.1 = (bf16[512,1152]{1,0:T(8,128)(2,1)}, bf16[512,384]{1,0:T(8,128)(2,1)S(1)}) custom-call(s32[1,384]{1,0:T(1,128)S(1)} %reshape.21.windows_ref, s32[3,384]{1,0:T(4,128)S(1)} %copy-done.18, bf16[384,1024]{1,0:T(8,128)(2,1)S(1)} %copy-done.13), custom_call_target="tpu_custom_call" | custom-call | tf_op jit(solution)/shard_map/place/pallas_call | solution.py:279
  4.6 0.7 copy-done.14
  5.3 7.4 %all-to-all-start = ((bf16[16,32,1152]{2,1,0:T(8,128)(2,1)}), bf16[16,32,1152]{2,1,0:T(8,128)(2,1)}, u32[]{:S(2)}, u32[]{:S(2)}) async-start(bf16[16,32,1152]{2,1,0:T(8,128)(2,1)} %bitcast.1), calls=%async_computation | async-start | bytes 2359296 | tf_op jit(solution)/shard_map/all_to_all | solution.py:290
  12.7 3.2 %copy.19 = bf16[1024,3,512]{0,2,1:T(8,128)(2,1)S(1)} copy(bf16[1024,3,512]{2,0,1:T(8,128)(2,1)} %param.12) | data formatting | bytes 6291456 | tf_op jit(solution)/shard_map/optimization_barrier | solution.py:298
  15.9 0.0 copy-start.21
  15.9 1.3 %dynamic-slice_bitcast_fusion = bf16[3,256,1024]{2,1,0:T(8,128)(2,1)} fusion(bf16[1024,3,512]{0,2,1:T(8,128)(2,1)S(1)} %copy.19, s32[]{:T(128)S(6)} %select_n.2), kind=kLoop, calls=%fused_computation | loop fusion | bytes 3145732 | tf_op jit(solution)/shard_map/transpose | solution.py:304
  17.2 1.5 %collective-permute-start.1 = (bf16[3,256,1024]{2,1,0:T(8,128)(2,1)}, bf16[3,256,1024]{2,1,0:T(8,128)(2,1)}, u32[]{:S(2)}, u32[]{:S(2)}) collective-permute-start(bf16[3,256,1024]{2,1,0:T(8,128)(2,1)} %dynamic-slice_bitcast_fusion), channel_id=1, source_target_pairs={{0,1},{1,0},{2,3},{3,2},{4,5},{5,4},{6,7},{7,6},{8,9},{9,8},{10,11... | collective-permute-start | bytes 4718600 | tf_op jit(solution)/shard_map/ppermute | solution.py:311
  18.8 0.0 copy-done.21
  18.8 0.5 collective-permute-start.2
  19.3 0.3 fusion.3
  19.6 0.1 pad_maximum_fusion.1
  19.6 0.2 reduce-precision_convert_fusion.1
  19.8 0.0 copy-start.16
  19.9 0.0 copy-start.19
  19.9 1.1 pad_maximum_fusion.table_ref
  21.0 1.0 copy.20.gain_ref
  22.0 19.9 %all-to-all-done = bf16[16,32,1152]{2,1,0:T(8,128)(2,1)} async-done(((bf16[16,32,1152]{2,1,0:T(8,128)(2,1)}), bf16[16,32,1152]{2,1,0:T(8,128)(2,1)}, u32[]{:S(2)}, u32[]{:S(2)}) %all-to-all-start) | async-done | bytes 1179680 | tf_op jit(solution)/shard_map/all_to_all | solution.py:290
  41.9 0.0 copy-done.16
  41.9 0.0 copy-done.19
  41.9 1.3 %copy-done.6 = bf16[576,1024]{1,0:T(8,128)(2,1)S(1)} copy-done((bf16[576,1024]{1,0:T(8,128)(2,1)S(1)}, bf16[576,1024]{1,0:T(8,128)(2,1)}, u32[]{:S(2)}) %copy-start.6) | copy-done | bytes 1179672
  43.2 1.2 %copy-done.7 = bf16[512,1024]{1,0:T(8,128)(2,1)S(1)} copy-done((bf16[512,1024]{1,0:T(8,128)(2,1)S(1)}, bf16[512,1024]{1,0:T(8,128)(2,1)}, u32[]{:S(2)}) %copy-start.7) | copy-done | bytes 1048600
  44.4 1.0 copy-done.8
  45.5 16.6 %own_heads.1 = (bf16[3,512,1024]{2,1,0:T(8,128)(2,1)S(1)}, bf16[3,256,1024]{2,1,0:T(8,128)(2,1)S(1)}, f32[256,1024]{1,0:T(8,128)S(1)}, f32[8,512]{1,0:T(8,128)S(1)}) custom-call(f32[2]{0:T(128)S(1)} %copy-done.19, bf16[512,1152]{1,0:T(8,128)(2,1)} %bitcast.2.rows_ref, bf16[576,1024]{1,0:T(8,128)(2,1)S(1)} %copy-done.6, f32[3,3,1024]{2,1,0:T(4,128)S(1)} %copy-done.16, ...), custom_call_target="tpu_custom_call" | custom-call | tf_op jit(solution)/shard_map/own_heads/pallas_call | solution.py:314
  62.1 0.0 copy-start
  62.1 1.6 %copy-done = bf16[3,512,1024]{2,1,0:T(8,128)(2,1)} copy-done((bf16[3,512,1024]{2,1,0:T(8,128)(2,1)}, bf16[3,512,1024]{2,1,0:T(8,128)(2,1)S(1)}, u32[]{:S(2)}) %copy-start) | copy-done | bytes 3145752
  63.7 1.2 %copy-done.3 = bf16[3,256,1024]{2,1,0:T(8,128)(2,1)} copy-done((bf16[3,256,1024]{2,1,0:T(8,128)(2,1)}, bf16[3,256,1024]{2,1,0:T(8,128)(2,1)S(1)}, u32[]{:S(2)}) %copy-start.3) | copy-done | bytes 1572888
  64.9 0.0 collective-permute-done.2
  64.9 0.0 collective-permute-done.1.w_ref
  64.9 0.1 collective-permute-start.3
  65.0 1.0 constant_dynamic-slice_fusion.1
  66.0 0.1 copy-done.9
  66.1 1.5 %collective-permute-start = (bf16[256,1024]{1,0:T(8,128)(2,1)}, bf16[256,1024]{1,0:T(8,128)(2,1)}, u32[]{:S(2)}, u32[]{:S(2)}) collective-permute-start(bf16[256,1024]{1,0:T(8,128)(2,1)} %constant_dynamic-slice_fusion.1), channel_id=1, source_target_pairs={{0,1},{1,0},{2,3},{3,2},{4,5},{5,4},{6,7},{7,6},{8,9},{9,8},{10,11... | collective-permute-start | bytes 1572872 | tf_op jit(solution)/shard_map/ppermute | solution.py:311
  67.6 0.9 copy.22.gain_ref
  68.5 0.0 copy-done.22
  68.5 1.9 %copy-done.1 = bf16[3,512,1024]{2,1,0:T(8,128)(2,1)S(1)} copy-done((bf16[3,512,1024]{2,1,0:T(8,128)(2,1)S(1)}, bf16[3,512,1024]{2,1,0:T(8,128)(2,1)}, u32[]{:S(2)}) %copy-start.1) | copy-done | bytes 3145752
  70.4 1.4 %copy-done.4 = bf16[3,256,1024]{2,1,0:T(8,128)(2,1)S(1)} copy-done((bf16[3,256,1024]{2,1,0:T(8,128)(2,1)S(1)}, bf16[3,256,1024]{2,1,0:T(8,128)(2,1)}, u32[]{:S(2)}) %copy-start.4) | copy-done | bytes 1572888
  71.8 0.9 copy-done.12
  72.7 7.4 %other_heads.2.refs_0_ = bf16[3,256,256]{2,1,0:T(8,128)(2,1)S(1)} custom-call(bf16[3,512,1024]{2,1,0:T(8,128)(2,1)S(1)} %copy-done.1, bf16[3,256,1024]{2,1,0:T(8,128)(2,1)S(1)} %copy-done.4, f32[8,512]{1,0:T(8,128)S(1)} %get-tuple-element.26.bias_ref, bf16[3,256,1024]{2,1,0:T(8,128)(2,1)} %collective-permute-done.1.w_ref, f32[2,256,1]{2,1,0:T(8,128)S(1)} %copy-done.12), custom_call_target="tpu_custom_call" | custom-call | tf_op jit(solution)/shard_map/other_heads/pallas_call | solution.py:338
  80.1 0.3 collective-permute-done.refs_2_
  80.5 0.0 collective-permute-start.5
  80.5 0.0 copy-done.23
  80.5 0.5 collective-permute-start.4
  81.0 1.2 collective-permute-done.4
  82.2 1.5 %copy.23.gain_ref = f32[2,256,1]{2,1,0:T(8,128)} copy(f32[2,256,1]{1,0,2:T(2,128)} %bitcast.7) | data formatting | bytes 4096 | tf_op jit(solution)/shard_map/broadcast_in_dim | solution.py:345
  83.7 0.0 collective-permute-done.3.w_ref
  83.7 0.0 copy-done.2
  83.7 1.4 %copy-done.5 = bf16[3,256,1024]{2,1,0:T(8,128)(2,1)S(1)} copy-done((bf16[3,256,1024]{2,1,0:T(8,128)(2,1)S(1)}, bf16[3,256,1024]{2,1,0:T(8,128)(2,1)}, u32[]{:S(2)}) %copy-start.5) | copy-done | bytes 1572888
  85.1 0.9 copy-done.11
  86.1 7.3 %other_heads.3.refs_1_ = bf16[3,256,256]{2,1,0:T(8,128)(2,1)S(1)} custom-call(bf16[3,512,1024]{2,1,0:T(8,128)(2,1)S(1)} %copy-done.2, bf16[3,256,1024]{2,1,0:T(8,128)(2,1)S(1)} %copy-done.5, f32[8,512]{1,0:T(8,128)S(1)} %get-tuple-element.26.bias_ref, bf16[3,256,1024]{2,1,0:T(8,128)(2,1)} %collective-permute-done.3.w_ref, f32[2,256,1]{2,1,0:T(8,128)S(1)} %copy-done.11), custom_call_target="tpu_custom_call" | custom-call | tf_op jit(solution)/shard_map/other_heads/pallas_call | solution.py:338
  93.4 0.0 collective-permute-done.5.refs_3_
  93.4 0.0 copy-done.10
  93.4 0.0 copy-done.17
  93.4 0.0 copy-done.20
  93.4 0.0 copy-start.15
  93.4 3.1 %finish.1 = bf16[16,2,16,512]{3,2,1,0:T(8,128)(2,1)} custom-call(f32[2]{0:T(128)S(1)} %copy-done.20, f32[256,1024]{1,0:T(8,128)S(1)} %copy-done.10, f32[3,3,1024]{2,1,0:T(4,128)S(1)} %copy-done.17, bf16[3,256,256]{2,1,0:T(8,128)(2,1)S(1)} %other_heads.2.refs_0_, bf16[3,256,256]{2,1,0:T(8,128)(2,1)S(1)} %other_heads.3.refs_1_, ...), custom_call_target="tpu_custom_call" | custom-call | tf_op jit(solution)/shard_map/finish/pallas_call | solution.py:365
  96.5 3.3 %all-to-all-start.1 = ((bf16[32,16,512]{2,1,0:T(8,128)(2,1)}), bf16[32,16,512]{2,1,0:T(8,128)(2,1)S(1)}, u32[]{:S(2)}, u32[]{:S(2)}) async-start(bf16[32,16,512]{2,1,0:T(8,128)(2,1)} %bitcast.8), calls=%async_computation.1 | async-start | bytes 1048576 | tf_op jit(solution)/shard_map/all_to_all | solution.py:375
  99.8 0.0 copy-done.15
  99.8 0.2 copy.18
  100.0 16.6 %all-to-all-done.1 = bf16[32,16,512]{2,1,0:T(8,128)(2,1)S(1)} async-done(((bf16[32,16,512]{2,1,0:T(8,128)(2,1)}), bf16[32,16,512]{2,1,0:T(8,128)(2,1)S(1)}, u32[]{:S(2)}, u32[]{:S(2)}) %all-to-all-start.1) | async-done | bytes 524320 | tf_op jit(solution)/shard_map/all_to_all | solution.py:375
  116.6 1.1 return_rows.1
  (20 shorter events, 0.0 us)
Async XLA Ops:
  0.7 1.1 copy-start.13
  1.8 0.7 copy-start.18
  4.6 0.7 copy-start.14
  5.3 36.6 %all-to-all-start = ((bf16[16,32,1152]{2,1,0:T(8,128)(2,1)}), bf16[16,32,1152]{2,1,0:T(8,128)(2,1)}, u32[]{:S(2)}, u32[]{:S(2)}) async-start(bf16[16,32,1152]{2,1,0:T(8,128)(2,1)} %bitcast.1), calls=%async_computation | async-start | bytes 2359296 | tf_op jit(solution)/shard_map/all_to_all | solution.py:290
  15.9 2.8 %copy-start.21 = (f32[2,512]{1,0:T(2,128)S(1)}, f32[2,512]{1,0:T(2,128)}, u32[]{:S(2)}) copy-start(f32[2,512]{1,0:T(2,128)} %param.14) | copy-start | bytes 12292
  17.2 47.7 %collective-permute-start.1 = (bf16[3,256,1024]{2,1,0:T(8,128)(2,1)}, bf16[3,256,1024]{2,1,0:T(8,128)(2,1)}, u32[]{:S(2)}, u32[]{:S(2)}) collective-permute-start(bf16[3,256,1024]{2,1,0:T(8,128)(2,1)} %dynamic-slice_bitcast_fusion), channel_id=1, source_target_pairs={{0,1},{1,0},{2,3},{3,2},{4,5},{5,4},{6,7},{7,6},{8,9},{9,8},{10,11... | collective-permute-start | bytes 4718600 | tf_op jit(solution)/shard_map/ppermute | solution.py:311
  18.8 46.2 %collective-permute-start.2 = (f32[2,256]{1,0:T(2,128)S(1)}, f32[2,256]{1,0:T(2,128)S(1)}, u32[]{:S(2)}, u32[]{:S(2)}) collective-permute-start(f32[2,256]{1,0:T(2,128)S(1)} %constant_dynamic-slice_fusion), channel_id=1, source_target_pairs={{0,1},{1,0},{2,3},{3,2},{4,5},{5,4},{6,7},{7,6},{8,9},{9,8},{10,11... | collective-permute-start | bytes 6152 | tf_op jit(solution)/shard_map/ppermute | solution.py:311
  19.8 22.1 %copy-start.16 = (f32[3,3,1024]{2,1,0:T(4,128)S(1)}, f32[3,3,1024]{2,1,0:T(4,128)}, u32[]{:S(2)}) copy-start(f32[3,3,1024]{2,1,0:T(4,128)} %modulation_ref.3) | copy-start | bytes 110596
  19.9 22.1 %copy-start.19 = (f32[2]{0:T(128)S(1)}, f32[2]{0:T(128)}, u32[]{:S(2)}) copy-start(f32[2]{0:T(128)} %guidance_ref.3) | copy-start | bytes 28
  41.9 1.3 %copy-start.6 = (bf16[576,1024]{1,0:T(8,128)(2,1)S(1)}, bf16[576,1024]{1,0:T(8,128)(2,1)}, u32[]{:S(2)}) copy-start(bf16[576,1024]{1,0:T(8,128)(2,1)} %pad_maximum_fusion.table_ref) | copy-start | bytes 3538948
  43.2 1.2 %copy-start.7 = (bf16[512,1024]{1,0:T(8,128)(2,1)S(1)}, bf16[512,1024]{1,0:T(8,128)(2,1)}, u32[]{:S(2)}) copy-start(bf16[512,1024]{1,0:T(8,128)(2,1)} %w_out_ref.1) | copy-start | bytes 3145732
  44.4 1.0 copy-start.8
  62.1 1.6 %copy-start = (bf16[3,512,1024]{2,1,0:T(8,128)(2,1)}, bf16[3,512,1024]{2,1,0:T(8,128)(2,1)S(1)}, u32[]{:S(2)}) copy-start(bf16[3,512,1024]{2,1,0:T(8,128)(2,1)S(1)} %get-tuple-element.24.normed_ref) | copy-start | bytes 9437188
  63.7 1.2 %copy-start.3 = (bf16[3,256,1024]{2,1,0:T(8,128)(2,1)}, bf16[3,256,1024]{2,1,0:T(8,128)(2,1)S(1)}, u32[]{:S(2)}) copy-start(bf16[3,256,1024]{2,1,0:T(8,128)(2,1)S(1)} %get-tuple-element.25.normed_q_ref) | copy-start | bytes 4718596
  64.9 1.2 %copy-start.9 = (f32[256,1024]{1,0:T(8,128)}, f32[256,1024]{1,0:T(8,128)S(1)}, u32[]{:S(2)}) copy-start(f32[256,1024]{1,0:T(8,128)S(1)} %get-tuple-element.22.acc_ref) | copy-start | bytes 3145732
  64.9 3.5 %copy-start.22 = (f32[2,256]{1,0:T(2,128)}, f32[2,256]{1,0:T(2,128)S(1)}, u32[]{:S(2)}) copy-start(f32[2,256]{1,0:T(2,128)S(1)} %collective-permute-done.2) | copy-start | bytes 6148
  64.9 18.7 %collective-permute-start.3 = (bf16[3,256,1024]{2,1,0:T(8,128)(2,1)}, bf16[3,256,1024]{2,1,0:T(8,128)(2,1)}, u32[]{:S(2)}, u32[]{:S(2)}) collective-permute-start(bf16[3,256,1024]{2,1,0:T(8,128)(2,1)} %collective-permute-done.1.w_ref), channel_id=1, source_target_pairs={{0,16},{16,0},{1,17},{17,1},{2,18},{18,2},{3,19},{19,3},{4,20},{20... | collective-permute-start | bytes 4718600 | tf_op jit(solution)/shard_map/ppermute | solution.py:351
  66.1 14.4 %collective-permute-start = (bf16[256,1024]{1,0:T(8,128)(2,1)}, bf16[256,1024]{1,0:T(8,128)(2,1)}, u32[]{:S(2)}, u32[]{:S(2)}) collective-permute-start(bf16[256,1024]{1,0:T(8,128)(2,1)} %constant_dynamic-slice_fusion.1), channel_id=1, source_target_pairs={{0,1},{1,0},{2,3},{3,2},{4,5},{5,4},{6,7},{7,6},{8,9},{9,8},{10,11... | collective-permute-start | bytes 1572872 | tf_op jit(solution)/shard_map/ppermute | solution.py:311
  68.5 1.9 %copy-start.1 = (bf16[3,512,1024]{2,1,0:T(8,128)(2,1)S(1)}, bf16[3,512,1024]{2,1,0:T(8,128)(2,1)}, u32[]{:S(2)}) copy-start(bf16[3,512,1024]{2,1,0:T(8,128)(2,1)} %copy-done) | copy-start | bytes 9437188
  70.4 1.4 %copy-start.4 = (bf16[3,256,1024]{2,1,0:T(8,128)(2,1)S(1)}, bf16[3,256,1024]{2,1,0:T(8,128)(2,1)}, u32[]{:S(2)}) copy-start(bf16[3,256,1024]{2,1,0:T(8,128)(2,1)} %copy-done.3) | copy-start | bytes 4718596
  71.8 0.9 copy-start.12
  72.7 7.8 %copy-start.23 = (f32[2,256]{1,0:T(2,128)S(1)}, f32[2,256]{1,0:T(2,128)}, u32[]{:S(2)}) copy-start(f32[2,256]{1,0:T(2,128)} %copy-done.22) | copy-start | bytes 6148
  72.7 10.9 %copy-start.2 = (bf16[3,512,1024]{2,1,0:T(8,128)(2,1)S(1)}, bf16[3,512,1024]{2,1,0:T(8,128)(2,1)}, u32[]{:S(2)}) copy-start(bf16[3,512,1024]{2,1,0:T(8,128)(2,1)} %copy-done) | copy-start | bytes 9437188
  80.5 12.9 %collective-permute-start.5 = (bf16[256,1024]{1,0:T(8,128)(2,1)}, bf16[256,1024]{1,0:T(8,128)(2,1)}, u32[]{:S(2)}, u32[]{:S(2)}) collective-permute-start(bf16[256,1024]{1,0:T(8,128)(2,1)} %collective-permute-done.refs_2_), channel_id=1, source_target_pairs={{0,16},{16,0},{1,17},{17,1},{2,18},{18,2},{3,19},{19,3},{4,20},{20... | collective-permute-start | bytes 1572872 | tf_op jit(solution)/shard_map/ppermute | solution.py:354
  80.5 1.7 %collective-permute-start.4 = (f32[2,256]{1,0:T(2,128)S(1)}, f32[2,256]{1,0:T(2,128)}, u32[]{:S(2)}, u32[]{:S(2)}) collective-permute-start(f32[2,256]{1,0:T(2,128)S(1)} %copy-done.23), channel_id=1, source_target_pairs={{0,16},{16,0},{1,17},{17,1},{2,18},{18,2},{3,19},{19,3},{4,20},{20... | collective-permute-start | bytes 6152 | tf_op jit(solution)/shard_map/ppermute | solution.py:351
  83.7 1.4 %copy-start.5 = (bf16[3,256,1024]{2,1,0:T(8,128)(2,1)S(1)}, bf16[3,256,1024]{2,1,0:T(8,128)(2,1)}, u32[]{:S(2)}) copy-start(bf16[3,256,1024]{2,1,0:T(8,128)(2,1)} %copy-done.3) | copy-start | bytes 4718596
  85.1 0.9 copy-start.11
  86.0 7.4 %copy-start.10 = (f32[256,1024]{1,0:T(8,128)S(1)}, f32[256,1024]{1,0:T(8,128)}, u32[]{:S(2)}) copy-start(f32[256,1024]{1,0:T(8,128)} %copy-done.9) | copy-start | bytes 3145732
  86.1 7.4 %copy-start.17 = (f32[3,3,1024]{2,1,0:T(4,128)S(1)}, f32[3,3,1024]{2,1,0:T(4,128)}, u32[]{:S(2)}) copy-start(f32[3,3,1024]{2,1,0:T(4,128)} %modulation_ref.3) | copy-start | bytes 110596
  86.1 7.4 %copy-start.20 = (f32[2]{0:T(128)S(1)}, f32[2]{0:T(128)}, u32[]{:S(2)}) copy-start(f32[2]{0:T(128)} %guidance_ref.3) | copy-start | bytes 28
  93.4 6.4 %copy-start.15 = (bf16[512,384]{1,0:T(8,128)(2,1)S(1)}, bf16[512,384]{1,0:T(8,128)(2,1)}, u32[]{:S(2)}) copy-start(bf16[512,384]{1,0:T(8,128)(2,1)} %copy-done.14) | copy-start | bytes 1179652
  96.5 20.1 %all-to-all-start.1 = ((bf16[32,16,512]{2,1,0:T(8,128)(2,1)}), bf16[32,16,512]{2,1,0:T(8,128)(2,1)S(1)}, u32[]{:S(2)}, u32[]{:S(2)}) async-start(bf16[32,16,512]{2,1,0:T(8,128)(2,1)} %bitcast.8), calls=%async_computation.1 | async-start | bytes 1048576 | tf_op jit(solution)/shard_map/all_to_all | solution.py:375

commit v3 on v2

--- a/solution.py
+++ b/solution.py
@@ -15,6 +15,7 @@
 F32 = jnp.float32
 VMEM = pl.BlockSpec(memory_space=pltpu.VMEM)
 SMEM = pl.BlockSpec(memory_space=pltpu.SMEM)
+HBM = pl.BlockSpec(memory_space=pltpu.HBM)
 NT = (((1,), (1,)), ((), ()))
 TN = (((0,), (0,)), ((), ()))
 
@@ -48,26 +49,28 @@
     return jnp.concatenate([top, middle, low], axis=0).astype(BF16)
 
 
-def place_kernel(senders, capacity, windows_ref, coords_ref, x_ref, out_ref, placing_ref):
-    windows = windows_ref[...]
-    voxels = windows.shape[1]
-    width = x_ref.shape[1]
+def place_kernel(senders, capacity, windows_ref, coords_ref, x_hbm, out_ref, placed_ref, x_ref, sem):
+    load = pltpu.make_async_copy(x_hbm, x_ref, sem)
+    load.start()
+    voxels, width = x_hbm.shape
+    windows = windows_ref[...].reshape(1, voxels)
     member = windows == iota((senders, voxels), 0)
     earlier = (iota((voxels, voxels), 0) < iota((voxels, voxels), 1)).astype(F32).astype(BF16)
     member_f = member.astype(F32)
     before = dot(member_f.astype(BF16), earlier)
     rank = jnp.sum(before * member_f, axis=0, keepdims=True).astype(jnp.int32)
     placed = windows * capacity + rank
+    placed_ref[...] = placed.astype(F32)
     placing = (placed == iota((SLOTS, voxels), 0)).astype(F32).astype(BF16)
-    placing_ref[...] = placing
     row = iota((EXTRA, voxels), 0)
     extra = jnp.where(row == 3, 1.0, 0.0).astype(F32)
     for c in range(3):
         extra = jnp.where(row == c, coords_ref[c : c + 1, :].astype(F32), extra)
-    out_ref[:, :width] = dot(placing, x_ref[...]).astype(BF16)
     out_ref[:, width:] = lax.dot_general(
         placing, extra.astype(BF16), NT, preferred_element_type=F32
     ).astype(BF16)
+    load.wait()
+    out_ref[:, :width] = dot(placing, x_ref[...]).astype(BF16)
 
 
 def column_norm(rows, gain, head_size):
@@ -79,12 +82,12 @@
     return jnp.concatenate(blocks, axis=0).astype(BF16)
 
 
-def attend_tile(normed, normed_q, w_query, w_key, w_value, gain_ref, features, bias, head_size):
+def attend_tile(normed, normed_q, w_query, w_key, w_value, gains, bias, head_size):
     queries, tile = normed_q.shape[0], w_query.shape[0]
     query = lax.dot_general(w_query, normed_q, NT, preferred_element_type=F32)
-    query = column_norm(query, gain_ref[0, features, :], head_size)
+    query = column_norm(query, gains[:, 0:1], head_size)
     key = lax.dot_general(w_key, normed, NT, preferred_element_type=F32)
-    key = column_norm(key, gain_ref[1, features, :], head_size)
+    key = column_norm(key, gains[:, 1:2], head_size)
     value = lax.dot_general(normed, w_value, NT, preferred_element_type=F32).astype(BF16)
     query = (query.astype(F32) * (1.0 / head_size**0.5)).T
     lane_head = iota((queries, tile), 1) // head_size
@@ -123,9 +126,18 @@
     senders,
     head_size,
     guidance_ref,
+    modulation_ref,
+    rows_hbm,
+    table_hbm,
+    w_hbm,
+    gain_hbm,
+    w_out_hbm,
+    normed_hbm,
+    normed_q_hbm,
+    acc_hbm,
+    bias_hbm,
     rows_ref,
     table_ref,
-    modulation_ref,
     w_ref,
     gain_ref,
     w_out_ref,
@@ -135,7 +147,34 @@
     bias_ref,
     hidden_ref,
     att_ref,
+    in_sems,
+    out_sems,
 ):
+    loads = [
+        pltpu.make_async_copy(source, target, in_sems.at[n])
+        for n, (source, target) in enumerate(
+            (
+                (rows_hbm, rows_ref),
+                (table_hbm, table_ref),
+                (w_hbm, w_ref),
+                (gain_hbm, gain_ref),
+                (w_out_hbm, w_out_ref),
+            )
+        )
+    ]
+    stores = [
+        pltpu.make_async_copy(source, target, out_sems.at[n])
+        for n, (source, target) in enumerate(
+            (
+                (normed_ref, normed_hbm),
+                (normed_q_ref, normed_q_hbm),
+                (bias_ref, bias_hbm),
+                (acc_ref, acc_hbm),
+            )
+        )
+    ]
+    for load in loads:
+        load.start()
     branches, slots, width = normed_ref.shape
     queries = normed_q_ref.shape[1]
     group = att_ref.shape[1]
@@ -145,6 +184,7 @@
     scales = branch_scales(guidance_ref)
     total = (scales[0] + scales[1]) + scales[2]
 
+    loads[0].wait()
     extra = rows_ref[:, width:]
     pick = ((iota((8, EXTRA), 1) == 3)).astype(F32).astype(BF16)
     live = lax.dot_general(pick, extra, NT, preferred_element_type=F32)
@@ -159,6 +199,7 @@
     )
     chosen = (wanted == (lane % GRID).astype(F32)).astype(F32).astype(BF16)
     chosen = jnp.concatenate([chosen, chosen, chosen], axis=1)
+    loads[1].wait()
     hidden_ref[...] = dot(chosen, table_ref[...]) + rows_ref[:, :width].astype(F32)
 
     chunk = 32
@@ -176,6 +217,8 @@
         return carry
 
     lax.fori_loop(0, slots // chunk, normalise, 0, unroll=2)
+    stores[0].start()
+    stores[2].start()
 
     if share % 16 == 0:
         for s in range(senders):
@@ -194,9 +237,12 @@
         acc_ref[...] = picked * total
         for b in range(branches):
             normed_q_ref[b] = dot(chooser.astype(BF16), normed_ref[b]).astype(BF16)
+    stores[1].start()
 
     bias = bias_ref[0:1, :]
     tile = min(256, group)
+    for load in loads[2:]:
+        load.wait()
 
     def branch(b, carry):
         for start in range(0, group, tile):
@@ -207,8 +253,7 @@
                 w_ref[0, features, :],
                 w_ref[1, features, :],
                 w_ref[2, features, :],
-                gain_ref,
-                features,
+                gain_ref[features, :],
                 bias,
                 head_size,
             )
@@ -218,38 +263,92 @@
         return carry
 
     lax.fori_loop(0, branches, branch, 0)
-
-
-def other_kernel(head_size, normed_ref, normed_q_ref, bias_ref, w_ref, gain_ref, att_ref):
+    stores[3].start()
+    for store in stores:
+        store.wait()
+
+
+def other_kernel(
+    head_size,
+    swapped,
+    normed_hbm,
+    normed_q_hbm,
+    bias_hbm,
+    w_hbm,
+    gain_hbm,
+    att_hbm,
+    normed_ref,
+    normed_q_ref,
+    bias_ref,
+    w_ref,
+    gain_ref,
+    att_ref,
+    in_sems,
+    normed_sems,
+    normed_q_sems,
+    out_sems,
+):
     branches, tile = att_ref.shape[0], att_ref.shape[2]
+    small = [
+        pltpu.make_async_copy(source, target, in_sems.at[n])
+        for n, (source, target) in enumerate(
+            ((w_hbm, w_ref), (bias_hbm, bias_ref), (gain_hbm, gain_ref))
+        )
+    ]
+
+    def load(b):
+        return (
+            pltpu.make_async_copy(normed_q_hbm.at[b], normed_q_ref.at[b], normed_q_sems.at[b]),
+            pltpu.make_async_copy(normed_hbm.at[b], normed_ref.at[b], normed_sems.at[b]),
+        )
+
+    def store(b):
+        return pltpu.make_async_copy(att_ref.at[b], att_hbm.at[b], out_sems.at[b])
+
+    for copy in small:
+        copy.start()
+    for b in range(branches):
+        for copy in load(b):
+            copy.start()
+    core = lax.axis_index("cfg")
+    core = 1 - core if swapped else core
+    features = pl.ds(pl.multiple_of(core * tile, tile), tile)
+    for copy in small:
+        copy.wait()
     bias = bias_ref[0:1, :]
+    gains = gain_ref[features, :]
 
     def branch(b, carry):
+        for copy in load(b):
+            copy.wait()
         att_ref[b] = attend_tile(
-            normed_ref[b],
-            normed_q_ref[b],
-            w_ref[0],
-            w_ref[1],
-            w_ref[2],
-            gain_ref,
-            slice(0, tile),
-            bias,
-            head_size,
-        )
+            normed_ref[b], normed_q_ref[b], w_ref[0], w_ref[1], w_ref[2], gains, bias, head_size
+        )
+        store(b).start()
         return carry
 
     lax.fori_loop(0, branches, branch, 0)
-
-
-def finish_kernel(out_parts, guidance_ref, acc_ref, modulation_ref, *refs):
-    out_ref, pairs = refs[-1], refs[:-1]
-    half = len(pairs) // 2
+    for b in range(branches):
+        store(b).wait()
+
+
+def finish_kernel(out_parts, count, guidance_ref, modulation_ref, acc_hbm, *refs):
+    sources = refs[: 2 * count] + (acc_hbm,)
+    out_ref, held, sems = refs[2 * count], refs[2 * count + 1 : -1], refs[-1]
+    loads = [
+        pltpu.make_async_copy(source, target, sems.at[n])
+        for n, (source, target) in enumerate(zip(sources, held))
+    ]
+    for load in loads:
+        load.start()
     scales = branch_scales(guidance_ref)
-    total = acc_ref[...]
+    for load in loads:
+        load.wait()
+    total = held[-1][...]
     for b in range(modulation_ref.shape[0]):
-        part = dot(pairs[0][b], pairs[half][...])
-        for n in range(1, half):
-            part = part + dot(pairs[n][b], pairs[half + n][...])
+        part = dot(held[0][b], held[count][...])
+        for n in range(1, count):
+            part = part + dot(held[n][b], held[count + n][...])
         total = total + part * (scales[b] * modulation_ref[b, 2:3, :])
     if out_parts is None:
         out_ref[...] = total.astype(BF16)
@@ -260,8 +359,18 @@
             out_ref[:, h] = piece.reshape(senders, share, columns)
 
 
-def return_kernel(placing_ref, rows_ref, out_ref):
-    out_ref[...] = dot(placing_ref[...], rows_ref[...]).astype(BF16)
+def return_kernel(placed_ref, rows_hbm, out_ref, rows_ref, sem):
+    load = pltpu.make_async_copy(rows_hbm, rows_ref, sem)
+    load.start()
+    voxels = placed_ref.shape[1]
+    column = jnp.broadcast_to(placed_ref[...], (128, voxels)).T
+    column = column.astype(jnp.int32)
+    lane = iota((voxels, 128), 1)
+    placing = jnp.concatenate(
+        [(column == lane + start).astype(F32).astype(BF16) for start in range(0, SLOTS, 128)], axis=1
+    )
+    load.wait()
+    out_ref[...] = dot(placing, rows_ref[...]).astype(BF16)
 
 
 def on_device(x_latent, windows, coords, modulation, w_qkv, w_out, qk_gain, guidance):
@@ -276,17 +385,20 @@
     queries = SLOTS // heads
     share = capacity // heads
 
-    outgoing, placing = pl.pallas_call(
+    tile = group // cores
+    vmem, dma = pltpu.VMEM, pltpu.SemaphoreType.DMA
+    outgoing, placed = pl.pallas_call(
         functools.partial(place_kernel, senders, capacity),
         out_shape=(
             jax.ShapeDtypeStruct((SLOTS, width + EXTRA), BF16),
-            jax.ShapeDtypeStruct((SLOTS, voxels), BF16),
+            jax.ShapeDtypeStruct((1, voxels), F32),
         ),
-        in_specs=[VMEM] * 3,
+        in_specs=[VMEM, VMEM, HBM],
         out_specs=(VMEM, VMEM),
+        scratch_shapes=[vmem((voxels, width), BF16), dma(())],
         compiler_params=params(16),
         name="place",
-    )(windows.reshape(1, voxels), coords, x_latent)
+    )(windows, coords, x_latent)
     arrived = lax.all_to_all(
         outgoing.reshape(senders, capacity, width + EXTRA),
         ("cfg", "vox"),
@@ -299,18 +411,21 @@
         (w_qkv, w_out, qk_gain, outgoing)
     )
     del outgoing_done
-    tile = group // cores
     start = lax.axis_index("cfg") * tile
     half = jnp.transpose(lax.dynamic_slice_in_dim(w_qkv, start, tile, 2), (1, 2, 0))
     out_half = lax.dynamic_slice_in_dim(w_out_sent, start, tile, 0)
-    gain_half = lax.dynamic_slice_in_dim(qk_gain, start, tile, 1)
     swap = [(c, (c + 1) % cores) for c in range(cores)]
-    fetched = []
+    fetched, gain_columns = [], []
     for distance in range(1, heads):
         turn = [(h, (h + distance) % heads) for h in range(heads)]
-        fetched.append(tuple(lax.ppermute(a, "head", turn) for a in (half, gain_half, out_half)))
-
+        fetched.append((lax.ppermute(half, "head", turn), lax.ppermute(out_half, "head", turn)))
+        gain_columns.append(lax.ppermute(qk_gain, "head", turn).T)
+    own_gain = qk_gain.T
     table = position_parts(width)
+    arrived, own_gain, table, *gain_columns = lax.optimization_barrier(
+        (arrived, own_gain, table, *gain_columns)
+    )
+
     normed, normed_q, acc, bias = pl.pallas_call(
         functools.partial(own_kernel, senders, head_size),
         out_shape=(
@@ -319,40 +434,66 @@
             jax.ShapeDtypeStruct((queries, width), F32),
             jax.ShapeDtypeStruct((8, SLOTS), F32),
         ),
-        in_specs=[SMEM] + [VMEM] * 6,
-        out_specs=(VMEM,) * 4,
-        scratch_shapes=[pltpu.VMEM((SLOTS, width), F32), pltpu.VMEM((queries, group), BF16)],
-        compiler_params=params(26),
+        in_specs=[SMEM, VMEM] + [HBM] * 5,
+        out_specs=(HBM,) * 4,
+        scratch_shapes=[
+            vmem((SLOTS, width + EXTRA), BF16),
+            vmem(table.shape, BF16),
+            vmem((3, group, width), BF16),
+            vmem((group, 2), F32),
+            vmem((group, width), BF16),
+            vmem((branches, SLOTS, width), BF16),
+            vmem((branches, queries, width), BF16),
+            vmem((queries, width), F32),
+            vmem((8, SLOTS), F32),
+            vmem((SLOTS, width), F32),
+            vmem((queries, group), BF16),
+            dma((5,)),
+            dma((4,)),
+        ],
+        compiler_params=params(40),
         name="own_heads",
     )(
         guidance,
+        modulation,
         arrived,
         table,
-        modulation,
         jnp.transpose(w_qkv, (1, 2, 0)),
-        qk_gain[:, :, None],
+        own_gain,
         w_out,
     )
 
-    def attend(weights, gain):
+    def attend(weights, gain, swapped):
         return pl.pallas_call(
-            functools.partial(other_kernel, head_size),
+            functools.partial(other_kernel, head_size, swapped),
             out_shape=jax.ShapeDtypeStruct((branches, queries, tile), BF16),
-            in_specs=[VMEM] * 5,
-            out_specs=VMEM,
-            compiler_params=params(20),
+            in_specs=[HBM] * 5,
+            out_specs=HBM,
+            scratch_shapes=[
+                vmem((branches, SLOTS, width), BF16),
+                vmem((branches, queries, width), BF16),
+                vmem((8, SLOTS), F32),
+                vmem((3, tile, width), BF16),
+                vmem((group, 2), F32),
+                vmem((branches, queries, tile), BF16),
+                dma((3,)),
+                dma((branches,)),
+                dma((branches,)),
+                dma((branches,)),
+            ],
+            compiler_params=params(32),
             name="other_heads",
-        )(normed, normed_q, bias, weights, gain[:, :, None])
+        )(normed, normed_q, bias, weights, gain)
 
     attended, outs = [], []
     ahead = bias
-    for weights, gain, out_rows in fetched:
-        weights, gain, ahead = lax.optimization_barrier((weights, gain, ahead))
-        swapped = lax.ppermute(weights, "cfg", swap), lax.ppermute(gain, "cfg", swap)
-        mine = attend(weights, gain)
+    for (weights, out_rows), gain in zip(fetched, gain_columns):
+        weights, ahead = lax.optimization_barrier((weights, ahead))
+        swapped = lax.ppermute(weights, "cfg", swap)
+        mine = attend(weights, gain, False)
         out_rows, mine = lax.optimization_barrier((out_rows, mine))
         out_swapped = lax.ppermute(out_rows, "cfg", swap)
-        theirs = attend(*swapped)
+        theirs = attend(swapped, gain, True)
         ahead = theirs
         attended += [mine, theirs]
         outs += [out_rows, out_swapped]
@@ -362,14 +503,18 @@
     if share % 16 == 0:
         parts = (senders, heads, share, width // heads)
         shape = jax.ShapeDtypeStruct(parts, BF16)
+    count = len(outs)
     acc = pl.pallas_call(
-        functools.partial(finish_kernel, parts),
+        functools.partial(finish_kernel, parts, count),
         out_shape=shape,
-        in_specs=[SMEM] + [VMEM] * (2 + 2 * len(outs)),
+        in_specs=[SMEM, VMEM] + [HBM] * (1 + 2 * count),
         out_specs=VMEM,
-        compiler_params=params(20),
+        scratch_shapes=[vmem((branches, queries, tile), BF16)] * count
+        + [vmem((tile, width), BF16)] * count
+        + [vmem((queries, width), F32), dma((2 * count + 1,))],
+        compiler_params=params(32),
         name="finish",
-    )(guidance, acc, modulation, *attended, *outs)
+    )(guidance, modulation, acc, *attended, *outs)
     if share % 16 != 0:
         acc = acc.reshape(senders, share, heads, width // heads).transpose(0, 2, 1, 3)
     back = lax.all_to_all(
@@ -382,11 +527,12 @@
     return pl.pallas_call(
         return_kernel,
         out_shape=jax.ShapeDtypeStruct((voxels, width // heads), BF16),
-        in_specs=[VMEM] * 2,
+        in_specs=[VMEM, HBM],
         out_specs=VMEM,
+        scratch_shapes=[vmem((SLOTS, width // heads), BF16), dma(())],
         compiler_params=params(16),
         name="return_rows",
-    )(placing.T, back.reshape(SLOTS, width // heads))
+    )(placed, back.reshape(SLOTS, width // heads))
 
 
 def solution(mesh):

time: 119 us -> 128 us (1.076)
  blocking collectives: 0 us -> 22.4 us
  local copies, waits for them, and re-layouts: 25.4 us -> 10.4 us
  waiting for transfers between devices: 38.1 us -> 43.4 us
  starting transfers between devices: 14.8 us -> 11.2 us
    ppermute x5 -> x4, waiting for transfers between devices: 1.51 us -> 43.4 us  [the longest x1 38.5 us: on_device(): gain_columns.append(lax.ppermute(qk_gain, 'head', turn).T)]
    all_to_all x0 -> x1, blocking collectives: none -> 22.4 us  [on_device(): lax.all_to_all(acc.reshape(senders * heads, share, width // heads), ('cfg...]
    all_to_all x1, waiting for transfers between devices: 19.9 us -> 0.01 us  [on_device(): lax.all_to_all(outgoing.reshape(senders, capacity, width + EXTRA), ('cfg'...]
    all_to_all x1 -> x0, waiting for transfers between devices: 16.6 us -> none  [on_device(): lax.all_to_all(acc.reshape(senders * heads, share, width // heads), ('cfg...]
    unnamed x48 -> x20, local copies, waits for them, and re-layouts: 15.7 us -> 5.72 us
    broadcast_in_dim x3 -> x0, local copies, waits for them, and re-layouts: 3.4 us -> none  [the longest x2 2.37 us: attend(): gain[:, :, None]]
    all_to_all x1 -> x0, starting transfers between devices: 3.26 us -> none  [on_device(): lax.all_to_all(acc.reshape(senders * heads, share, width // heads), ('cfg...]
    ppermute x5 -> x4, starting transfers between devices: 4.14 us -> 3.76 us  [the longest x1 1.59 us: on_device(): lax.ppermute(out_half, 'head', turn)]
  transfers between devices with their start and end apart: 8 -> 6, of which waited for: 4 -> 2; matrix products, arithmetic and copies ran while one was open for 9% -> 5% of each run, Pallas kernels for 27% -> 26%
where the time goes in v3:
time: 128 us
  waiting for transfers between devices  43.4 us (34%)
  Pallas kernels  38.3 us (30%)
  blocking collectives  22.4 us (18%)
  starting transfers between devices  11.2 us (9%)
  local copies, waits for them, and re-layouts  10.4 us (8%)
  other arithmetic  1.67 us (1%)
    ppermute x1, waiting for transfers between devices, on_device(): gain_columns.append(lax.ppermute(qk_gain, 'head', turn).T)  38.5 us
    all_to_all x1, blocking collectives, on_device(): lax.all_to_all(acc.reshape(senders * heads, share, width // heads), ('cfg...  22.4 us
    pallas_call x1, Pallas kernels, on_device(): pl.pallas_call(functools.partial(own_kernel, senders, head_size), out_sha...  17.7 us
    pallas_call x2, Pallas kernels, attend(): pl.pallas_call(functools.partial(other_kernel, head_size, swapped), out_s...  14.9 us
    all_to_all x1, starting transfers between devices, on_device(): lax.all_to_all(outgoing.reshape(senders, capacity, width + EXTRA), ('cfg'...  7.42 us
    unnamed x20, local copies, waits for them, and re-layouts  5.72 us
    ppermute x1, waiting for transfers between devices, on_device(): lax.ppermute(out_half, 'head', turn)  4.86 us
    optimization_barrier x2, local copies, waits for them, and re-layouts, on_device(): lax.optimization_barrier((w_qkv, w_out, qk_gain, outgoing))  3.33 us
  transfers between devices with their start and end apart: 6, of which 2 were waited for; matrix products, arithmetic and copies ran while one was open for 5% of the time, Pallas kernels for 26%

profile of v3, /device:TPU:0, one launch (start us, length us, event | category | flops | bytes accessed | tf_op | source)
XLA Modules:
  0.0 127.5 jit_solution(3392824967634405857)
XLA Ops:
  0.0 0.0 copy-start.4
  0.0 1.1 copy-done.4
  1.1 0.0 copy-start.6
  1.1 0.7 copy-done.6
  1.8 0.0 copy-start.7
  1.8 0.7 copy-done.7
  2.5 2.3 %place.1 = (bf16[512,1152]{1,0:T(8,128)(2,1)}, f32[1,384]{1,0:T(1,128)S(1)}) custom-call(s32[384]{0:T(512)S(1)} %copy-done.7, s32[3,384]{1,0:T(4,128)S(1)} %copy-done.6, bf16[384,1024]{1,0:T(8,128)(2,1)S(1)} %copy-done.4), custom_call_target="tpu_custom_call" | custom-call | tf_op jit(solution)/shard_map/place/pallas_call | solution.py:390
  4.8 7.4 %all-to-all-start = ((bf16[16,32,1152]{2,1,0:T(8,128)(2,1)}), bf16[16,32,1152]{2,1,0:T(8,128)(2,1)}, u32[]{:S(2)}, u32[]{:S(2)}) async-start(bf16[16,32,1152]{2,1,0:T(8,128)(2,1)} %bitcast), calls=%async_computation | async-start | bytes 2359296 | tf_op jit(solution)/shard_map/all_to_all | solution.py:402
  12.3 3.2 %copy.11 = bf16[1024,3,512]{0,2,1:T(8,128)(2,1)S(1)} copy(bf16[1024,3,512]{2,0,1:T(8,128)(2,1)} %param.12) | data formatting | bytes 6291456 | tf_op jit(solution)/shard_map/optimization_barrier | solution.py:410
  15.5 0.0 copy-start.9
  15.5 1.3 %dynamic-slice_bitcast_fusion = bf16[3,256,1024]{2,1,0:T(8,128)(2,1)} fusion(bf16[1024,3,512]{0,2,1:T(8,128)(2,1)S(1)} %copy.11, s32[]{:T(128)S(6)} %select_n.4), kind=kLoop, calls=%fused_computation | loop fusion | bytes 3145732 | tf_op jit(solution)/shard_map/transpose | solution.py:415
  16.8 1.5 %collective-permute-start.2 = (bf16[3,256,1024]{2,1,0:T(8,128)(2,1)}, bf16[3,256,1024]{2,1,0:T(8,128)(2,1)}, u32[]{:S(2)}, u32[]{:S(2)}) collective-permute-start(bf16[3,256,1024]{2,1,0:T(8,128)(2,1)} %dynamic-slice_bitcast_fusion), channel_id=1, source_target_pairs={{0,1},{1,0},{2,3},{3,2},{4,5},{5,4},{6,7},{7,6},{8,9},{9,8},{10,11... | collective-permute-start | bytes 4718600 | tf_op jit(solution)/shard_map/ppermute | solution.py:421
  18.3 0.0 copy-done.9
  18.3 0.1 copy.9
  18.5 0.6 collective-permute-start
  19.0 0.3 fusion.3
  19.3 0.1 pad_maximum_fusion.1
  19.4 0.0 copy-start.5
  19.4 0.0 copy-start.8
  19.4 0.2 reduce-precision_convert_fusion.1
  19.6 1.1 pad_maximum_fusion.table_hbm
  20.7 38.5 %collective-permute-done = f32[2,512]{0,1:T(8,128)S(1)} collective-permute-done((f32[2,512]{0,1:T(8,128)S(1)}, f32[2,512]{0,1:T(8,128)S(1)}, u32[]{:S(2)}, u32[]{:S(2)}) %collective-permute-start) | collective-permute-done | bytes 4128 | tf_op jit(solution)/shard_map/ppermute | solution.py:422
  59.3 0.0 copy-start.2
  59.3 0.7 copy-done.2
  60.0 0.0 all-to-all-done
  60.0 0.0 copy-done.5
  60.0 0.0 copy-done.8
  60.0 0.0 copy-start
  60.0 1.3 copy-done
  61.2 0.0 copy-start.1
  61.3 1.2 copy-done.1
  62.5 0.0 copy-start.3
  62.5 17.7 %own_heads.1 = (bf16[3,512,1024]{2,1,0:T(8,128)(2,1)S(1)}, bf16[3,256,1024]{2,1,0:T(8,128)(2,1)S(1)}, f32[256,1024]{1,0:T(8,128)S(1)}, f32[8,512]{1,0:T(8,128)S(1)}) custom-call(f32[2]{0:T(128)S(1)} %copy-done.8, f32[3,3,1024]{2,1,0:T(4,128)S(1)} %copy-done.5, bf16[512,1152]{1,0:T(8,128)(2,1)} %bitcast.1.rows_hbm, bf16[576,1024]{1,0:T(8,128)(2,1)S(1)} %copy-done, ...), custom_call_target="tpu_custom_call" | custom-call | tf_op jit(solution)/shard_map/own_heads/pallas_call | solution.py:429
  80.1 0.0 collective-permute-done.2.w_hbm
  80.1 0.1 collective-permute-start.3
  80.3 1.6 %collective-permute-start.1 = (bf16[256,1024]{1,0:T(8,128)(2,1)S(1)}, bf16[256,1024]{1,0:T(8,128)(2,1)S(1)}, u32[]{:S(2)}, u32[]{:S(2)}) collective-permute-start(bf16[256,1024]{1,0:T(8,128)(2,1)S(1)} %constant_dynamic-slice_fusion), channel_id=1, source_target_pairs={{0,1},{1,0},{2,3},{3,2},{4,5},{5,4},{6,7},{7,6},{8,9},{9,8},{10,11... | collective-permute-start | bytes 1572872 | tf_op jit(solution)/shard_map/ppermute | solution.py:421
  81.9 0.0 copy-done.3
  81.9 7.9 %other_heads.2.refs_0_ = bf16[3,256,256]{2,1,0:T(8,128)(2,1)S(1)} custom-call(bf16[3,512,1024]{2,1,0:T(8,128)(2,1)S(1)} %get-tuple-element.30.normed_hbm, bf16[3,256,1024]{2,1,0:T(8,128)(2,1)S(1)} %get-tuple-element.31.normed_q_hbm, f32[8,512]{1,0:T(8,128)S(1)} %get-tuple-element.32.bias_hbm, bf16[3,256,1024]{2,1,0:T(8,128)(2,1)} %collective-permute-done.2.w_hbm, ...), custom_call_target="tpu_custom_call" | custom-call | tf_op jit(solution)/shard_map/other_heads/pallas_call | solution.py:467
  89.8 4.9 %collective-permute-done.1.refs_2_ = bf16[256,1024]{1,0:T(8,128)(2,1)S(1)} collective-permute-done((bf16[256,1024]{1,0:T(8,128)(2,1)S(1)}, bf16[256,1024]{1,0:T(8,128)(2,1)S(1)}, u32[]{:S(2)}, u32[]{:S(2)}) %collective-permute-start.1) | collective-permute-done | bytes 524320 | tf_op jit(solution)/shard_map/ppermute | solution.py:421
  94.7 0.0 collective-permute-start.4
  94.7 0.0 collective-permute-done.3.w_hbm
  94.7 7.0 %other_heads.3.refs_1_ = bf16[3,256,256]{2,1,0:T(8,128)(2,1)S(1)} custom-call(bf16[3,512,1024]{2,1,0:T(8,128)(2,1)S(1)} %get-tuple-element.30.normed_hbm, bf16[3,256,1024]{2,1,0:T(8,128)(2,1)S(1)} %get-tuple-element.31.normed_q_hbm, f32[8,512]{1,0:T(8,128)S(1)} %get-tuple-element.32.bias_hbm, bf16[3,256,1024]{2,1,0:T(8,128)(2,1)S(1)} %collective-permute-done.3.w_hbm, ...), custom_call_target="tpu_custom_call" | custom-call | tf_op jit(solution)/shard_map/other_heads/pallas_call | solution.py:467
  101.7 0.0 collective-permute-done.4.refs_3_
  101.7 2.1 %finish.1 = bf16[16,2,16,512]{3,2,1,0:T(8,128)(2,1)S(1)} custom-call(f32[2]{0:T(128)S(1)} %copy-done.8, f32[3,3,1024]{2,1,0:T(4,128)S(1)} %copy-done.5, f32[256,1024]{1,0:T(8,128)S(1)} %get-tuple-element.28.acc_hbm, bf16[3,256,256]{2,1,0:T(8,128)(2,1)S(1)} %other_heads.2.refs_0_, bf16[3,256,256]{2,1,0:T(8,128)(2,1)S(1)} %other_heads.3.refs_1_, ...), custom_call_target="tpu_custom_call" | custom-call | tf_op jit(solution)/shard_map/finish/pallas_call | solution.py:507
  103.8 22.4 %all_to_all.10 = bf16[32,16,512]{2,1,0:T(8,128)(2,1)S(1)} all-to-all(bf16[32,16,512]{2,1,0:T(8,128)(2,1)S(1)} %bitcast.11), channel_id=1, replica_groups=mesh['cfg'=2,'vox'=8,'head'=2] {'cfg','vox','head'}, dimensions={0} | all-to-all | bytes 1048576 | tf_op jit(solution)/shard_map/all_to_all | solution.py:520
  126.2 1.3 %return_rows.1 = bf16[384,512]{1,0:T(8,128)(2,1)} custom-call(f32[1,384]{1,0:T(1,128)S(1)} %get-tuple-element.21.placed_ref, bf16[512,512]{1,0:T(8,128)(2,1)S(1)} %bitcast.10), custom_call_target="tpu_custom_call" | custom-call | tf_op jit(solution)/shard_map/return_rows/pallas_call | solution.py:527
  (2 shorter events, 0.1 us)
Async XLA Ops:
  0.0 1.1 copy-start.4
  1.1 0.7 copy-start.6
  1.8 0.7 copy-start.7
  4.8 55.1 %all-to-all-start = ((bf16[16,32,1152]{2,1,0:T(8,128)(2,1)}), bf16[16,32,1152]{2,1,0:T(8,128)(2,1)}, u32[]{:S(2)}, u32[]{:S(2)}) async-start(bf16[16,32,1152]{2,1,0:T(8,128)(2,1)} %bitcast), calls=%async_computation | async-start | bytes 2359296 | tf_op jit(solution)/shard_map/all_to_all | solution.py:402
  15.5 2.8 %copy-start.9 = (f32[2,512]{1,0:T(2,128)S(1)}, f32[2,512]{1,0:T(2,128)}, u32[]{:S(2)}) copy-start(f32[2,512]{1,0:T(2,128)} %param.14) | copy-start | bytes 12292
  16.8 63.4 %collective-permute-start.2 = (bf16[3,256,1024]{2,1,0:T(8,128)(2,1)}, bf16[3,256,1024]{2,1,0:T(8,128)(2,1)}, u32[]{:S(2)}, u32[]{:S(2)}) collective-permute-start(bf16[3,256,1024]{2,1,0:T(8,128)(2,1)} %dynamic-slice_bitcast_fusion), channel_id=1, source_target_pairs={{0,1},{1,0},{2,3},{3,2},{4,5},{5,4},{6,7},{7,6},{8,9},{9,8},{10,11... | collective-permute-start | bytes 4718600 | tf_op jit(solution)/shard_map/ppermute | solution.py:421
  18.5 40.8 %collective-permute-start = (f32[2,512]{0,1:T(8,128)S(1)}, f32[2,512]{0,1:T(8,128)S(1)}, u32[]{:S(2)}, u32[]{:S(2)}) collective-permute-start(f32[2,512]{0,1:T(8,128)S(1)} %copy.9), channel_id=1, source_target_pairs={{0,1},{1,0},{2,3},{3,2},{4,5},{5,4},{6,7},{7,6},{8,9},{9,8},{10,11... | collective-permute-start | bytes 12296 | tf_op jit(solution)/shard_map/ppermute | solution.py:422
  19.4 40.6 %copy-start.5 = (f32[3,3,1024]{2,1,0:T(4,128)S(1)}, f32[3,3,1024]{2,1,0:T(4,128)}, u32[]{:S(2)}) copy-start(f32[3,3,1024]{2,1,0:T(4,128)} %modulation_ref.3) | copy-start | bytes 110596
  19.4 40.6 %copy-start.8 = (f32[2]{0:T(128)S(1)}, f32[2]{0:T(128)}, u32[]{:S(2)}) copy-start(f32[2]{0:T(128)} %guidance_ref.3) | copy-start | bytes 28
  59.3 0.7 copy-start.2
  60.0 1.3 copy-start
  61.2 1.2 copy-start.1
  62.5 19.4 %copy-start.3 = (f32[2,512]{0,1:T(8,128)S(1)}, f32[2,512]{0,1:T(8,128)}, u32[]{:S(2)}) copy-start(f32[2,512]{0,1:T(8,128)} %copy-done.2) | copy-start | bytes 12292
  80.1 14.5 %collective-permute-start.3 = (bf16[3,256,1024]{2,1,0:T(8,128)(2,1)}, bf16[3,256,1024]{2,1,0:T(8,128)(2,1)S(1)}, u32[]{:S(2)}, u32[]{:S(2)}) collective-permute-start(bf16[3,256,1024]{2,1,0:T(8,128)(2,1)} %collective-permute-done.2.w_hbm), channel_id=1, source_target_pairs={{0,16},{16,0},{1,17},{17,1},{2,18},{18,2},{3,19},{19,3},{4,20},{20... | collective-permute-start | bytes 4718600 | tf_op jit(solution)/shard_map/ppermute | solution.py:492
  80.3 14.4 %collective-permute-start.1 = (bf16[256,1024]{1,0:T(8,128)(2,1)S(1)}, bf16[256,1024]{1,0:T(8,128)(2,1)S(1)}, u32[]{:S(2)}, u32[]{:S(2)}) collective-permute-start(bf16[256,1024]{1,0:T(8,128)(2,1)S(1)} %constant_dynamic-slice_fusion), channel_id=1, source_target_pairs={{0,1},{1,0},{2,3},{3,2},{4,5},{5,4},{6,7},{7,6},{8,9},{9,8},{10,11... | collective-permute-start | bytes 1572872 | tf_op jit(solution)/shard_map/ppermute | solution.py:421
  94.7 7.0 %collective-permute-start.4 = (bf16[256,1024]{1,0:T(8,128)(2,1)S(1)}, bf16[256,1024]{1,0:T(8,128)(2,1)S(1)}, u32[]{:S(2)}, u32[]{:S(2)}) collective-permute-start(bf16[256,1024]{1,0:T(8,128)(2,1)S(1)} %collective-permute-done.1.refs_2_), channel_id=1, source_target_pairs={{0,16},{16,0},{1,17},{17,1},{2,18},{18,2},{3,19},{19,3},{4,20},{20... | collective-permute-start | bytes 1572872 | tf_op jit(solution)/shard_map/ppermute | solution.py:495

commit v4 on v3

--- a/solution.py
+++ b/solution.py
@@ -16,8 +16,8 @@
 VMEM = pl.BlockSpec(memory_space=pltpu.VMEM)
 SMEM = pl.BlockSpec(memory_space=pltpu.SMEM)
 HBM = pl.BlockSpec(memory_space=pltpu.HBM)
+LITTLE = pl.CostEstimate(flops=1, bytes_accessed=1, transcendentals=1)
 NT = (((1,), (1,)), ((), ()))
-TN = (((0,), (0,)), ((), ()))
 
 
 def params(megabytes):
@@ -49,10 +49,29 @@
     return jnp.concatenate([top, middle, low], axis=0).astype(BF16)
 
 
-def place_kernel(senders, capacity, windows_ref, coords_ref, x_hbm, out_ref, placed_ref, x_ref, sem):
-    load = pltpu.make_async_copy(x_hbm, x_ref, sem)
-    load.start()
+def place_kernel(
+    senders,
+    capacity,
+    windows_hbm,
+    coords_hbm,
+    x_hbm,
+    out_ref,
+    placed_ref,
+    x_ref,
+    windows_ref,
+    coords_ref,
+    sems,
+):
+    loads = [
+        pltpu.make_async_copy(source, target, sems.at[n])
+        for n, (source, target) in enumerate(
+            ((windows_hbm, windows_ref), (coords_hbm, coords_ref), (x_hbm, x_ref))
+        )
+    ]
+    for load in loads:
+        load.start()
     voxels, width = x_hbm.shape
+    loads[0].wait()
     windows = windows_ref[...].reshape(1, voxels)
     member = windows == iota((senders, voxels), 0)
     earlier = (iota((voxels, voxels), 0) < iota((voxels, voxels), 1)).astype(F32).astype(BF16)
@@ -62,6 +81,7 @@
     placed = windows * capacity + rank
     placed_ref[...] = placed.astype(F32)
     placing = (placed == iota((SLOTS, voxels), 0)).astype(F32).astype(BF16)
+    loads[1].wait()
     row = iota((EXTRA, voxels), 0)
     extra = jnp.where(row == 3, 1.0, 0.0).astype(F32)
     for c in range(3):
@@ -69,7 +89,7 @@
     out_ref[:, width:] = lax.dot_general(
         placing, extra.astype(BF16), NT, preferred_element_type=F32
     ).astype(BF16)
-    load.wait()
+    loads[2].wait()
     out_ref[:, :width] = dot(placing, x_ref[...]).astype(BF16)
 
 
@@ -333,8 +353,9 @@
 
 
 def finish_kernel(out_parts, count, guidance_ref, modulation_ref, acc_hbm, *refs):
-    sources = refs[: 2 * count] + (acc_hbm,)
-    out_ref, held, sems = refs[2 * count], refs[2 * count + 1 : -1], refs[-1]
+    arrays = (len(refs) - 2) // 2
+    sources = refs[:arrays] + (acc_hbm,)
+    out_ref, held, sems = refs[arrays], refs[arrays + 1 : -1], refs[-1]
     loads = [
         pltpu.make_async_copy(source, target, sems.at[n])
         for n, (source, target) in enumerate(zip(sources, held))
@@ -342,13 +363,20 @@
     for load in loads:
         load.start()
     scales = branch_scales(guidance_ref)
+    tile = held[0].shape[2]
+    core = lax.axis_index("cfg")
+    rows = [
+        pl.ds(pl.multiple_of(core * tile, tile), tile),
+        pl.ds(pl.multiple_of((1 - core) * tile, tile), tile),
+    ]
     for load in loads:
         load.wait()
     total = held[-1][...]
     for b in range(modulation_ref.shape[0]):
-        part = dot(held[0][b], held[count][...])
-        for n in range(1, count):
-            part = part + dot(held[n][b], held[count + n][...])
+        part = None
+        for n in range(count):
+            term = dot(held[n][b], held[count + n // 2][rows[n % 2], :])
+            part = term if part is None else part + term
         total = total + part * (scales[b] * modulation_ref[b, 2:3, :])
     if out_parts is None:
         out_ref[...] = total.astype(BF16)
@@ -393,10 +421,15 @@
             jax.ShapeDtypeStruct((SLOTS, width + EXTRA), BF16),
             jax.ShapeDtypeStruct((1, voxels), F32),
         ),
-        in_specs=[VMEM, VMEM, HBM],
+        in_specs=[HBM] * 3,
         out_specs=(VMEM, VMEM),
-        scratch_shapes=[vmem((voxels, width), BF16), dma(())],
-        compiler_params=params(16),
+        scratch_shapes=[
+            vmem((voxels, width), BF16),
+            vmem(windows.shape, jnp.int32),
+            vmem(coords.shape, jnp.int32),
+            dma((3,)),
+        ],
+        compiler_params=params(64),
         name="place",
     )(windows, coords, x_latent)
     arrived = lax.all_to_all(
@@ -413,18 +446,21 @@
     del outgoing_done
     start = lax.axis_index("cfg") * tile
     half = jnp.transpose(lax.dynamic_slice_in_dim(w_qkv, start, tile, 2), (1, 2, 0))
-    out_half = lax.dynamic_slice_in_dim(w_out_sent, start, tile, 0)
     swap = [(c, (c + 1) % cores) for c in range(cores)]
-    fetched, gain_columns = [], []
-    for distance in range(1, heads):
-        turn = [(h, (h + distance) % heads) for h in range(heads)]
-        fetched.append((lax.ppermute(half, "head", turn), lax.ppermute(out_half, "head", turn)))
-        gain_columns.append(lax.ppermute(qk_gain, "head", turn).T)
+    turns = [[(h, (h + d) % heads) for h in range(heads)] for d in range(1, heads)]
+    count = group // senders
+    piece = lax.dynamic_slice_in_dim(w_out_sent, lax.axis_index(("cfg", "vox")) * count, count, 0)
+    first = [(lax.ppermute(qk_gain, "head", t), lax.ppermute(piece, "head", t)) for t in turns]
+    half, first = lax.optimization_barrier((half, first))
+    gain_columns = [gain.T for gain, _ in first]
+    fetched = [lax.ppermute(half, "head", turn) for turn in turns]
     own_gain = qk_gain.T
     table = position_parts(width)
-    arrived, own_gain, table, *gain_columns = lax.optimization_barrier(
-        (arrived, own_gain, table, *gain_columns)
-    )
+    pieces = [p for _, p in first]
+    arrived, own_gain, table, gain_columns, pieces = lax.optimization_barrier(
+        (arrived, own_gain, table, gain_columns, pieces)
+    )
+    outs = [lax.all_gather(p, ("cfg", "vox"), axis=0, tiled=True) for p in pieces]
 
     normed, normed_q, acc, bias = pl.pallas_call(
         functools.partial(own_kernel, senders, head_size),
@@ -451,7 +487,8 @@
             dma((5,)),
             dma((4,)),
         ],
-        compiler_params=params(40),
+        compiler_params=params(64),
+        cost_estimate=LITTLE,
         name="own_heads",
     )(
         guidance,
@@ -481,38 +518,35 @@
                 dma((branches,)),
                 dma((branches,)),
             ],
-            compiler_params=params(32),
+            compiler_params=params(64),
+            cost_estimate=LITTLE,
             name="other_heads",
         )(normed, normed_q, bias, weights, gain)
 
-    attended, outs = [], []
+    attended = []
     ahead = bias
-    for (weights, out_rows), gain in zip(fetched, gain_columns):
+    for weights, gain in zip(fetched, gain_columns):
         weights, ahead = lax.optimization_barrier((weights, ahead))
         swapped = lax.ppermute(weights, "cfg", swap)
-        mine = attend(weights, gain, False)
-        out_rows, mine = lax.optimization_barrier((out_rows, mine))
-        out_swapped = lax.ppermute(out_rows, "cfg", swap)
-        theirs = attend(swapped, gain, True)
-        ahead = theirs
-        attended += [mine, theirs]
-        outs += [out_rows, out_swapped]
+        attended.append(attend(weights, gain, False))
+        ahead = attend(swapped, gain, True)
+        attended.append(ahead)
 
     parts = None
     shape = jax.ShapeDtypeStruct((queries, width), BF16)
     if share % 16 == 0:
         parts = (senders, heads, share, width // heads)
         shape = jax.ShapeDtypeStruct(parts, BF16)
-    count = len(outs)
+    count = len(attended)
     acc = pl.pallas_call(
         functools.partial(finish_kernel, parts, count),
         out_shape=shape,
-        in_specs=[SMEM, VMEM] + [HBM] * (1 + 2 * count),
+        in_specs=[SMEM, VMEM] + [HBM] * (1 + count + len(outs)),
         out_specs=VMEM,
         scratch_shapes=[vmem((branches, queries, tile), BF16)] * count
-        + [vmem((tile, width), BF16)] * count
-        + [vmem((queries, width), F32), dma((2 * count + 1,))],
-        compiler_params=params(32),
+        + [vmem((group, width), BF16)] * len(outs)
+        + [vmem((queries, width), F32), dma((count + len(outs) + 1,))],
+        compiler_params=params(64),
         name="finish",
     )(guidance, modulation, acc, *attended, *outs)
     if share % 16 != 0:
@@ -530,7 +564,7 @@
         in_specs=[VMEM, HBM],
         out_specs=VMEM,
         scratch_shapes=[vmem((SLOTS, width // heads), BF16), dma(())],
-        compiler_params=params(16),
+        compiler_params=params(64),
         name="return_rows",
     )(placed, back.reshape(SLOTS, width // heads))
 

time: 128 us -> 119 us (0.930)
  waiting for transfers between devices: 43.4 us -> 17.8 us
  between operations: 0.17 us -> 13.6 us
  Pallas kernels: 38.3 us -> 46.6 us
  local copies, waits for them, and re-layouts: 10.4 us -> 6.33 us
  blocking collectives: 22.4 us -> 21.1 us
    ppermute x4 -> x3, waiting for transfers between devices: 43.4 us -> 1.75 us  [the longest x1 1.01 us: on_device(): lax.ppermute(qk_gain, 'head', t)]
    all_to_all x1, waiting for transfers between devices: 0.01 us -> 15.7 us  [on_device(): lax.all_to_all(outgoing.reshape(senders, capacity, width + EXTRA), ('cfg'...]
    unnamed x20 -> x8, local copies, waits for them, and re-layouts: 5.72 us -> 0.76 us
    pallas_call x2, Pallas kernels: 14.9 us -> 17.9 us  [attend(): pl.pallas_call(functools.partial(other_kernel, head_size, swapped), out_s...]
    pallas_call x1, Pallas kernels: 2.12 us -> 4.42 us  [on_device(): pl.pallas_call(functools.partial(finish_kernel, parts, count), out_shape=...]
    pallas_call x1, Pallas kernels: 1.31 us -> 2.84 us  [on_device(): pl.pallas_call(return_kernel, out_shape=jax.ShapeDtypeStruct((voxels, wid...]
    all_to_all x1, blocking collectives: 22.4 us -> 21.1 us  [on_device(): lax.all_to_all(acc.reshape(senders * heads, share, width // heads), ('cfg...]
    ppermute x4 -> x3, starting transfers between devices: 3.7 us -> 3.62 us  [the longest x1 1.6 us: on_device(): lax.ppermute(qk_gain, 'head', t)]
  transfers between devices with their start and end apart: 6 -> 6, of which waited for: 2 -> 4; matrix products, arithmetic and copies ran while one was open for 5% -> 6% of each run, Pallas kernels for 26% -> 31%
where the time goes in v4:
time: 119 us; the launch traced here: 118 us
  Pallas kernels  46.6 us (39%)
  blocking collectives  21.1 us (18%)
  waiting for transfers between devices  17.8 us (15%)
  between operations  13.6 us (11%)
  starting transfers between devices  11.2 us (9%)
  local copies, waits for them, and re-layouts  6.33 us (5%)
  other arithmetic  1.71 us (1%)
    all_to_all x1, blocking collectives, on_device(): lax.all_to_all(acc.reshape(senders * heads, share, width // heads), ('cfg...  21.1 us
    pallas_call x1, Pallas kernels, on_device(): pl.pallas_call(functools.partial(own_kernel, senders, head_size), out_sha...  18.4 us
    pallas_call x2, Pallas kernels, attend(): pl.pallas_call(functools.partial(other_kernel, head_size, swapped), out_s...  17.9 us
    all_to_all x1, waiting for transfers between devices, on_device(): lax.all_to_all(outgoing.reshape(senders, capacity, width + EXTRA), ('cfg'...  15.7 us
    all_to_all x1, starting transfers between devices, on_device(): lax.all_to_all(outgoing.reshape(senders, capacity, width + EXTRA), ('cfg'...  7.41 us
    pallas_call x1, Pallas kernels, on_device(): pl.pallas_call(functools.partial(finish_kernel, parts, count), out_shape=...  4.42 us
    optimization_barrier x2, local copies, waits for them, and re-layouts, on_device(): lax.optimization_barrier((w_qkv, w_out, qk_gain, outgoing))  3.32 us
    pallas_call x1, Pallas kernels, on_device(): pl.pallas_call(functools.partial(place_kernel, senders, capacity), out_sh...  3.02 us
  transfers between devices with their start and end apart: 6, of which 4 were waited for; matrix products, arithmetic and copies ran while one was open for 6% of the time, Pallas kernels for 31%

profile of v4, /device:TPU:0, one launch (start us, length us, event | category | flops | bytes accessed | tf_op | source)
XLA Modules:
  0.0 118.2 jit_solution(16790912742721375339)
XLA Ops:
  6.5 3.0 %place.1 = (bf16[512,1152]{1,0:T(8,128)(2,1)}, f32[1,384]{1,0:T(1,128)}) custom-call(s32[384]{0:T(512)} %windows_hbm.1, s32[3,384]{1,0:T(4,128)} %coords_hbm.1, bf16[384,1024]{1,0:T(8,128)(2,1)} %x_hbm.1), custom_call_target="tpu_custom_call" | custom-call | tf_op jit(solution)/shard_map/place/pallas_call | solution.py:418
  9.6 0.0 copy-start.3
  9.6 7.4 %all-to-all-start = ((bf16[16,32,1152]{2,1,0:T(8,128)(2,1)}), bf16[16,32,1152]{2,1,0:T(8,128)(2,1)}, u32[]{:S(2)}, u32[]{:S(2)}) async-start(bf16[16,32,1152]{2,1,0:T(8,128)(2,1)} %bitcast.12), calls=%async_computation | async-start | bytes 2359296 | tf_op jit(solution)/shard_map/all_to_all | solution.py:435
  17.0 0.0 all-gather.2.cloned.1.call-start
  17.0 0.0 copy-done.3
  17.1 0.1 copy.9
  17.2 0.0 copy-start.1
  17.2 1.6 %collective-permute-start = (f32[2,512]{0,1:T(8,128)S(1)}, f32[2,512]{0,1:T(8,128)}, u32[]{:S(2)}, u32[]{:S(2)}) collective-permute-start(f32[2,512]{0,1:T(8,128)S(1)} %copy.9), channel_id=1, source_target_pairs={{0,1},{1,0},{2,3},{3,2},{4,5},{5,4},{6,7},{7,6},{8,9},{9,8},{10,11... | collective-permute-start | bytes 12296 | tf_op jit(solution)/shard_map/ppermute | solution.py:453
  18.8 0.8 constant_dynamic-slice_fusion
  19.7 0.5 collective-permute-start.1
  20.2 3.2 %copy.10 = bf16[1024,3,512]{0,2,1:T(8,128)(2,1)S(1)} copy(bf16[1024,3,512]{2,0,1:T(8,128)(2,1)} %param.12) | data formatting | bytes 6291456 | tf_op jit(solution)/shard_map/optimization_barrier | solution.py:443
  23.4 0.0 copy-done.1
  23.4 0.0 copy-start
  23.4 1.4 %dynamic-slice_bitcast_fusion = bf16[3,256,1024]{2,1,0:T(8,128)(2,1)} fusion(bf16[1024,3,512]{0,2,1:T(8,128)(2,1)S(1)} %copy.10, s32[]{:T(128)S(6)} %select_n.6), kind=kLoop, calls=%fused_computation | loop fusion | bytes 3145732 | tf_op jit(solution)/shard_map/transpose | solution.py:448
  24.8 0.7 copy-done
  25.5 1.0 collective-permute-done
  26.5 0.7 collective-permute-done.1
  27.3 0.0 copy-start.2
  27.3 1.5 %collective-permute-start.2 = (bf16[3,256,1024]{2,1,0:T(8,128)(2,1)}, bf16[3,256,1024]{2,1,0:T(8,128)(2,1)}, u32[]{:S(2)}, u32[]{:S(2)}) collective-permute-start(bf16[3,256,1024]{2,1,0:T(8,128)(2,1)} %dynamic-slice_bitcast_fusion), channel_id=1, source_target_pairs={{0,1},{1,0},{2,3},{3,2},{4,5},{5,4},{6,7},{7,6},{8,9},{9,8},{10,11... | collective-permute-start | bytes 4718600 | tf_op jit(solution)/shard_map/ppermute | solution.py:456
  28.8 0.3 fusion.3
  29.1 0.1 pad_maximum_fusion.1
  29.1 0.2 reduce-precision_convert_fusion.1
  29.4 1.2 pad_maximum_fusion.table_hbm
  30.5 0.0 copy-done.2
  30.5 15.7 %all-to-all-done = bf16[16,32,1152]{2,1,0:T(8,128)(2,1)} async-done(((bf16[16,32,1152]{2,1,0:T(8,128)(2,1)}), bf16[16,32,1152]{2,1,0:T(8,128)(2,1)}, u32[]{:S(2)}, u32[]{:S(2)}) %all-to-all-start) | async-done | bytes 1179680 | tf_op jit(solution)/shard_map/all_to_all | solution.py:435
  46.2 0.0 all-gather.2.cloned.1.call-update
  46.2 18.4 %own_heads.1 = (bf16[3,512,1024]{2,1,0:T(8,128)(2,1)}, bf16[3,256,1024]{2,1,0:T(8,128)(2,1)}, f32[256,1024]{1,0:T(8,128)}, f32[8,512]{1,0:T(8,128)}) custom-call(f32[2]{0:T(128)} %guidance_ref.3, f32[3,3,1024]{2,1,0:T(4,128)} %modulation_ref.3, bf16[512,1152]{1,0:T(8,128)(2,1)} %bitcast.1.rows_hbm, bf16[576,1024]{1,0:T(8,128)(2,1)} %pad_maximum_fusion.table_hbm, ...), custom_call_target="tpu_custom_call" | custom-call | flops 1 | bytes 1 | tf_op jit(solution)/shard_map/own_heads/pallas_call | solution.py:465
  64.6 0.0 collective-permute-done.2.w_hbm
  64.6 0.1 collective-permute-start.3
  64.7 9.0 %other_heads.2.refs_0_ = bf16[3,256,256]{2,1,0:T(8,128)(2,1)} custom-call(bf16[3,512,1024]{2,1,0:T(8,128)(2,1)} %get-tuple-element.34.normed_hbm, bf16[3,256,1024]{2,1,0:T(8,128)(2,1)} %get-tuple-element.35.normed_q_hbm, f32[8,512]{1,0:T(8,128)} %get-tuple-element.36.bias_hbm, bf16[3,256,1024]{2,1,0:T(8,128)(2,1)} %collective-permute-done.2.w_hbm, ...), custom_call_target="tpu_custom_call" | custom-call | flops 1 | bytes 1 | tf_op jit(solution)/shard_map/other_heads/pallas_call | solution.py:504
  73.7 0.0 collective-permute-done.3.w_hbm
  73.7 9.0 %other_heads.3.refs_1_ = bf16[3,256,256]{2,1,0:T(8,128)(2,1)} custom-call(bf16[3,512,1024]{2,1,0:T(8,128)(2,1)} %get-tuple-element.34.normed_hbm, bf16[3,256,1024]{2,1,0:T(8,128)(2,1)} %get-tuple-element.35.normed_q_hbm, f32[8,512]{1,0:T(8,128)} %get-tuple-element.36.bias_hbm, bf16[3,256,1024]{2,1,0:T(8,128)(2,1)} %collective-permute-done.3.w_hbm, ...), custom_call_target="tpu_custom_call" | custom-call | flops 1 | bytes 1 | tf_op jit(solution)/shard_map/other_heads/pallas_call | solution.py:504
  82.7 0.3 all-gather.2.cloned.1.call-done.refs_2_
  83.0 4.4 %finish.1 = bf16[16,2,16,512]{3,2,1,0:T(8,128)(2,1)} custom-call(f32[2]{0:T(128)} %guidance_ref.3, f32[3,3,1024]{2,1,0:T(4,128)} %modulation_ref.3, f32[256,1024]{1,0:T(8,128)} %get-tuple-element.33.acc_hbm, bf16[3,256,256]{2,1,0:T(8,128)(2,1)} %other_heads.2.refs_0_, bf16[3,256,256]{2,1,0:T(8,128)(2,1)} %other_heads.3.refs_1_, ...), custom_call_target="tpu_custom_call" | custom-call | tf_op jit(solution)/shard_map/finish/pallas_call | solution.py:541
  87.4 21.1 %all_to_all.10 = bf16[32,16,512]{2,1,0:T(8,128)(2,1)} all-to-all(bf16[32,16,512]{2,1,0:T(8,128)(2,1)} %bitcast.11), channel_id=1, replica_groups=mesh['cfg'=2,'vox'=8,'head'=2] {'cfg','vox','head'}, dimensions={0} | all-to-all | bytes 1048576 | tf_op jit(solution)/shard_map/all_to_all | solution.py:554
  108.5 2.8 %return_rows.1 = bf16[384,512]{1,0:T(8,128)(2,1)} custom-call(f32[1,384]{1,0:T(1,128)} %get-tuple-element.23.placed_ref, bf16[512,512]{1,0:T(8,128)(2,1)} %bitcast.10), custom_call_target="tpu_custom_call" | custom-call | tf_op jit(solution)/shard_map/return_rows/pallas_call | solution.py:561
  (1 shorter events, 0.0 us)
Async XLA Ops:
  9.6 7.5 %copy-start.3 = (f32[2,512]{1,0:T(2,128)S(1)}, f32[2,512]{1,0:T(2,128)}, u32[]{:S(2)}) copy-start(f32[2,512]{1,0:T(2,128)} %param.14) | copy-start | bytes 12292
  9.6 36.6 %all-to-all-start = ((bf16[16,32,1152]{2,1,0:T(8,128)(2,1)}), bf16[16,32,1152]{2,1,0:T(8,128)(2,1)}, u32[]{:S(2)}, u32[]{:S(2)}) async-start(bf16[16,32,1152]{2,1,0:T(8,128)(2,1)} %bitcast.12), calls=%async_computation | async-start | bytes 2359296 | tf_op jit(solution)/shard_map/all_to_all | solution.py:435
  17.0 66.0 %all-gather.2.cloned.1.call-start = ((), (), s32[]{:S(2)}) async-start(), calls=%async_computation.2 | async-start | bytes 1114112 | tf_op jit(solution)/shard_map/all_gather | solution.py:463
  17.2 6.2 %copy-start.1 = (f32[2,512]{0,1:T(8,128)}, f32[2,512]{0,1:T(8,128)S(1)}, u32[]{:S(2)}) copy-start(f32[2,512]{0,1:T(8,128)S(1)} %copy.9) | copy-start | bytes 12292
  17.2 9.3 %collective-permute-start = (f32[2,512]{0,1:T(8,128)S(1)}, f32[2,512]{0,1:T(8,128)}, u32[]{:S(2)}, u32[]{:S(2)}) collective-permute-start(f32[2,512]{0,1:T(8,128)S(1)} %copy.9), channel_id=1, source_target_pairs={{0,1},{1,0},{2,3},{3,2},{4,5},{5,4},{6,7},{7,6},{8,9},{9,8},{10,11... | collective-permute-start | bytes 12296 | tf_op jit(solution)/shard_map/ppermute | solution.py:453
  19.7 7.6 %collective-permute-start.1 = (bf16[32,1024]{1,0:T(8,128)(2,1)S(1)}, bf16[32,1024]{1,0:T(8,128)(2,1)S(1)}, u32[]{:S(2)}, u32[]{:S(2)}) collective-permute-start(bf16[32,1024]{1,0:T(8,128)(2,1)S(1)} %constant_dynamic-slice_fusion), channel_id=1, source_target_pairs={{0,1},{1,0},{2,3},{3,2},{4,5},{5,4},{6,7},{7,6},{8,9},{9,8},{10,11... | collective-permute-start | bytes 196616 | tf_op jit(solution)/shard_map/ppermute | solution.py:453
  23.4 2.2 %copy-start = (bf16[1024,3,512]{0,2,1:T(8,128)(2,1)}, bf16[1024,3,512]{0,2,1:T(8,128)(2,1)S(1)}, u32[]{:S(2)}) copy-start(bf16[1024,3,512]{0,2,1:T(8,128)(2,1)S(1)} %copy.10) | copy-start | bytes 9437188
  27.3 3.3 %copy-start.2 = (bf16[32,1024]{1,0:T(8,128)(2,1)}, bf16[32,1024]{1,0:T(8,128)(2,1)S(1)}, u32[]{:S(2)}) copy-start(bf16[32,1024]{1,0:T(8,128)(2,1)S(1)} %collective-permute-done.1) | copy-start | bytes 196612
  27.3 37.3 %collective-permute-start.2 = (bf16[3,256,1024]{2,1,0:T(8,128)(2,1)}, bf16[3,256,1024]{2,1,0:T(8,128)(2,1)}, u32[]{:S(2)}, u32[]{:S(2)}) collective-permute-start(bf16[3,256,1024]{2,1,0:T(8,128)(2,1)} %dynamic-slice_bitcast_fusion), channel_id=1, source_target_pairs={{0,1},{1,0},{2,3},{3,2},{4,5},{5,4},{6,7},{7,6},{8,9},{9,8},{10,11... | collective-permute-start | bytes 4718600 | tf_op jit(solution)/shard_map/ppermute | solution.py:456
  64.6 9.1 %collective-permute-start.3 = (bf16[3,256,1024]{2,1,0:T(8,128)(2,1)}, bf16[3,256,1024]{2,1,0:T(8,128)(2,1)}, u32[]{:S(2)}, u32[]{:S(2)}) collective-permute-start(bf16[3,256,1024]{2,1,0:T(8,128)(2,1)} %collective-permute-done.2.w_hbm), channel_id=1, source_target_pairs={{0,16},{16,0},{1,17},{17,1},{2,18},{18,2},{3,19},{19,3},{4,20},{20... | collective-permute-start | bytes 4718600 | tf_op jit(solution)/shard_map/ppermute | solution.py:530
Sparse Core Ops, SparseCore 0:
  46.3 36.6 all-gather.1

commit v5 on v4

v5 whole, which is shorter than its diff:
```python
import functools

import jax
import jax.numpy as jnp
from jax import lax
from jax.experimental import pallas as pl
from jax.experimental.pallas import tpu as pltpu
from jax.sharding import PartitionSpec as P

HEADS = 16
SLOTS = 512
GRID = 64
EXTRA = 128
BF16 = jnp.bfloat16
F32 = jnp.float32
VMEM = pl.BlockSpec(memory_space=pltpu.VMEM)
SMEM = pl.BlockSpec(memory_space=pltpu.SMEM)
HBM = pl.BlockSpec(memory_space=pltpu.HBM)
NT = (((1,), (1,)), ((), ()))


def params(megabytes):
    return pltpu.CompilerParams(vmem_limit_bytes=megabytes * 1024 * 1024)


def iota(shape, dim):
    return lax.broadcasted_iota(jnp.int32, shape, dim)


def dot(a, b):
    return jnp.dot(a, b, preferred_element_type=F32)


def position_parts(model_width):
    freq_count = model_width // 3 // 2
    frequency = 1.0 / 10000.0 ** (jnp.arange(freq_count, dtype=F32) / freq_count)
    angles = jnp.arange(GRID, dtype=F32)[:, None] * frequency[None, :]
    block = jnp.concatenate([jnp.sin(angles), jnp.cos(angles)], axis=1)
    width = 2 * freq_count
    rows = [
        jnp.pad(block, ((0, 0), (c * width, model_width - (c + 1) * width))) for c in range(3)
    ]
    table = jnp.concatenate(rows, axis=0)
    top = lax.reduce_precision(table, 8, 7)
    rest = table - top
    middle = lax.reduce_precision(rest, 8, 7)
    low = rest - middle
    return jnp.concatenate([top, middle, low], axis=0).astype(BF16)


def place_kernel(
    senders,
    capacity,
    windows_hbm,
    coords_hbm,
    x_hbm,
    out_ref,
    placed_ref,
    x_ref,
    windows_ref,
    coords_ref,
    sems,
):
    loads = [
        pltpu.make_async_copy(source, target, sems.at[n])
        for n, (source, target) in enumerate(
            ((windows_hbm, windows_ref), (coords_hbm, coords_ref), (x_hbm, x_ref))
        )
    ]
    for load in loads:
        load.start()
    voxels, width = x_hbm.shape
    loads[0].wait()
    windows = windows_ref[...].reshape(1, voxels)
    member = windows == iota((senders, voxels), 0)
    earlier = (iota((voxels, voxels), 0) < iota((voxels, voxels), 1)).astype(F32).astype(BF16)
    member_f = member.astype(F32)
    before = dot(member_f.astype(BF16), earlier)
    rank = jnp.sum(before * member_f, axis=0, keepdims=True).astype(jnp.int32)
    placed = windows * capacity + rank
    placed_ref[...] = placed.astype(F32)
    placing = (placed == iota((SLOTS, voxels), 0)).astype(F32).astype(BF16)
    loads[1].wait()
    row = iota((EXTRA, voxels), 0)
    extra = jnp.where(row == 3, 1.0, 0.0).astype(F32)
    for c in range(3):
        extra = jnp.where(row == c, coords_ref[c : c + 1, :].astype(F32), extra)
    out_ref[:, width:] = lax.dot_general(
        placing, extra.astype(BF16), NT, preferred_element_type=F32
    ).astype(BF16)
    loads[2].wait()
    out_ref[:, :width] = dot(placing, x_ref[...]).astype(BF16)


def column_norm(rows, gain, head_size):
    blocks = []
    for start in range(0, rows.shape[0], head_size):
        block = rows[start : start + head_size]
        mean = jnp.sum(block * block, axis=0, keepdims=True) * (1.0 / head_size)
        blocks.append(block * lax.rsqrt(mean + 1e-06) * gain[start : start + head_size])
    return jnp.concatenate(blocks, axis=0).astype(BF16)


def project_keys(normed, w_key, gain, head_size):
    key = lax.dot_general(w_key, normed, NT, preferred_element_type=F32)
    return column_norm(key, gain, head_size)


def project_values(normed, w_value):
    return lax.dot_general(normed, w_value, NT, preferred_element_type=F32).astype(BF16)


def attend_tile(normed_q, w_query, gain, key, value, bias, head_size):
    queries, tile = normed_q.shape[0], w_query.shape[0]
    query = lax.dot_general(w_query, normed_q, NT, preferred_element_type=F32)
    query = column_norm(query, gain, head_size)
    query = (query.astype(F32) * (1.0 / head_size**0.5)).T
    lane_head = iota((queries, tile), 1) // head_size
    count = tile // head_size

    def score(head):
        return dot(jnp.where(lane_head == head, query, 0.0).astype(BF16), key)

    scores = score(0)
    mixed = jnp.zeros((queries, tile), F32)
    step = min(32, queries)
    for head in range(count):
        following = score(head + 1) if head + 1 < count else None
        pieces = []
        for r in range(0, queries, step):
            piece = scores[r : r + step] + bias
            weights = jnp.exp(piece - jnp.max(piece, axis=1, keepdims=True))
            total = jnp.sum(weights, axis=1, keepdims=True)
            pieces.append((weights * (1.0 / total)).astype(BF16))
        attend = jnp.concatenate(pieces, axis=0)
        mixed = jnp.where(lane_head == head, dot(attend, value), mixed)
        scores = following
    return mixed.astype(BF16)


def branch_scales(guidance_ref):
    g0, g1 = guidance_ref[0], guidance_ref[1]
    return 1.0 - g0, g0 - g1, g1


def pick_scale(b, scales):
    return jnp.where(b == 0, scales[0], jnp.where(b == 1, scales[1], scales[2]))


def copies(pairs, sems):
    return [
        pltpu.make_async_copy(source, target, sems.at[n])
        for n, (source, target) in enumerate(pairs)
    ]


def first_kernel(
    senders,
    head_size,
    guidance_ref,
    modulation_ref,
    rows_hbm,
    table_hbm,
    w_hbm,
    gain_hbm,
    w_out_hbm,
    normed_q_hbm,
    keys_hbm,
    values_hbm,
    residual_hbm,
    bias_hbm,
    sent_hbm,
    rows_ref,
    table_ref,
    w_ref,
    gain_ref,
    w_out_ref,
    normed_ref,
    normed_q_ref,
    keys_ref,
    values_ref,
    residual_ref,
    bias_ref,
    sent_ref,
    hidden_ref,
    att_ref,
    sum_ref,
    in_sems,
    out_sems,
    key_sems,
    value_sems,
):
    loads = copies(
        (
            (rows_hbm, rows_ref),
            (table_hbm, table_ref),
            (w_hbm, w_ref),
            (gain_hbm, gain_ref),
            (w_out_hbm, w_out_ref),
        ),
        in_sems,
    )
    stores = copies(
        (
            (normed_q_ref, normed_q_hbm),
            (bias_ref, bias_hbm),
            (residual_ref, residual_hbm),
            (sent_ref, sent_hbm),
        ),
        out_sems,
    )
    for load in loads:
        load.start()
    branches, slots, width = normed_ref.shape
    heads, _, queries, _ = normed_q_ref.shape
    group = att_ref.shape[1]
    capacity = slots // senders
    share = queries // senders
    me = lax.axis_index("head")
    scales = branch_scales(guidance_ref)
    total = (scales[0] + scales[1]) + scales[2]

    loads[0].wait()
    extra = rows_ref[:, width:]
    pick = ((iota((8, EXTRA), 1) == 3)).astype(F32).astype(BF16)
    live = lax.dot_general(pick, extra, NT, preferred_element_type=F32)
    bias_ref[...] = jnp.where(live > 0.5, 0.0, -1e30)
    stores[1].start()

    spots = extra.astype(F32)
    lane = iota((slots, 3 * GRID), 1)
    wanted = jnp.where(
        lane < GRID,
        spots[:, 0:1],
        jnp.where(lane < 2 * GRID, spots[:, 1:2], spots[:, 2:3]),
    )
    chosen = (wanted == (lane % GRID).astype(F32)).astype(F32).astype(BF16)
    chosen = jnp.concatenate([chosen, chosen, chosen], axis=1)
    loads[1].wait()
    hidden_ref[...] = dot(chosen, table_ref[...]) + rows_ref[:, :width].astype(F32)

    chunk = 32

    def normalise(i, carry):
        rows = pl.ds(pl.multiple_of(i * chunk, chunk), chunk)
        hidden = hidden_ref[rows, :]
        centred = hidden - jnp.mean(hidden, axis=1, keepdims=True)
        spread = jnp.mean(centred * centred, axis=1, keepdims=True)
        normal = centred * lax.rsqrt(spread + 1e-06)
        for b in range(branches):
            normed_ref[b, rows, :] = (
                normal * (1.0 + modulation_ref[b, 1:2, :]) + modulation_ref[b, 0:1, :]
            ).astype(BF16)
        return carry

    lax.fori_loop(0, slots // chunk, normalise, 0, unroll=2)

    for d in range(heads):
        first = lax.rem(me + d + 1, heads) * share
        if share % 16 == 0:
            for s in range(senders):
                source = pl.ds(pl.multiple_of(s * capacity + first, 16), share)
                target = slice(s * share, (s + 1) * share)
                if d == heads - 1:
                    residual_ref[target, :] = hidden_ref[source, :] * total
                for b in range(branches):
                    normed_q_ref[d, b, target, :] = normed_ref[b, source, :]
        else:
            row = iota((queries, slots), 0)
            wanted_slot = (row // share) * capacity + first + row % share
            chooser = (wanted_slot == iota((queries, slots), 1)).astype(F32)
            if d == heads - 1:
                picked = jnp.dot(
                    chooser,
                    hidden_ref[...],
                    preferred_element_type=F32,
                    precision=lax.Precision.HIGHEST,
                )
                residual_ref[...] = picked * total
            for b in range(branches):
                normed_q_ref[d, b] = dot(chooser.astype(BF16), normed_ref[b]).astype(BF16)
    stores[0].start()
    stores[2].start()

    bias = bias_ref[0:1, :]
    tile = min(256, group)
    for load in loads[2:]:
        load.wait()
    sum_ref[...] = jnp.zeros_like(sum_ref)

    def store(b):
        return (
            pltpu.make_async_copy(keys_ref.at[b], keys_hbm.at[b], key_sems.at[b]),
            pltpu.make_async_copy(values_ref.at[b], values_hbm.at[b], value_sems.at[b]),
        )

    def branch(b, carry):
        for start in range(0, group, tile):
            features = slice(start, start + tile)
            gains = gain_ref[features, :]
            key = project_keys(normed_ref[b], w_ref[1, features, :], gains[:, 1:2], head_size)
            value = project_values(normed_ref[b], w_ref[2, features, :])
            keys_ref[b, features, :] = key
            values_ref[b, :, features] = value
            att_ref[:, features] = attend_tile(
                normed_q_ref[0, b],
                w_ref[0, features, :],
                gains[:, 0:1],
                key,
                value,
                bias,
                head_size,
            )
        for copy in store(b):
            copy.start()
        sum_ref[...] += dot(att_ref[...], w_out_ref[...]) * (
            pick_scale(b, scales) * modulation_ref[b, 2:3, :]
        )
        return carry

    lax.fori_loop(0, branches, branch, 0)
    sent_ref[...] = sum_ref[...].astype(BF16)
    stores[3].start()
    for copy in stores:
        copy.wait()
    for b in range(branches):
        for copy in store(b):
            copy.wait()


def query_kernel(
    head_size,
    distance,
    guidance_ref,
    modulation_ref,
    normed_q_hbm,
    keys_hbm,
    values_hbm,
    bias_hbm,
    w_hbm,
    gain_hbm,
    w_out_hbm,
    out_hbm,
    normed_q_ref,
    keys_ref,
    values_ref,
    bias_ref,
    w_ref,
    gain_ref,
    w_out_ref,
    sum_ref,
    out_ref,
    att_ref,
    in_sems,
    query_sems,
    key_sems,
    value_sems,
    out_sem,
):
    branches, _, slots = keys_ref.shape
    group = att_ref.shape[1]
    loads = copies(
        (
            (w_hbm.at[0], w_ref),
            (gain_hbm, gain_ref),
            (bias_hbm, bias_ref),
            (w_out_hbm, w_out_ref),
        ),
        in_sems,
    )

    def load(b):
        return (
            pltpu.make_async_copy(
                normed_q_hbm.at[distance, b], normed_q_ref.at[b], query_sems.at[b]
            ),
            pltpu.make_async_copy(keys_hbm.at[b], keys_ref.at[b], key_sems.at[b]),
            pltpu.make_async_copy(values_hbm.at[b], values_ref.at[b], value_sems.at[b]),
        )

    loads[0].start()
    for copy in load(0):
        copy.start()
    for copy in loads[1:]:
        copy.start()
    for b in range(1, branches):
        for copy in load(b):
            copy.start()
    scales = branch_scales(guidance_ref)
    tile = min(256, group)
    sum_ref[...] = jnp.zeros_like(sum_ref)
    for copy in loads:
        copy.wait()
    bias = bias_ref[0:1, :]

    def branch(b, carry):
        for copy in load(b):
            copy.wait()
        for start in range(0, group, tile):
            features = slice(start, start + tile)
            att_ref[:, features] = attend_tile(
                normed_q_ref[b],
                w_ref[features, :],
                gain_ref[features, 0:1],
                keys_ref[b, features, :],
                values_ref[b, :, features],
                bias,
                head_size,
            )
        sum_ref[...] += dot(att_ref[...], w_out_ref[...]) * (
            pick_scale(b, scales) * modulation_ref[b, 2:3, :]
        )
        return carry

    lax.fori_loop(0, branches, branch, 0)
    out_ref[...] = sum_ref[...].astype(out_ref.dtype)
    store = pltpu.make_async_copy(out_ref, out_hbm, out_sem)
    store.start()
    store.wait()


def finish_kernel(out_parts, *refs):
    arrays = (len(refs) - 2) // 2
    out_ref, held, sems = refs[arrays], refs[arrays + 1 : -1], refs[-1]
    loads = copies(zip(refs[:arrays], held), sems)
    for load in loads:
        load.start()
    for load in loads:
        load.wait()
    step = 32 if out_parts is not None else held[0].shape[0]
    for r in range(0, held[0].shape[0], step):
        total = held[0][r : r + step, :]
        for term in held[1:]:
            total = total + term[r : r + step, :].astype(F32)
        if out_parts is None:
            out_ref[r : r + step, :] = total.astype(BF16)
        else:
            senders, heads, share, columns = out_parts
            for h in range(heads):
                piece = total[:, h * columns : (h + 1) * columns].astype(BF16)
                first = r // share
                out_ref[first : first + step // share, h] = piece.reshape(
                    step // share, share, columns
                )


def return_kernel(placed_ref, rows_hbm, out_ref, rows_ref, sem):
    load = pltpu.make_async_copy(rows_hbm, rows_ref, sem)
    load.start()
    voxels = placed_ref.shape[1]
    column = jnp.broadcast_to(placed_ref[...], (128, voxels)).T
    column = column.astype(jnp.int32)
    lane = iota((voxels, 128), 1)
    placing = jnp.concatenate(
        [(column == lane + start).astype(F32).astype(BF16) for start in range(0, SLOTS, 128)], axis=1
    )
    load.wait()
    out_ref[...] = dot(placing, rows_ref[...]).astype(BF16)


def on_device(x_latent, windows, coords, modulation, w_qkv, w_out, qk_gain, guidance):
    voxels, width = x_latent.shape
    group = w_qkv.shape[2]
    head_size = width // HEADS
    branches = modulation.shape[0]
    senders = lax.axis_size(("cfg", "vox"))
    heads = lax.axis_size("head")
    capacity = SLOTS // senders
    queries = SLOTS // heads
    share = capacity // heads

    vmem, dma = pltpu.VMEM, pltpu.SemaphoreType.DMA
    outgoing, placed = pl.pallas_call(
        functools.partial(place_kernel, senders, capacity),
        out_shape=(
            jax.ShapeDtypeStruct((SLOTS, width + EXTRA), BF16),
            jax.ShapeDtypeStruct((1, voxels), F32),
        ),
        in_specs=[HBM] * 3,
        out_specs=(VMEM, VMEM),
        scratch_shapes=[
            vmem((voxels, width), BF16),
            vmem(windows.shape, jnp.int32),
            vmem(coords.shape, jnp.int32),
            dma((3,)),
        ],
        compiler_params=params(64),
        name="place",
    )(windows, coords, x_latent)
    arrived = lax.all_to_all(
        outgoing.reshape(senders, capacity, width + EXTRA),
        ("cfg", "vox"),
        split_axis=0,
        concat_axis=0,
        tiled=True,
    ).reshape(SLOTS, width + EXTRA)

    own_gain = qk_gain.T
    table = position_parts(width)
    flat = jnp.transpose(w_qkv, (1, 2, 0))
    arrived, own_gain, table, flat = lax.optimization_barrier((arrived, own_gain, table, flat))

    shapes = dict(
        normed_q=((heads, branches, queries, width), BF16),
        keys=((branches, group, SLOTS), BF16),
        values=((branches, SLOTS, group), BF16),
        residual=((queries, width), F32),
        bias=((8, SLOTS), F32),
        sent=((queries, width), BF16),
    )
    made = pl.pallas_call(
        functools.partial(first_kernel, senders, head_size),
        out_shape=tuple(jax.ShapeDtypeStruct(*shape) for shape in shapes.values()),
        in_specs=[SMEM, VMEM] + [HBM] * 5,
        out_specs=(HBM,) * 6,
        scratch_shapes=[
            vmem((SLOTS, width + EXTRA), BF16),
            vmem(table.shape, BF16),
            vmem((3, group, width), BF16),
            vmem((group, 2), F32),
            vmem((group, width), BF16),
            vmem((branches, SLOTS, width), BF16),
        ]
        + [vmem(*shape) for shape in shapes.values()]
        + [
            vmem((SLOTS, width), F32),
            vmem((queries, group), BF16),
            vmem((queries, width), F32),
            dma((5,)),
            dma((4,)),
            dma((branches,)),
            dma((branches,)),
        ],
        compiler_params=params(64),
        name="first_queries",
    )(guidance, modulation, arrived, table, flat, own_gain, w_out)
    normed_q, keys, values, residual, bias, partial = made

    def attend(distance, dtype):
        return pl.pallas_call(
            functools.partial(query_kernel, head_size, distance),
            out_shape=jax.ShapeDtypeStruct((queries, width), dtype),
            in_specs=[SMEM, VMEM] + [HBM] * 7,
            out_specs=HBM,
            scratch_shapes=[
                vmem((branches, queries, width), BF16),
                vmem(*shapes["keys"]),
                vmem(*shapes["values"]),
                vmem(*shapes["bias"]),
                vmem((group, width), BF16),
                vmem((group, 2), F32),
                vmem((group, width), BF16),
                vmem((queries, width), F32),
                vmem((queries, width), dtype),
                vmem((queries, group), BF16),
                dma((4,)),
                dma((branches,)),
                dma((branches,)),
                dma((branches,)),
                dma(()),
            ],
            compiler_params=params(64),
            name="more_queries",
        )(guidance, modulation, normed_q, keys, values, bias, flat, own_gain, w_out)

    terms = []
    for distance in range(1, heads):
        turn = [(h, (h + distance) % heads) for h in range(heads)]
        terms.append(lax.ppermute(partial, "head", turn))
        last = distance == heads - 1
        partial = attend(distance, F32 if last else BF16)
    terms = [residual, partial] + terms

    parts = None
    shape = jax.ShapeDtypeStruct((queries, width), BF16)
    if share % 16 == 0:
        parts = (senders, heads, share, width // heads)
        shape = jax.ShapeDtypeStruct(parts, BF16)
    acc = pl.pallas_call(
        functools.partial(finish_kernel, parts),
        out_shape=shape,
        in_specs=[HBM] * len(terms),
        out_specs=VMEM,
        scratch_shapes=[vmem((queries, width), term.dtype) for term in terms] + [dma((len(terms),))],
        compiler_params=params(64),
        name="finish",
    )(*terms)
    if share % 16 != 0:
        acc = acc.reshape(senders, share, heads, width // heads).transpose(0, 2, 1, 3)
    back = lax.all_to_all(
        acc.reshape(senders * heads, share, width // heads),
        ("cfg", "vox", "head"),
        split_axis=0,
        concat_axis=0,
        tiled=True,
    )
    return pl.pallas_call(
        return_kernel,
        out_shape=jax.ShapeDtypeStruct((voxels, width // heads), BF16),
        in_specs=[VMEM, HBM],
        out_specs=VMEM,
        scratch_shapes=[vmem((SLOTS, width // heads), BF16), dma(())],
        compiler_params=params(64),
        name="return_rows",
    )(placed, back.reshape(SLOTS, width // heads))


def solution(mesh):
    placed = (
        P(("cfg", "vox"), None),
        P(("cfg", "vox")),
        P(None, ("cfg", "vox")),
        P(),
        P(None, None, "head"),
        P("head", None),
        P(None, "head"),
        P(),
    )
    return jax.shard_map(
        on_device, mesh=mesh, in_specs=placed, out_specs=P(("cfg", "vox"), "head"), check_vma=False
    )
```

time: 119 us -> 101 us (0.85)
  between operations: 13.6 us -> 0.09 us
  Pallas kernels: 46.6 us -> 42.2 us
  waiting for transfers between devices: 17.8 us -> 22 us
  starting transfers between devices: 11.2 us -> 9.02 us
    all_to_all x1, waiting for transfers between devices: 15.7 us -> 22 us  [on_device(): lax.all_to_all(outgoing.reshape(senders, capacity, width + EXTRA), ('cfg'...]
    unnamed x8 -> x4, local copies, waits for them, and re-layouts: 0.76 us -> 5.52 us
    pallas_call x4 -> x3, Pallas kernels: 40.7 us -> 36.4 us  [the longest x1 19.1 us: on_device(): pl.pallas_call(functools.partial(first_kernel, senders, head_size), out_s...]
    optimization_barrier x2 -> x0, local copies, waits for them, and re-layouts: 3.32 us -> none  [on_device(): lax.optimization_barrier((w_qkv, w_out, qk_gain, outgoing))]
    ppermute x4 -> x1, starting transfers between devices: 3.7 us -> 1.61 us  [on_device(): terms.append(lax.ppermute(partial, 'head', turn))]
    ppermute x4 -> x1, waiting for transfers between devices: 1.75 us -> 0.01 us  [on_device(): terms.append(lax.ppermute(partial, 'head', turn))]
    transpose x1 -> x0, local copies, waits for them, and re-layouts: 1.4 us -> none  [on_device(): jnp.transpose(lax.dynamic_slice_in_dim(w_qkv, start, tile, 2), (1, 2, 0))]
  transfers between devices with their start and end apart: 6 -> 2, of which waited for: 4 -> 1; matrix products, arithmetic and copies ran while one was open for 6% -> 7% of each run, Pallas kernels for 31% -> 15%
where the time goes in v5:
time: 101 us
  Pallas kernels  42.2 us (42%)
  waiting for transfers between devices  22 us (22%)
  blocking collectives  20.2 us (20%)
  starting transfers between devices  9.02 us (9%)
  local copies, waits for them, and re-layouts  5.52 us (5%)
  other arithmetic  1.66 us (2%)
    all_to_all x1, waiting for transfers between devices, on_device(): lax.all_to_all(outgoing.reshape(senders, capacity, width + EXTRA), ('cfg'...  22 us
    all_to_all x1, blocking collectives, on_device(): lax.all_to_all(acc.reshape(senders * heads, share, width // heads), ('cfg...  20.2 us
    pallas_call x1, Pallas kernels, on_device(): pl.pallas_call(functools.partial(first_kernel, senders, head_size), out_s...  19.1 us
    pallas_call x1, Pallas kernels, attend(): pl.pallas_call(functools.partial(query_kernel, head_size, distance), out_...  14.7 us
    all_to_all x1, starting transfers between devices, on_device(): lax.all_to_all(outgoing.reshape(senders, capacity, width + EXTRA), ('cfg'...  7.41 us
    unnamed x4, local copies, waits for them, and re-layouts  5.52 us
    pallas_call x1, Pallas kernels, on_device(): pl.pallas_call(functools.partial(place_kernel, senders, capacity), out_sh...  3.02 us
    pallas_call x1, Pallas kernels, on_device(): pl.pallas_call(return_kernel, out_shape=jax.ShapeDtypeStruct((voxels, wid...  2.82 us
  transfers between devices with their start and end apart: 2, of which 1 were waited for; matrix products, arithmetic and copies ran while one was open for 7% of the time, Pallas kernels for 15%

profile of v5, /device:TPU:0, one launch (start us, length us, event | category | flops | bytes accessed | tf_op | source)
XLA Modules:
  0.0 100.7 jit_solution(7210174263030752348)
XLA Ops:
  0.0 3.0 %place.1 = (bf16[512,1152]{1,0:T(8,128)(2,1)}, f32[1,384]{1,0:T(1,128)}) custom-call(s32[384]{0:T(512)} %windows_hbm.1, s32[3,384]{1,0:T(4,128)} %coords_hbm.1, bf16[384,1024]{1,0:T(8,128)(2,1)} %x_hbm.1), custom_call_target="tpu_custom_call" | custom-call | tf_op jit(solution)/shard_map/place/pallas_call | solution.py:473
  3.0 0.0 copy-start
  3.0 7.4 %all-to-all-start = ((bf16[16,32,1152]{2,1,0:T(8,128)(2,1)}), bf16[16,32,1152]{2,1,0:T(8,128)(2,1)}, u32[]{:S(2)}, u32[]{:S(2)}) async-start(bf16[16,32,1152]{2,1,0:T(8,128)(2,1)} %bitcast.12), calls=%async_computation | async-start | bytes 2359296 | tf_op jit(solution)/shard_map/all_to_all | solution.py:490
  10.5 0.0 copy-done
  10.5 0.9 copy.9
  11.3 4.7 %copy.10 = bf16[1024,3,512]{0,2,1:T(8,128)(2,1)} copy(bf16[1024,3,512]{2,0,1:T(8,128)(2,1)} %param.12) | data formatting | bytes 6291456 | tf_op args[4]
  16.0 0.3 fusion.3
  16.3 0.1 pad_maximum_fusion.1
  16.4 0.2 reduce-precision_convert_fusion.1
  16.6 1.1 %pad_maximum_fusion.table_hbm = bf16[576,1024]{1,0:T(8,128)(2,1)} fusion(bf16[192,1024]{1,0:T(8,128)(2,1)S(1)} %get-tuple-element.31, bf16[192,1024]{1,0:T(8,128)(2,1)S(1)} %get-tuple-element.30, bf16[192,1024]{1,0:T(8,128)(2,1)S(1)} %get-tuple-element.29), kind=kLoop, calls=%fused_computation.2 | loop fusion | flops 3538944 | bytes 2359296 | tf_op jit(solution)/shard_map/concatenate | solution.py:48
  17.7 22.0 %all-to-all-done = bf16[16,32,1152]{2,1,0:T(8,128)(2,1)} async-done(((bf16[16,32,1152]{2,1,0:T(8,128)(2,1)}), bf16[16,32,1152]{2,1,0:T(8,128)(2,1)}, u32[]{:S(2)}, u32[]{:S(2)}) %all-to-all-start) | async-done | bytes 1179680 | tf_op jit(solution)/shard_map/all_to_all | solution.py:490
  39.7 19.1 %first_queries.1 = (bf16[2,3,256,1024]{3,2,1,0:T(8,128)(2,1)}, bf16[3,512,512]{2,1,0:T(8,128)(2,1)}, bf16[3,512,512]{2,1,0:T(8,128)(2,1)}, f32[256,1024]{1,0:T(8...) custom-call(f32[2]{0:T(128)} %guidance_ref.3, f32[3,3,1024]{2,1,0:T(4,128)} %modulation_ref.3, ...), custom_call_target="tpu_custom_call" | custom-call | tf_op jit(solution)/shard_map/first_queries/pallas_call | solution.py:511
  58.7 1.6 %collective-permute-start = (bf16[256,1024]{1,0:T(8,128)(2,1)}, bf16[256,1024]{1,0:T(8,128)(2,1)}, u32[]{:S(2)}, u32[]{:S(2)}) collective-permute-start(bf16[256,1024]{1,0:T(8,128)(2,1)} %get-tuple-element.28), channel_id=1, source_target_pairs={{0,1},{1,0},{2,3},{3,2},{4,5},{5,4},{6,7},{7,6},{8,9},{9,8},{10,11... | collective-permute-start | bytes 1572872 | tf_op jit(solution)/shard_map/ppermute | solution.py:569
  60.3 14.7 %more_queries.1.refs_1_ = f32[256,1024]{1,0:T(8,128)} custom-call(f32[2]{0:T(128)} %guidance_ref.3, f32[3,3,1024]{2,1,0:T(4,128)} %modulation_ref.3, bf16[2,3,256,1024]{3,2,1,0:T(8,128)(2,1)} %get-tuple-element.24.normed_q_hbm, bf16[3,512,512]{2,1,0:T(8,128)(2,1)} %get-tuple-element.25.keys_hbm, bf16[3,512,512]{2,1,0:T(8,128)(2,1)} %get-tuple-element.26.values_hbm, ...), custom_call_target="tpu_custom_call" | custom-call | tf_op jit(solution)/shard_map/more_queries/pallas_call | solution.py:540
  75.1 0.0 collective-permute-done.refs_2_
  75.1 2.6 %finish.1 = bf16[16,2,16,512]{3,2,1,0:T(8,128)(2,1)} custom-call(f32[256,1024]{1,0:T(8,128)} %get-tuple-element.23.refs_0_, f32[256,1024]{1,0:T(8,128)} %more_queries.1.refs_1_, bf16[256,1024]{1,0:T(8,128)(2,1)} %collective-permute-done.refs_2_), custom_call_target="tpu_custom_call" | custom-call | tf_op jit(solution)/shard_map/finish/pallas_call | solution.py:579
  77.7 20.2 %all_to_all.10 = bf16[32,16,512]{2,1,0:T(8,128)(2,1)} all-to-all(bf16[32,16,512]{2,1,0:T(8,128)(2,1)} %bitcast.11), channel_id=1, replica_groups=mesh['cfg'=2,'vox'=8,'head'=2] {'cfg','vox','head'}, dimensions={0} | all-to-all | bytes 1048576 | tf_op jit(solution)/shard_map/all_to_all | solution.py:590
  97.8 2.8 %return_rows.1 = bf16[384,512]{1,0:T(8,128)(2,1)} custom-call(f32[1,384]{1,0:T(1,128)} %get-tuple-element.17.placed_ref, bf16[512,512]{1,0:T(8,128)(2,1)} %bitcast.10), custom_call_target="tpu_custom_call" | custom-call | tf_op jit(solution)/shard_map/return_rows/pallas_call | solution.py:597
  (1 shorter events, 0.0 us)
Async XLA Ops:
  3.0 7.4 %copy-start = (f32[2,512]{1,0:T(2,128)S(1)}, f32[2,512]{1,0:T(2,128)}, u32[]{:S(2)}) copy-start(f32[2,512]{1,0:T(2,128)} %param.14) | copy-start | bytes 12292
  3.0 36.6 %all-to-all-start = ((bf16[16,32,1152]{2,1,0:T(8,128)(2,1)}), bf16[16,32,1152]{2,1,0:T(8,128)(2,1)}, u32[]{:S(2)}, u32[]{:S(2)}) async-start(bf16[16,32,1152]{2,1,0:T(8,128)(2,1)} %bitcast.12), calls=%async_computation | async-start | bytes 2359296 | tf_op jit(solution)/shard_map/all_to_all | solution.py:490
  58.7 16.3 %collective-permute-start = (bf16[256,1024]{1,0:T(8,128)(2,1)}, bf16[256,1024]{1,0:T(8,128)(2,1)}, u32[]{:S(2)}, u32[]{:S(2)}) collective-permute-start(bf16[256,1024]{1,0:T(8,128)(2,1)} %get-tuple-element.28), channel_id=1, source_target_pairs={{0,1},{1,0},{2,3},{3,2},{4,5},{5,4},{6,7},{7,6},{8,9},{9,8},{10,11... | collective-permute-start | bytes 1572872 | tf_op jit(solution)/shard_map/ppermute | solution.py:569

commit v6 on v5

--- a/solution.py
+++ b/solution.py
@@ -16,6 +16,7 @@
 VMEM = pl.BlockSpec(memory_space=pltpu.VMEM)
 SMEM = pl.BlockSpec(memory_space=pltpu.SMEM)
 HBM = pl.BlockSpec(memory_space=pltpu.HBM)
+SENT_SCALE = 2.0**-7
 NT = (((1,), (1,)), ((), ()))
 
 
@@ -319,7 +320,7 @@
         return carry
 
     lax.fori_loop(0, branches, branch, 0)
-    sent_ref[...] = sum_ref[...].astype(BF16)
+    sent_ref[...] = sum_ref[...] * SENT_SCALE
     stores[3].start()
     for copy in stores:
         copy.wait()
@@ -331,6 +332,7 @@
 def query_kernel(
     head_size,
     distance,
+    last,
     guidance_ref,
     modulation_ref,
     normed_q_hbm,
@@ -340,6 +342,7 @@
     w_hbm,
     gain_hbm,
     w_out_hbm,
+    start_hbm,
     out_hbm,
     normed_q_ref,
     keys_ref,
@@ -365,9 +368,12 @@
             (gain_hbm, gain_ref),
             (bias_hbm, bias_ref),
             (w_out_hbm, w_out_ref),
+            (start_hbm, sum_ref),
         ),
         in_sems,
     )
+    if not last:
+        loads = loads[:-1]
 
     def load(b):
         return (
@@ -388,7 +394,8 @@
             copy.start()
     scales = branch_scales(guidance_ref)
     tile = min(256, group)
-    sum_ref[...] = jnp.zeros_like(sum_ref)
+    if not last:
+        sum_ref[...] = jnp.zeros_like(sum_ref)
     for copy in loads:
         copy.wait()
     bias = bias_ref[0:1, :]
@@ -413,35 +420,13 @@
         return carry
 
     lax.fori_loop(0, branches, branch, 0)
-    out_ref[...] = sum_ref[...].astype(out_ref.dtype)
+    if last:
+        out_ref[...] = sum_ref[...]
+    else:
+        out_ref[...] = sum_ref[...] * SENT_SCALE
     store = pltpu.make_async_copy(out_ref, out_hbm, out_sem)
     store.start()
     store.wait()
-
-
-def finish_kernel(out_parts, *refs):
-    arrays = (len(refs) - 2) // 2
-    out_ref, held, sems = refs[arrays], refs[arrays + 1 : -1], refs[-1]
-    loads = copies(zip(refs[:arrays], held), sems)
-    for load in loads:
-        load.start()
-    for load in loads:
-        load.wait()
-    step = 32 if out_parts is not None else held[0].shape[0]
-    for r in range(0, held[0].shape[0], step):
-        total = held[0][r : r + step, :]
-        for term in held[1:]:
-            total = total + term[r : r + step, :].astype(F32)
-        if out_parts is None:
-            out_ref[r : r + step, :] = total.astype(BF16)
-        else:
-            senders, heads, share, columns = out_parts
-            for h in range(heads):
-                piece = total[:, h * columns : (h + 1) * columns].astype(BF16)
-                first = r // share
-                out_ref[first : first + step // share, h] = piece.reshape(
-                    step // share, share, columns
-                )
 
 
 def return_kernel(placed_ref, rows_hbm, out_ref, rows_ref, sem):
@@ -506,7 +491,7 @@
         values=((branches, SLOTS, group), BF16),
         residual=((queries, width), F32),
         bias=((8, SLOTS), F32),
-        sent=((queries, width), BF16),
+        sent=((queries, width), F32),
     )
     made = pl.pallas_call(
         functools.partial(first_kernel, senders, head_size),
@@ -536,11 +521,11 @@
     )(guidance, modulation, arrived, table, flat, own_gain, w_out)
     normed_q, keys, values, residual, bias, partial = made
 
-    def attend(distance, dtype):
+    def attend(distance, last):
         return pl.pallas_call(
-            functools.partial(query_kernel, head_size, distance),
-            out_shape=jax.ShapeDtypeStruct((queries, width), dtype),
-            in_specs=[SMEM, VMEM] + [HBM] * 7,
+            functools.partial(query_kernel, head_size, distance, last),
+            out_shape=jax.ShapeDtypeStruct((queries, width), F32),
+            in_specs=[SMEM, VMEM] + [HBM] * 8,
             out_specs=HBM,
             scratch_shapes=[
                 vmem((branches, queries, width), BF16),
@@ -551,9 +536,9 @@
                 vmem((group, 2), F32),
                 vmem((group, width), BF16),
                 vmem((queries, width), F32),
-                vmem((queries, width), dtype),
+                vmem((queries, width), F32),
                 vmem((queries, group), BF16),
-                dma((4,)),
+                dma((5,)),
                 dma((branches,)),
                 dma((branches,)),
                 dma((branches,)),
@@ -561,34 +546,25 @@
             ],
             compiler_params=params(64),
             name="more_queries",
-        )(guidance, modulation, normed_q, keys, values, bias, flat, own_gain, w_out)
+        )(guidance, modulation, normed_q, keys, values, bias, flat, own_gain, w_out, residual)
 
     terms = []
     for distance in range(1, heads):
         turn = [(h, (h + distance) % heads) for h in range(heads)]
-        terms.append(lax.ppermute(partial, "head", turn))
-        last = distance == heads - 1
-        partial = attend(distance, F32 if last else BF16)
-    terms = [residual, partial] + terms
-
-    parts = None
-    shape = jax.ShapeDtypeStruct((queries, width), BF16)
-    if share % 16 == 0:
-        parts = (senders, heads, share, width // heads)
-        shape = jax.ShapeDtypeStruct(parts, BF16)
-    acc = pl.pallas_call(
-        functools.partial(finish_kernel, parts),
-        out_shape=shape,
-        in_specs=[HBM] * len(terms),
-        out_specs=VMEM,
-        scratch_shapes=[vmem((queries, width), term.dtype) for term in terms] + [dma((len(terms),))],
-        compiler_params=params(64),
-        name="finish",
-    )(*terms)
-    if share % 16 != 0:
-        acc = acc.reshape(senders, share, heads, width // heads).transpose(0, 2, 1, 3)
+        terms.append(lax.ppermute(partial.astype(jnp.float16), "head", turn))
+        partial = attend(distance, distance == heads - 1)
+    for term in terms:
+        partial = partial + term.astype(F32) * (1.0 / SENT_SCALE)
+    columns = width // heads
+    rows = jnp.concatenate(
+        [
+            partial[:, h * columns : (h + 1) * columns].reshape(senders, 1, share, columns)
+            for h in range(heads)
+        ],
+        axis=1,
+    ).astype(BF16)
     back = lax.all_to_all(
-        acc.reshape(senders * heads, share, width // heads),
+        rows.reshape(senders * heads, share, width // heads),
         ("cfg", "vox", "head"),
         split_axis=0,
         concat_axis=0,

time: 101 us -> 102 us (level)
  other arithmetic: 1.66 us -> 5.36 us
  Pallas kernels: 42.2 us -> 40.1 us
    pallas_call x2 -> x1, Pallas kernels: 17.3 us -> 15 us  [attend(): pl.pallas_call(functools.partial(query_kernel, head_size, distance, last)...]
    convert_element_type x0 -> x1, other arithmetic: none -> 2.13 us  [on_device(): terms.append(lax.ppermute(partial.astype(jnp.float16), 'head', turn))]
    another operation x1 -> x2, other arithmetic: 0.2 us -> 1.72 us
where the time goes in v6:
time: 102 us; the launch traced here: 101 us
  Pallas kernels  40.1 us (39%)
  waiting for transfers between devices  22 us (22%)
  blocking collectives  19.2 us (19%)
  starting transfers between devices  8.93 us (9%)
  local copies, waits for them, and re-layouts  5.59 us (5%)
  other arithmetic  5.36 us (5%)
    all_to_all x1, waiting for transfers between devices, on_device(): lax.all_to_all(outgoing.reshape(senders, capacity, width + EXTRA), ('cfg'...  22 us
    pallas_call x1, Pallas kernels, on_device(): pl.pallas_call(functools.partial(first_kernel, senders, head_size), out_s...  19.3 us
    all_to_all x1, blocking collectives, on_device(): lax.all_to_all(rows.reshape(senders * heads, share, width // heads), ('cf...  19.2 us
    pallas_call x1, Pallas kernels, attend(): pl.pallas_call(functools.partial(query_kernel, head_size, distance, last)...  15 us
    all_to_all x1, starting transfers between devices, on_device(): lax.all_to_all(outgoing.reshape(senders, capacity, width + EXTRA), ('cfg'...  7.41 us
    unnamed x4, local copies, waits for them, and re-layouts  5.51 us
    pallas_call x1, Pallas kernels, on_device(): pl.pallas_call(functools.partial(place_kernel, senders, capacity), out_sh...  3.04 us
    pallas_call x1, Pallas kernels, on_device(): pl.pallas_call(return_kernel, out_shape=jax.ShapeDtypeStruct((voxels, wid...  2.8 us
  transfers between devices with their start and end apart: 2, of which 1 were waited for; matrix products, arithmetic and copies ran while one was open for 7% of the time, Pallas kernels for 15%

profile of v6, /device:TPU:0, one launch (start us, length us, event | category | flops | bytes accessed | tf_op | source)
XLA Modules:
  0.0 101.4 jit_solution(12399140386155604828)
XLA Ops:
  0.0 3.0 %place.1 = (bf16[512,1152]{1,0:T(8,128)(2,1)}, f32[1,384]{1,0:T(1,128)}) custom-call(s32[384]{0:T(512)} %windows_hbm.1, s32[3,384]{1,0:T(4,128)} %coords_hbm.1, bf16[384,1024]{1,0:T(8,128)(2,1)} %x_hbm.1), custom_call_target="tpu_custom_call" | custom-call | tf_op jit(solution)/shard_map/place/pallas_call | solution.py:458
  3.0 0.0 copy-start
  3.1 7.4 %all-to-all-start = ((bf16[16,32,1152]{2,1,0:T(8,128)(2,1)}), bf16[16,32,1152]{2,1,0:T(8,128)(2,1)}, u32[]{:S(2)}, u32[]{:S(2)}) async-start(bf16[16,32,1152]{2,1,0:T(8,128)(2,1)} %bitcast.14), calls=%async_computation | async-start | bytes 2359296 | tf_op jit(solution)/shard_map/all_to_all | solution.py:475
  10.5 0.0 copy-done
  10.5 0.9 copy.9
  11.3 4.6 %copy.10 = bf16[1024,3,512]{0,2,1:T(8,128)(2,1)} copy(bf16[1024,3,512]{2,0,1:T(8,128)(2,1)} %param.12) | data formatting | bytes 6291456 | tf_op args[4]
  16.0 0.3 fusion.3
  16.3 0.1 pad_maximum_fusion.2
  16.4 0.2 reduce-precision_convert_fusion.1
  16.6 1.1 %pad_maximum_fusion.table_hbm = bf16[576,1024]{1,0:T(8,128)(2,1)} fusion(bf16[192,1024]{1,0:T(8,128)(2,1)S(1)} %get-tuple-element.33, bf16[192,1024]{1,0:T(8,128)(2,1)S(1)} %get-tuple-element.32, bf16[192,1024]{1,0:T(8,128)(2,1)S(1)} %get-tuple-element.31), kind=kLoop, calls=%fused_computation.2 | loop fusion | flops 3538944 | bytes 2359296 | tf_op jit(solution)/shard_map/concatenate | solution.py:49
  17.7 22.0 %all-to-all-done = bf16[16,32,1152]{2,1,0:T(8,128)(2,1)} async-done(((bf16[16,32,1152]{2,1,0:T(8,128)(2,1)}), bf16[16,32,1152]{2,1,0:T(8,128)(2,1)}, u32[]{:S(2)}, u32[]{:S(2)}) %all-to-all-start) | async-done | bytes 1179680 | tf_op jit(solution)/shard_map/all_to_all | solution.py:475
  39.7 19.3 %first_queries.1 = (bf16[2,3,256,1024]{3,2,1,0:T(8,128)(2,1)}, bf16[3,512,512]{2,1,0:T(8,128)(2,1)}, bf16[3,512,512]{2,1,0:T(8,128)(2,1)}, f32[256,1024]{1,0:T(8...) custom-call(f32[2]{0:T(128)} %guidance_ref.3, f32[3,3,1024]{2,1,0:T(4,128)} %modulation_ref.3, ...), custom_call_target="tpu_custom_call" | custom-call | tf_op jit(solution)/shard_map/first_queries/pallas_call | solution.py:496
  59.0 2.1 %convert_element_type.18 = f16[256,1024]{1,0:T(8,128)(2,1)} convert(f32[256,1024]{1,0:T(8,128)} %get-tuple-element.28) | non-fusion elementwise | flops 262144 | bytes 1572864 | tf_op jit(solution)/shard_map/convert_element_type | solution.py:554
  61.1 1.5 %collective-permute-start = (f16[256,1024]{1,0:T(8,128)(2,1)}, f16[256,1024]{1,0:T(8,128)(2,1)}, u32[]{:S(2)}, u32[]{:S(2)}) collective-permute-start(f16[256,1024]{1,0:T(8,128)(2,1)} %convert_element_type.18), channel_id=1, source_target_pairs={{0,1},{1,0},{2,3},{3,2},{4,5},{5,4},{6,7},{7,6},{8,9},{9,8},{10,11... | collective-permute-start | bytes 1572872 | tf_op jit(solution)/shard_map/ppermute | solution.py:554
  62.6 15.0 %more_queries.1 = f32[256,1024]{1,0:T(8,128)} custom-call(f32[2]{0:T(128)} %guidance_ref.3, f32[3,3,1024]{2,1,0:T(4,128)} %modulation_ref.3, bf16[2,3,256,1024]{3,2,1,0:T(8,128)(2,1)} %get-tuple-element.23.normed_q_hbm, bf16[3,512,512]{2,1,0:T(8,128)(2,1)} %get-tuple-element.24.keys_hbm, bf16[3,512,512]{2,1,0:T(8,128)(2,1)} %get-tuple-element.25.values_hbm, ...), custom_call_target="tpu_custom_call" | custom-call | tf_op jit(solution)/shard_map/more_queries/pallas_call | solution.py:525
  77.7 0.0 collective-permute-done
  77.7 1.5 %add_convert_fusion = bf16[256,1024]{1,0:T(8,128)(2,1)S(1)} fusion(f32[256,1024]{1,0:T(8,128)} %more_queries.1, f16[256,1024]{1,0:T(8,128)(2,1)} %collective-permute-done), kind=kLoop, calls=%fused_computation.7 | loop fusion | flops 1048576 | bytes 2097152 | tf_op jit(solution)/shard_map/convert.5
  79.2 0.1 pad_maximum_fusion.1
  79.3 19.2 %all_to_all.10 = bf16[32,16,512]{2,1,0:T(8,128)(2,1)} all-to-all(bf16[32,16,512]{2,1,0:T(8,128)(2,1)S(1)} %bitcast.13), channel_id=1, replica_groups=mesh['cfg'=2,'vox'=8,'head'=2] {'cfg','vox','head'}, dimensions={0} | all-to-all | bytes 1048576 | tf_op jit(solution)/shard_map/all_to_all | solution.py:566
  98.6 2.8 %return_rows.1 = bf16[384,512]{1,0:T(8,128)(2,1)} custom-call(f32[1,384]{1,0:T(1,128)} %get-tuple-element.17.placed_ref, bf16[512,512]{1,0:T(8,128)(2,1)} %bitcast.12), custom_call_target="tpu_custom_call" | custom-call | tf_op jit(solution)/shard_map/return_rows/pallas_call | solution.py:573
  (3 shorter events, 0.1 us)
Async XLA Ops:
  3.0 7.4 %copy-start = (f32[2,512]{1,0:T(2,128)S(1)}, f32[2,512]{1,0:T(2,128)}, u32[]{:S(2)}) copy-start(f32[2,512]{1,0:T(2,128)} %param.14) | copy-start | bytes 12292
  3.1 36.6 %all-to-all-start = ((bf16[16,32,1152]{2,1,0:T(8,128)(2,1)}), bf16[16,32,1152]{2,1,0:T(8,128)(2,1)}, u32[]{:S(2)}, u32[]{:S(2)}) async-start(bf16[16,32,1152]{2,1,0:T(8,128)(2,1)} %bitcast.14), calls=%async_computation | async-start | bytes 2359296 | tf_op jit(solution)/shard_map/all_to_all | solution.py:475
  61.1 16.5 %collective-permute-start = (f16[256,1024]{1,0:T(8,128)(2,1)}, f16[256,1024]{1,0:T(8,128)(2,1)}, u32[]{:S(2)}, u32[]{:S(2)}) collective-permute-start(f16[256,1024]{1,0:T(8,128)(2,1)} %convert_element_type.18), channel_id=1, source_target_pairs={{0,1},{1,0},{2,3},{3,2},{4,5},{5,4},{6,7},{7,6},{8,9},{9,8},{10,11... | collective-permute-start | bytes 1572872 | tf_op jit(solution)/shard_map/ppermute | solution.py:554

commit v7 on v6

--- a/solution.py
+++ b/solution.py
@@ -111,22 +111,22 @@
     return lax.dot_general(normed, w_value, NT, preferred_element_type=F32).astype(BF16)
 
 
-def attend_tile(normed_q, w_query, gain, key, value, bias, head_size):
-    queries, tile = normed_q.shape[0], w_query.shape[0]
-    query = lax.dot_general(w_query, normed_q, NT, preferred_element_type=F32)
-    query = column_norm(query, gain, head_size)
-    query = (query.astype(F32) * (1.0 / head_size**0.5)).T
+def attend_heads(query, key, value, before_head, att_ref, bias, tile, head_size):
+    queries, group = att_ref.shape
     lane_head = iota((queries, tile), 1) // head_size
-    count = tile // head_size
-
-    def score(head):
-        return dot(jnp.where(lane_head == head, query, 0.0).astype(BF16), key)
+    per_tile = tile // head_size
+    heads = group // head_size
+
+    def score(i):
+        one = jnp.where(lane_head == i % per_tile, query(i // per_tile), 0.0).astype(BF16)
+        return dot(one, key(i // per_tile))
 
     scores = score(0)
     mixed = jnp.zeros((queries, tile), F32)
     step = min(32, queries)
-    for head in range(count):
-        following = score(head + 1) if head + 1 < count else None
+    for i in range(heads):
+        before_head(i)
+        following = score(i + 1) if i + 1 < heads else None
         pieces = []
         for r in range(0, queries, step):
             piece = scores[r : r + step] + bias
@@ -134,9 +134,17 @@
             total = jnp.sum(weights, axis=1, keepdims=True)
             pieces.append((weights * (1.0 / total)).astype(BF16))
         attend = jnp.concatenate(pieces, axis=0)
-        mixed = jnp.where(lane_head == head, dot(attend, value), mixed)
+        mixed = jnp.where(lane_head == i % per_tile, dot(attend, value(i // per_tile)), mixed)
+        if (i + 1) % per_tile == 0:
+            start = i // per_tile * tile
+            att_ref[:, start : start + tile] = mixed.astype(BF16)
         scores = following
-    return mixed.astype(BF16)
+
+
+def project_query(normed_q, w_query, gain, head_size):
+    query = lax.dot_general(w_query, normed_q, NT, preferred_element_type=F32)
+    query = column_norm(query, gain, head_size)
+    return (query.astype(F32) * (1.0 / head_size**0.5)).T
 
 
 def branch_scales(guidance_ref):
@@ -203,7 +211,7 @@
     )
     stores = copies(
         (
-            (normed_q_ref, normed_q_hbm),
+            (normed_q_ref.at[pl.ds(1, normed_q_hbm.shape[0])], normed_q_hbm),
             (bias_ref, bias_hbm),
             (residual_ref, residual_hbm),
             (sent_ref, sent_hbm),
@@ -238,23 +246,18 @@
     chosen = (wanted == (lane % GRID).astype(F32)).astype(F32).astype(BF16)
     chosen = jnp.concatenate([chosen, chosen, chosen], axis=1)
     loads[1].wait()
-    hidden_ref[...] = dot(chosen, table_ref[...]) + rows_ref[:, :width].astype(F32)
-
-    chunk = 32
-
-    def normalise(i, carry):
-        rows = pl.ds(pl.multiple_of(i * chunk, chunk), chunk)
-        hidden = hidden_ref[rows, :]
+    chunk = min(128, slots)
+    shifts = [modulation_ref[b, 0:1, :] for b in range(branches)]
+    stretches = [1.0 + modulation_ref[b, 1:2, :] for b in range(branches)]
+    for start in range(0, slots, chunk):
+        rows = slice(start, start + chunk)
+        hidden = dot(chosen[rows], table_ref[...]) + rows_ref[rows, :width].astype(F32)
+        hidden_ref[rows, :] = hidden
         centred = hidden - jnp.mean(hidden, axis=1, keepdims=True)
         spread = jnp.mean(centred * centred, axis=1, keepdims=True)
         normal = centred * lax.rsqrt(spread + 1e-06)
         for b in range(branches):
-            normed_ref[b, rows, :] = (
-                normal * (1.0 + modulation_ref[b, 1:2, :]) + modulation_ref[b, 0:1, :]
-            ).astype(BF16)
-        return carry
-
-    lax.fori_loop(0, slots // chunk, normalise, 0, unroll=2)
+            normed_ref[b, rows, :] = (normal * stretches[b] + shifts[b]).astype(BF16)
 
     for d in range(heads):
         first = lax.rem(me + d + 1, heads) * share
@@ -285,9 +288,8 @@
 
     bias = bias_ref[0:1, :]
     tile = min(256, group)
-    for load in loads[2:]:
+    for load in loads[2:4]:
         load.wait()
-    sum_ref[...] = jnp.zeros_like(sum_ref)
 
     def store(b):
         return (
@@ -295,31 +297,57 @@
             pltpu.make_async_copy(values_ref.at[b], values_hbm.at[b], value_sems.at[b]),
         )
 
-    def branch(b, carry):
-        for start in range(0, group, tile):
-            features = slice(start, start + tile)
-            gains = gain_ref[features, :]
-            key = project_keys(normed_ref[b], w_ref[1, features, :], gains[:, 1:2], head_size)
-            value = project_values(normed_ref[b], w_ref[2, features, :])
-            keys_ref[b, features, :] = key
-            values_ref[b, :, features] = value
-            att_ref[:, features] = attend_tile(
-                normed_q_ref[0, b],
-                w_ref[0, features, :],
-                gains[:, 0:1],
-                key,
-                value,
-                bias,
-                head_size,
-            )
+    for b in range(branches):
+        made = {}
+
+        def make(kind, t):
+            features = slice(t * tile, (t + 1) * tile)
+            if kind == "query":
+                array = project_query(
+                    normed_q_ref[0, b], w_ref[0, features, :], gain_ref[features, 0:1], head_size
+                )
+            elif kind == "key":
+                array = project_keys(
+                    normed_ref[b], w_ref[1, features, :], gain_ref[features, 1:2], head_size
+                )
+                keys_ref[b, features, :] = array
+            else:
+                array = project_values(normed_ref[b], w_ref[2, features, :])
+                values_ref[b, :, features] = array
+            made[kind, t] = array
+
+        def get(kind, t):
+            if (kind, t) not in made:
+                make(kind, t)
+            return made[kind, t]
+
+        for kind in ("query", "key", "value"):
+            make(kind, 0)
+        waiting = [(kind, t) for t in range(1, group // tile) for kind in ("query", "key", "value")]
+
+        def before_head(i):
+            if i < len(waiting):
+                get(*waiting[i])
+
+        attend_heads(
+            functools.partial(get, "query"),
+            functools.partial(get, "key"),
+            functools.partial(get, "value"),
+            before_head,
+            att_ref,
+            bias,
+            tile,
+            head_size,
+        )
         for copy in store(b):
             copy.start()
-        sum_ref[...] += dot(att_ref[...], w_out_ref[...]) * (
-            pick_scale(b, scales) * modulation_ref[b, 2:3, :]
-        )
-        return carry
-
-    lax.fori_loop(0, branches, branch, 0)
+        if b == 0:
+            loads[4].wait()
+        term = dot(att_ref[...], w_out_ref[...]) * (scales[b] * modulation_ref[b, 2:3, :])
+        if b == 0:
+            sum_ref[...] = term
+        else:
+            sum_ref[...] += term
     sent_ref[...] = sum_ref[...] * SENT_SCALE
     stores[3].start()
     for copy in stores:
@@ -352,7 +380,6 @@
     gain_ref,
     w_out_ref,
     sum_ref,
-    out_ref,
     att_ref,
     in_sems,
     query_sems,
@@ -378,17 +405,16 @@
     def load(b):
         return (
             pltpu.make_async_copy(
-                normed_q_hbm.at[distance, b], normed_q_ref.at[b], query_sems.at[b]
+                normed_q_hbm.at[distance - 1, b], normed_q_ref.at[b], query_sems.at[b]
             ),
             pltpu.make_async_copy(keys_hbm.at[b], keys_ref.at[b], key_sems.at[b]),
             pltpu.make_async_copy(values_hbm.at[b], values_ref.at[b], value_sems.at[b]),
         )
 
-    loads[0].start()
-    for copy in load(0):
+    for copy in load(0)[:1] + (loads[0], loads[1]) + load(0)[1:] + (loads[2], loads[3]):
         copy.start()
-    for copy in loads[1:]:
-        copy.start()
+    if last:
+        loads[4].start()
     for b in range(1, branches):
         for copy in load(b):
             copy.start()
@@ -396,42 +422,47 @@
     tile = min(256, group)
     if not last:
         sum_ref[...] = jnp.zeros_like(sum_ref)
-    for copy in loads:
+    for copy in loads[:3]:
         copy.wait()
     bias = bias_ref[0:1, :]
 
-    def branch(b, carry):
+    for b in range(branches):
         for copy in load(b):
             copy.wait()
-        for start in range(0, group, tile):
-            features = slice(start, start + tile)
-            att_ref[:, features] = attend_tile(
-                normed_q_ref[b],
-                w_ref[features, :],
-                gain_ref[features, 0:1],
-                keys_ref[b, features, :],
-                values_ref[b, :, features],
-                bias,
-                head_size,
-            )
+        made = {}
+
+        def query(t):
+            if t not in made:
+                features = slice(t * tile, (t + 1) * tile)
+                made[t] = project_query(
+                    normed_q_ref[b], w_ref[features, :], gain_ref[features, 0:1], head_size
+                )
+            return made[t]
+
+        attend_heads(
+            query,
+            lambda t: keys_ref[b, t * tile : (t + 1) * tile, :],
+            lambda t: values_ref[b, :, t * tile : (t + 1) * tile],
+            lambda i: query(min(i, group // tile - 1)),
+            att_ref,
+            bias,
+            tile,
+            head_size,
+        )
+        if b == 0:
+            for copy in loads[3:]:
+                copy.wait()
         sum_ref[...] += dot(att_ref[...], w_out_ref[...]) * (
-            pick_scale(b, scales) * modulation_ref[b, 2:3, :]
+            scales[b] * modulation_ref[b, 2:3, :]
         )
-        return carry
-
-    lax.fori_loop(0, branches, branch, 0)
-    if last:
-        out_ref[...] = sum_ref[...]
-    else:
-        out_ref[...] = sum_ref[...] * SENT_SCALE
-    store = pltpu.make_async_copy(out_ref, out_hbm, out_sem)
+    if not last:
+        sum_ref[...] = sum_ref[...] * SENT_SCALE
+    store = pltpu.make_async_copy(sum_ref, out_hbm, out_sem)
     store.start()
     store.wait()
 
 
-def return_kernel(placed_ref, rows_hbm, out_ref, rows_ref, sem):
-    load = pltpu.make_async_copy(rows_hbm, rows_ref, sem)
-    load.start()
+def return_kernel(placed_ref, rows_ref, out_ref):
     voxels = placed_ref.shape[1]
     column = jnp.broadcast_to(placed_ref[...], (128, voxels)).T
     column = column.astype(jnp.int32)
@@ -439,7 +470,6 @@
     placing = jnp.concatenate(
         [(column == lane + start).astype(F32).astype(BF16) for start in range(0, SLOTS, 128)], axis=1
     )
-    load.wait()
     out_ref[...] = dot(placing, rows_ref[...]).astype(BF16)
 
 
@@ -486,7 +516,7 @@
     arrived, own_gain, table, flat = lax.optimization_barrier((arrived, own_gain, table, flat))
 
     shapes = dict(
-        normed_q=((heads, branches, queries, width), BF16),
+        normed_q=((heads - 1, branches, queries, width), BF16),
         keys=((branches, group, SLOTS), BF16),
         values=((branches, SLOTS, group), BF16),
         residual=((queries, width), F32),
@@ -506,7 +536,8 @@
             vmem((group, width), BF16),
             vmem((branches, SLOTS, width), BF16),
         ]
-        + [vmem(*shape) for shape in shapes.values()]
+        + [vmem((heads, branches, queries, width), BF16)]
+        + [vmem(*shape) for name, shape in shapes.items() if name != "normed_q"]
         + [
             vmem((SLOTS, width), F32),
             vmem((queries, group), BF16),
@@ -535,7 +566,6 @@
                 vmem((group, width), BF16),
                 vmem((group, 2), F32),
                 vmem((group, width), BF16),
-                vmem((queries, width), F32),
                 vmem((queries, width), F32),
                 vmem((queries, group), BF16),
                 dma((5,)),
@@ -573,10 +603,9 @@
     return pl.pallas_call(
         return_kernel,
         out_shape=jax.ShapeDtypeStruct((voxels, width // heads), BF16),
-        in_specs=[VMEM, HBM],
+        in_specs=[VMEM, VMEM],
         out_specs=VMEM,
-        scratch_shapes=[vmem((SLOTS, width // heads), BF16), dma(())],
-        compiler_params=params(64),
+        compiler_params=params(16),
         name="return_rows",
     )(placed, back.reshape(SLOTS, width // heads))
 

time: 102 us -> 95.6 us (0.937)
  Pallas kernels: 40.1 us -> 33.4 us
    pallas_call x1, Pallas kernels: 19.3 us -> 16.3 us  [on_device(): pl.pallas_call(functools.partial(first_kernel, senders, head_size), out_s...]
    pallas_call x1, Pallas kernels: 15 us -> 12.8 us  [attend(): pl.pallas_call(functools.partial(query_kernel, head_size, distance, last)...]
    pallas_call x1, Pallas kernels: 2.8 us -> 1.17 us  [on_device(): pl.pallas_call(return_kernel, out_shape=jax.ShapeDtypeStruct((voxels, wid...]
    unnamed x4 -> x6, local copies, waits for them, and re-layouts: 5.51 us -> 5.51 us
  transfers between devices with their start and end apart: 2 -> 2, of which waited for: 1 -> 1; matrix products, arithmetic and copies ran while one was open for 7% -> 7% of each run, Pallas kernels for 15% -> 13%
where the time goes in v7:
time: 95.6 us; the launch traced here: 95.1 us
  Pallas kernels  33.4 us (35%)
  waiting for transfers between devices  22 us (23%)
  blocking collectives  19.7 us (21%)
  starting transfers between devices  8.94 us (9%)
  local copies, waits for them, and re-layouts  5.58 us (6%)
  other arithmetic  5.34 us (6%)
    all_to_all x1, waiting for transfers between devices, on_device(): lax.all_to_all(outgoing.reshape(senders, capacity, width + EXTRA), ('cfg'...  22 us
    all_to_all x1, blocking collectives, on_device(): lax.all_to_all(rows.reshape(senders * heads, share, width // heads), ('cf...  19.7 us
    pallas_call x1, Pallas kernels, on_device(): pl.pallas_call(functools.partial(first_kernel, senders, head_size), out_s...  16.3 us
    pallas_call x1, Pallas kernels, attend(): pl.pallas_call(functools.partial(query_kernel, head_size, distance, last)...  12.8 us
    all_to_all x1, starting transfers between devices, on_device(): lax.all_to_all(outgoing.reshape(senders, capacity, width + EXTRA), ('cfg'...  7.41 us
    unnamed x6, local copies, waits for them, and re-layouts  5.51 us
    pallas_call x1, Pallas kernels, on_device(): pl.pallas_call(functools.partial(place_kernel, senders, capacity), out_sh...  3.04 us
    convert_element_type x1, other arithmetic, on_device(): terms.append(lax.ppermute(partial.astype(jnp.float16), 'head', turn))  2.14 us
  transfers between devices with their start and end apart: 2, of which 1 were waited for; matrix products, arithmetic and copies ran while one was open for 7% of the time, Pallas kernels for 13%

profile of v7, /device:TPU:0, one launch (start us, length us, event | category | flops | bytes accessed | tf_op | source)
XLA Modules:
  0.0 95.1 jit_solution(2941724377298949598)
XLA Ops:
  0.0 3.0 %place.1 = (bf16[512,1152]{1,0:T(8,128)(2,1)}, f32[1,384]{1,0:T(1,128)}) custom-call(s32[384]{0:T(512)} %windows_hbm.1, s32[3,384]{1,0:T(4,128)} %coords_hbm.1, bf16[384,1024]{1,0:T(8,128)(2,1)} %x_hbm.1), custom_call_target="tpu_custom_call" | custom-call | tf_op jit(solution)/shard_map/place/pallas_call | solution.py:488
  3.0 0.0 copy-start.1
  3.1 7.4 %all-to-all-start = ((bf16[16,32,1152]{2,1,0:T(8,128)(2,1)}), bf16[16,32,1152]{2,1,0:T(8,128)(2,1)}, u32[]{:S(2)}, u32[]{:S(2)}) async-start(bf16[16,32,1152]{2,1,0:T(8,128)(2,1)} %bitcast.14), calls=%async_computation | async-start | bytes 2359296 | tf_op jit(solution)/shard_map/all_to_all | solution.py:505
  10.5 0.0 copy-done.1
  10.5 0.9 copy.9
  11.3 4.6 %copy.10 = bf16[1024,3,512]{0,2,1:T(8,128)(2,1)} copy(bf16[1024,3,512]{2,0,1:T(8,128)(2,1)} %param.12) | data formatting | bytes 6291456 | tf_op args[4]
  16.0 0.3 fusion.3
  16.3 0.1 pad_maximum_fusion.2
  16.3 0.2 reduce-precision_convert_fusion.1
  16.6 1.1 %pad_maximum_fusion.table_hbm = bf16[576,1024]{1,0:T(8,128)(2,1)} fusion(bf16[192,1024]{1,0:T(8,128)(2,1)S(1)} %get-tuple-element.33, bf16[192,1024]{1,0:T(8,128)(2,1)S(1)} %get-tuple-element.32, bf16[192,1024]{1,0:T(8,128)(2,1)S(1)} %get-tuple-element.31), kind=kLoop, calls=%fused_computation.2 | loop fusion | flops 3538944 | bytes 2359296 | tf_op jit(solution)/shard_map/concatenate | solution.py:49
  17.6 22.0 %all-to-all-done = bf16[16,32,1152]{2,1,0:T(8,128)(2,1)} async-done(((bf16[16,32,1152]{2,1,0:T(8,128)(2,1)}), bf16[16,32,1152]{2,1,0:T(8,128)(2,1)}, u32[]{:S(2)}, u32[]{:S(2)}) %all-to-all-start) | async-done | bytes 1179680 | tf_op jit(solution)/shard_map/all_to_all | solution.py:505
  39.7 16.3 %first_queries.1 = (bf16[1,3,256,1024]{3,2,1,0:T(8,128)(2,1)}, bf16[3,512,512]{2,1,0:T(8,128)(2,1)}, bf16[3,512,512]{2,1,0:T(8,128)(2,1)}, f32[256,1024]{1,0:T(8...) custom-call(f32[2]{0:T(128)} %guidance_ref.3, f32[3,3,1024]{2,1,0:T(4,128)} %modulation_ref.3, ...), custom_call_target="tpu_custom_call" | custom-call | tf_op jit(solution)/shard_map/first_queries/pallas_call | solution.py:526
  56.0 2.1 %convert_element_type.18 = f16[256,1024]{1,0:T(8,128)(2,1)} convert(f32[256,1024]{1,0:T(8,128)} %get-tuple-element.28) | non-fusion elementwise | flops 262144 | bytes 1572864 | tf_op jit(solution)/shard_map/convert_element_type | solution.py:584
  58.2 1.5 %collective-permute-start = (f16[256,1024]{1,0:T(8,128)(2,1)}, f16[256,1024]{1,0:T(8,128)(2,1)}, u32[]{:S(2)}, u32[]{:S(2)}) collective-permute-start(f16[256,1024]{1,0:T(8,128)(2,1)} %convert_element_type.18), channel_id=1, source_target_pairs={{0,1},{1,0},{2,3},{3,2},{4,5},{5,4},{6,7},{7,6},{8,9},{9,8},{10,11... | collective-permute-start | bytes 1572872 | tf_op jit(solution)/shard_map/ppermute | solution.py:584
  59.7 12.8 %more_queries.1 = f32[256,1024]{1,0:T(8,128)} custom-call(f32[2]{0:T(128)} %guidance_ref.3, f32[3,3,1024]{2,1,0:T(4,128)} %modulation_ref.3, bf16[1,3,256,1024]{3,2,1,0:T(8,128)(2,1)} %get-tuple-element.23.normed_q_hbm, bf16[3,512,512]{2,1,0:T(8,128)(2,1)} %get-tuple-element.24.keys_hbm, bf16[3,512,512]{2,1,0:T(8,128)(2,1)} %get-tuple-element.25.values_hbm, ...), custom_call_target="tpu_custom_call" | custom-call | tf_op jit(solution)/shard_map/more_queries/pallas_call | solution.py:556
  72.5 0.0 collective-permute-done
  72.5 1.5 %add_convert_fusion = bf16[256,1024]{1,0:T(8,128)(2,1)S(1)} fusion(f32[256,1024]{1,0:T(8,128)} %more_queries.1, f16[256,1024]{1,0:T(8,128)(2,1)} %collective-permute-done), kind=kLoop, calls=%fused_computation.7 | loop fusion | flops 1048576 | bytes 2097152 | tf_op jit(solution)/shard_map/convert.5
  74.1 0.0 copy-start
  74.1 0.1 pad_maximum_fusion.1
  74.2 19.7 %all_to_all.10 = bf16[32,16,512]{2,1,0:T(8,128)(2,1)S(1)} all-to-all(bf16[32,16,512]{2,1,0:T(8,128)(2,1)S(1)} %bitcast.13), channel_id=1, replica_groups=mesh['cfg'=2,'vox'=8,'head'=2] {'cfg','vox','head'}, dimensions={0} | all-to-all | bytes 1048576 | tf_op jit(solution)/shard_map/all_to_all | solution.py:596
  93.9 0.0 copy-done
  93.9 1.2 %return_rows.1 = bf16[384,512]{1,0:T(8,128)(2,1)} custom-call(f32[1,384]{1,0:T(1,128)S(1)} %copy-done, bf16[512,512]{1,0:T(8,128)(2,1)S(1)} %bitcast.8), custom_call_target="tpu_custom_call" | custom-call | tf_op jit(solution)/shard_map/return_rows/pallas_call | solution.py:603
  (3 shorter events, 0.1 us)
Async XLA Ops:
  3.0 7.4 %copy-start.1 = (f32[2,512]{1,0:T(2,128)S(1)}, f32[2,512]{1,0:T(2,128)}, u32[]{:S(2)}) copy-start(f32[2,512]{1,0:T(2,128)} %param.14) | copy-start | bytes 12292
  3.1 36.6 %all-to-all-start = ((bf16[16,32,1152]{2,1,0:T(8,128)(2,1)}), bf16[16,32,1152]{2,1,0:T(8,128)(2,1)}, u32[]{:S(2)}, u32[]{:S(2)}) async-start(bf16[16,32,1152]{2,1,0:T(8,128)(2,1)} %bitcast.14), calls=%async_computation | async-start | bytes 2359296 | tf_op jit(solution)/shard_map/all_to_all | solution.py:505
  58.2 14.4 %collective-permute-start = (f16[256,1024]{1,0:T(8,128)(2,1)}, f16[256,1024]{1,0:T(8,128)(2,1)}, u32[]{:S(2)}, u32[]{:S(2)}) collective-permute-start(f16[256,1024]{1,0:T(8,128)(2,1)} %convert_element_type.18), channel_id=1, source_target_pairs={{0,1},{1,0},{2,3},{3,2},{4,5},{5,4},{6,7},{7,6},{8,9},{9,8},{10,11... | collective-permute-start | bytes 1572872 | tf_op jit(solution)/shard_map/ppermute | solution.py:584
  74.1 19.8 %copy-start = (f32[1,384]{1,0:T(1,128)S(1)}, f32[1,384]{1,0:T(1,128)}, u32[]{:S(2)}) copy-start(f32[1,384]{1,0:T(1,128)} %get-tuple-element.17.placed_ref) | copy-start | bytes 4612

commit v8 on v7

--- a/solution.py
+++ b/solution.py
@@ -163,23 +163,27 @@
     ]
 
 
+def gain_columns(gain_rows_ref):
+    rows = gain_rows_ref[...]
+    return jnp.concatenate([rows, rows, rows, rows], axis=0).T
+
+
 def first_kernel(
     senders,
     head_size,
     guidance_ref,
     modulation_ref,
-    rows_hbm,
+    gain_rows_ref,
+    rows_ref,
     table_hbm,
     w_hbm,
-    gain_hbm,
     w_out_hbm,
     normed_q_hbm,
     keys_hbm,
     values_hbm,
     residual_hbm,
     bias_hbm,
-    sent_hbm,
-    rows_ref,
+    sent_ref,
     table_ref,
     w_ref,
     gain_ref,
@@ -190,7 +194,6 @@
     values_ref,
     residual_ref,
     bias_ref,
-    sent_ref,
     hidden_ref,
     att_ref,
     sum_ref,
@@ -201,10 +204,8 @@
 ):
     loads = copies(
         (
-            (rows_hbm, rows_ref),
             (table_hbm, table_ref),
             (w_hbm, w_ref),
-            (gain_hbm, gain_ref),
             (w_out_hbm, w_out_ref),
         ),
         in_sems,
@@ -214,7 +215,6 @@
             (normed_q_ref.at[pl.ds(1, normed_q_hbm.shape[0])], normed_q_hbm),
             (bias_ref, bias_hbm),
             (residual_ref, residual_hbm),
-            (sent_ref, sent_hbm),
         ),
         out_sems,
     )
@@ -229,7 +229,7 @@
     scales = branch_scales(guidance_ref)
     total = (scales[0] + scales[1]) + scales[2]
 
-    loads[0].wait()
+    gain_ref[...] = gain_columns(gain_rows_ref)
     extra = rows_ref[:, width:]
     pick = ((iota((8, EXTRA), 1) == 3)).astype(F32).astype(BF16)
     live = lax.dot_general(pick, extra, NT, preferred_element_type=F32)
@@ -245,7 +245,7 @@
     )
     chosen = (wanted == (lane % GRID).astype(F32)).astype(F32).astype(BF16)
     chosen = jnp.concatenate([chosen, chosen, chosen], axis=1)
-    loads[1].wait()
+    loads[0].wait()
     chunk = min(128, slots)
     shifts = [modulation_ref[b, 0:1, :] for b in range(branches)]
     stretches = [1.0 + modulation_ref[b, 1:2, :] for b in range(branches)]
@@ -288,8 +288,7 @@
 
     bias = bias_ref[0:1, :]
     tile = min(256, group)
-    for load in loads[2:4]:
-        load.wait()
+    loads[1].wait()
 
     def store(b):
         return (
@@ -342,14 +341,13 @@
         for copy in store(b):
             copy.start()
         if b == 0:
-            loads[4].wait()
+            loads[2].wait()
         term = dot(att_ref[...], w_out_ref[...]) * (scales[b] * modulation_ref[b, 2:3, :])
         if b == 0:
             sum_ref[...] = term
         else:
             sum_ref[...] += term
     sent_ref[...] = sum_ref[...] * SENT_SCALE
-    stores[3].start()
     for copy in stores:
         copy.wait()
     for b in range(branches):
@@ -363,12 +361,12 @@
     last,
     guidance_ref,
     modulation_ref,
+    gain_rows_ref,
     normed_q_hbm,
     keys_hbm,
     values_hbm,
     bias_hbm,
     w_hbm,
-    gain_hbm,
     w_out_hbm,
     start_hbm,
     out_hbm,
@@ -392,7 +390,6 @@
     loads = copies(
         (
             (w_hbm.at[0], w_ref),
-            (gain_hbm, gain_ref),
             (bias_hbm, bias_ref),
             (w_out_hbm, w_out_ref),
             (start_hbm, sum_ref),
@@ -411,10 +408,8 @@
             pltpu.make_async_copy(values_hbm.at[b], values_ref.at[b], value_sems.at[b]),
         )
 
-    for copy in load(0)[:1] + (loads[0], loads[1]) + load(0)[1:] + (loads[2], loads[3]):
+    for copy in load(0)[:1] + (loads[0], loads[1]) + load(0)[1:] + tuple(loads[2:]):
         copy.start()
-    if last:
-        loads[4].start()
     for b in range(1, branches):
         for copy in load(b):
             copy.start()
@@ -422,7 +417,8 @@
     tile = min(256, group)
     if not last:
         sum_ref[...] = jnp.zeros_like(sum_ref)
-    for copy in loads[:3]:
+    gain_ref[...] = gain_columns(gain_rows_ref)
+    for copy in loads[:2]:
         copy.wait()
     bias = bias_ref[0:1, :]
 
@@ -450,7 +446,7 @@
             head_size,
         )
         if b == 0:
-            for copy in loads[3:]:
+            for copy in loads[2:]:
                 copy.wait()
         sum_ref[...] += dot(att_ref[...], w_out_ref[...]) * (
             scales[b] * modulation_ref[b, 2:3, :]
@@ -510,11 +506,8 @@
         tiled=True,
     ).reshape(SLOTS, width + EXTRA)
 
-    own_gain = qk_gain.T
     table = position_parts(width)
     flat = jnp.transpose(w_qkv, (1, 2, 0))
-    arrived, own_gain, table, flat = lax.optimization_barrier((arrived, own_gain, table, flat))
-
     shapes = dict(
         normed_q=((heads - 1, branches, queries, width), BF16),
         keys=((branches, group, SLOTS), BF16),
@@ -526,37 +519,36 @@
     made = pl.pallas_call(
         functools.partial(first_kernel, senders, head_size),
         out_shape=tuple(jax.ShapeDtypeStruct(*shape) for shape in shapes.values()),
-        in_specs=[SMEM, VMEM] + [HBM] * 5,
-        out_specs=(HBM,) * 6,
+        in_specs=[SMEM, VMEM, VMEM, VMEM] + [HBM] * 3,
+        out_specs=(HBM,) * 5 + (VMEM,),
         scratch_shapes=[
-            vmem((SLOTS, width + EXTRA), BF16),
             vmem(table.shape, BF16),
             vmem((3, group, width), BF16),
-            vmem((group, 2), F32),
+            vmem((group, 8), F32),
             vmem((group, width), BF16),
             vmem((branches, SLOTS, width), BF16),
         ]
         + [vmem((heads, branches, queries, width), BF16)]
-        + [vmem(*shape) for name, shape in shapes.items() if name != "normed_q"]
+        + [vmem(*shape) for name, shape in shapes.items() if name not in ("normed_q", "sent")]
         + [
             vmem((SLOTS, width), F32),
             vmem((queries, group), BF16),
             vmem((queries, width), F32),
-            dma((5,)),
-            dma((4,)),
+            dma((3,)),
+            dma((3,)),
             dma((branches,)),
             dma((branches,)),
         ],
-        compiler_params=params(64),
+        compiler_params=params(46),
         name="first_queries",
-    )(guidance, modulation, arrived, table, flat, own_gain, w_out)
+    )(guidance, modulation, qk_gain, arrived, table, flat, w_out)
     normed_q, keys, values, residual, bias, partial = made
 
     def attend(distance, last):
         return pl.pallas_call(
             functools.partial(query_kernel, head_size, distance, last),
             out_shape=jax.ShapeDtypeStruct((queries, width), F32),
-            in_specs=[SMEM, VMEM] + [HBM] * 8,
+            in_specs=[SMEM, VMEM, VMEM] + [HBM] * 7,
             out_specs=HBM,
             scratch_shapes=[
                 vmem((branches, queries, width), BF16),
@@ -564,19 +556,19 @@
                 vmem(*shapes["values"]),
                 vmem(*shapes["bias"]),
                 vmem((group, width), BF16),
-                vmem((group, 2), F32),
+                vmem((group, 8), F32),
                 vmem((group, width), BF16),
                 vmem((queries, width), F32),
                 vmem((queries, group), BF16),
-                dma((5,)),
+                dma((4,)),
                 dma((branches,)),
                 dma((branches,)),
                 dma((branches,)),
                 dma(()),
             ],
-            compiler_params=params(64),
+            compiler_params=params(46),
             name="more_queries",
-        )(guidance, modulation, normed_q, keys, values, bias, flat, own_gain, w_out, residual)
+        )(guidance, modulation, qk_gain, normed_q, keys, values, bias, flat, w_out, residual)
 
     terms = []
     for distance in range(1, heads):

time: 95.6 us -> 89.9 us (0.940)
  other arithmetic: 5.34 us -> 0.92 us
  Pallas kernels: 33.4 us -> 29.7 us
  waiting for transfers between devices: 22 us -> 23.7 us
    convert_element_type x1, other arithmetic: 2.14 us -> 0.08 us  [on_device(): terms.append(lax.ppermute(partial.astype(jnp.float16), 'head', turn))]
    pallas_call x1, Pallas kernels: 16.3 us -> 14.5 us  [on_device(): pl.pallas_call(functools.partial(first_kernel, senders, head_size), out_s...]
    pallas_call x1, Pallas kernels: 12.8 us -> 11.1 us  [attend(): pl.pallas_call(functools.partial(query_kernel, head_size, distance, last)...]
    all_to_all x1, waiting for transfers between devices: 22 us -> 23.7 us  [on_device(): lax.all_to_all(outgoing.reshape(senders, capacity, width + EXTRA), ('cfg'...]
    another operation x2, other arithmetic: 1.72 us -> 0.36 us
    concatenate x1, other arithmetic: 1.08 us -> 0.08 us  [position_parts(): return jnp.concatenate([top, middle, low], axis=0).astype(BF16)]
    unnamed x6 -> x15, local copies, waits for them, and re-layouts: 5.51 us -> 6.13 us
  transfers between devices with their start and end apart: 2 -> 2, of which waited for: 1 -> 1; matrix products, arithmetic and copies ran while one was open for 7% -> 6% of each run, Pallas kernels for 13% -> 12%
where the time goes in v8:
time: 89.9 us; the launch traced here: 89.5 us
  Pallas kernels  29.7 us (33%)
  waiting for transfers between devices  23.7 us (26%)
  blocking collectives  19.7 us (22%)
  starting transfers between devices  8.96 us (10%)
  local copies, waits for them, and re-layouts  6.21 us (7%)
  other arithmetic  0.92 us (1%)
    all_to_all x1, waiting for transfers between devices, on_device(): lax.all_to_all(outgoing.reshape(senders, capacity, width + EXTRA), ('cfg'...  23.7 us
    all_to_all x1, blocking collectives, on_device(): lax.all_to_all(rows.reshape(senders * heads, share, width // heads), ('cf...  19.7 us
    pallas_call x1, Pallas kernels, on_device(): pl.pallas_call(functools.partial(first_kernel, senders, head_size), out_s...  14.5 us
    pallas_call x1, Pallas kernels, attend(): pl.pallas_call(functools.partial(query_kernel, head_size, distance, last)...  11.1 us
    all_to_all x1, starting transfers between devices, on_device(): lax.all_to_all(outgoing.reshape(senders, capacity, width + EXTRA), ('cfg'...  7.37 us
    unnamed x15, local copies, waits for them, and re-layouts  6.13 us
    pallas_call x1, Pallas kernels, on_device(): pl.pallas_call(functools.partial(place_kernel, senders, capacity), out_sh...  3.01 us
  transfers between devices with their start and end apart: 2, of which 1 were waited for; matrix products, arithmetic and copies ran while one was open for 6% of the time, Pallas kernels for 12%

profile of v8, /device:TPU:0, one launch (start us, length us, event | category | flops | bytes accessed | tf_op | source)
XLA Modules:
  0.0 89.5 jit_solution(9388652073461209644)
XLA Ops:
  0.0 3.0 %place.1 = (bf16[512,1152]{1,0:T(8,128)(2,1)}, f32[1,384]{1,0:T(1,128)}) custom-call(s32[384]{0:T(512)} %windows_hbm.1, s32[3,384]{1,0:T(4,128)} %coords_hbm.1, bf16[384,1024]{1,0:T(8,128)(2,1)} %x_hbm.1), custom_call_target="tpu_custom_call" | custom-call | tf_op jit(solution)/shard_map/place/pallas_call | solution.py:484
  3.0 7.4 %all-to-all-start = ((bf16[16,32,1152]{2,1,0:T(8,128)(2,1)}), bf16[16,32,1152]{2,1,0:T(8,128)(2,1)S(1)}, u32[]{:S(2)}, u32[]{:S(2)}) async-start(bf16[16,32,1152]{2,1,0:T(8,128)(2,1)} %bitcast.12), calls=%async_computation | async-start | bytes 2359296 | tf_op jit(solution)/shard_map/all_to_all | solution.py:501
  10.4 4.7 %copy.9 = bf16[1024,3,512]{0,2,1:T(8,128)(2,1)} copy(bf16[1024,3,512]{2,0,1:T(8,128)(2,1)} %param.12) | data formatting | bytes 6291456 | tf_op args[4]
  15.1 0.3 fusion.3
  15.4 0.1 pad_maximum_fusion.2
  15.4 0.0 copy-start
  15.5 0.0 copy-start.3
  15.5 0.0 copy-start.4
  15.5 0.0 copy-start.5
  15.5 0.2 reduce-precision_convert_fusion.1
  15.7 0.1 pad_maximum_fusion.table_hbm
  15.8 23.7 %all-to-all-done = bf16[16,32,1152]{2,1,0:T(8,128)(2,1)S(1)} async-done(((bf16[16,32,1152]{2,1,0:T(8,128)(2,1)}), bf16[16,32,1152]{2,1,0:T(8,128)(2,1)S(1)}, u32[]{:S(2)}, u32[]{:S(2)}) %all-to-all-start) | async-done | bytes 1179680 | tf_op jit(solution)/shard_map/all_to_all | solution.py:501
  39.5 0.0 copy-done
  39.5 0.0 copy-done.3
  39.5 0.0 copy-done.4
  39.5 0.0 copy-done.5
  39.6 14.5 %first_queries.1 = (bf16[1,3,256,1024]{3,2,1,0:T(8,128)(2,1)S(1)}, bf16[3,512,512]{2,1,0:T(8,128)(2,1)}, bf16[3,512,512]{2,1,0:T(8,128)(2,1)}, f32[256,1024]{1,0...) custom-call(f32[2]{0:T(128)S(1)} %copy-done.5, f32[3,3,1024]{2,1,0:T(4,128)S(1)} %copy-done.3, ...), custom_call_target="tpu_custom_call" | custom-call | tf_op jit(solution)/shard_map/first_queries/pallas_call | solution.py:519
  54.1 0.0 copy-start.1
  54.1 0.1 convert_element_type.18
  54.2 1.6 %collective-permute-start = (f16[256,1024]{1,0:T(8,128)(2,1)S(1)}, f16[256,1024]{1,0:T(8,128)(2,1)S(1)}, u32[]{:S(2)}, u32[]{:S(2)}) collective-permute-start(f16[256,1024]{1,0:T(8,128)(2,1)S(1)} %convert_element_type.18), channel_id=1, source_target_pairs={{0,1},{1,0},{2,3},{3,2},{4,5},{5,4},{6,7},{7,6},{8,9},{9,8},{10,11... | collective-permute-start | bytes 1572872 | tf_op jit(solution)/shard_map/ppermute | solution.py:576
  55.7 0.0 copy-done.1
  55.7 0.0 copy-start.2
  55.7 1.4 %copy-done.2 = bf16[3,512,512]{2,1,0:T(8,128)(2,1)S(1)} copy-done((bf16[3,512,512]{2,1,0:T(8,128)(2,1)S(1)}, bf16[3,512,512]{2,1,0:T(8,128)(2,1)}, u32[]{:S(2)}) %copy-start.2) | copy-done | bytes 1572888
  57.2 11.1 %more_queries.1 = f32[256,1024]{1,0:T(8,128)S(1)} custom-call(f32[2]{0:T(128)S(1)} %copy-done.5, f32[3,3,1024]{2,1,0:T(4,128)S(1)} %copy-done.3, f32[2,512]{1,0:T(2,128)S(1)} %copy-done.4, bf16[1,3,256,1024]{3,2,1,0:T(8,128)(2,1)S(1)} %get-tuple-element.15.normed_q_hbm, bf16[3,512,512]{2,1,0:T(8,128)(2,1)S(1)} %copy-done.1, ...), custom_call_target="tpu_custom_call" | custom-call | tf_op jit(solution)/shard_map/more_queries/pallas_call | solution.py:548
  68.2 0.0 collective-permute-done
  68.3 0.2 add_convert_fusion
  68.5 0.0 copy-start.6
  68.5 0.1 pad_maximum_fusion.1
  68.6 19.7 %all_to_all.10 = bf16[32,16,512]{2,1,0:T(8,128)(2,1)S(1)} all-to-all(bf16[32,16,512]{2,1,0:T(8,128)(2,1)S(1)} %bitcast.11), channel_id=1, replica_groups=mesh['cfg'=2,'vox'=8,'head'=2] {'cfg','vox','head'}, dimensions={0} | all-to-all | bytes 1048576 | tf_op jit(solution)/shard_map/all_to_all | solution.py:588
  88.3 0.0 copy-done.6
  88.3 1.2 %return_rows.1 = bf16[384,512]{1,0:T(8,128)(2,1)} custom-call(f32[1,384]{1,0:T(1,128)S(1)} %copy-done.6, bf16[512,512]{1,0:T(8,128)(2,1)S(1)} %bitcast.8), custom_call_target="tpu_custom_call" | custom-call | tf_op jit(solution)/shard_map/return_rows/pallas_call | solution.py:595
  (3 shorter events, 0.1 us)
Async XLA Ops:
  3.0 36.5 %all-to-all-start = ((bf16[16,32,1152]{2,1,0:T(8,128)(2,1)}), bf16[16,32,1152]{2,1,0:T(8,128)(2,1)S(1)}, u32[]{:S(2)}, u32[]{:S(2)}) async-start(bf16[16,32,1152]{2,1,0:T(8,128)(2,1)} %bitcast.12), calls=%async_computation | async-start | bytes 2359296 | tf_op jit(solution)/shard_map/all_to_all | solution.py:501
  15.4 24.1 %copy-start = (bf16[512,1024]{1,0:T(8,128)(2,1)S(1)}, bf16[512,1024]{1,0:T(8,128)(2,1)}, u32[]{:S(2)}) copy-start(bf16[512,1024]{1,0:T(8,128)(2,1)} %w_out_hbm.3) | copy-start | bytes 3145732
  15.5 24.1 %copy-start.3 = (f32[3,3,1024]{2,1,0:T(4,128)S(1)}, f32[3,3,1024]{2,1,0:T(4,128)}, u32[]{:S(2)}) copy-start(f32[3,3,1024]{2,1,0:T(4,128)} %modulation_ref.3) | copy-start | bytes 110596
  15.5 24.1 %copy-start.4 = (f32[2,512]{1,0:T(2,128)S(1)}, f32[2,512]{1,0:T(2,128)}, u32[]{:S(2)}) copy-start(f32[2,512]{1,0:T(2,128)} %gain_rows_ref.3) | copy-start | bytes 12292
  15.5 24.1 %copy-start.5 = (f32[2]{0:T(128)S(1)}, f32[2]{0:T(128)}, u32[]{:S(2)}) copy-start(f32[2]{0:T(128)} %guidance_ref.3) | copy-start | bytes 28
  54.1 1.7 %copy-start.1 = (bf16[3,512,512]{2,1,0:T(8,128)(2,1)S(1)}, bf16[3,512,512]{2,1,0:T(8,128)(2,1)}, u32[]{:S(2)}) copy-start(bf16[3,512,512]{2,1,0:T(8,128)(2,1)} %get-tuple-element.16.keys_hbm) | copy-start | bytes 4718596
  54.2 14.1 %collective-permute-start = (f16[256,1024]{1,0:T(8,128)(2,1)S(1)}, f16[256,1024]{1,0:T(8,128)(2,1)S(1)}, u32[]{:S(2)}, u32[]{:S(2)}) collective-permute-start(f16[256,1024]{1,0:T(8,128)(2,1)S(1)} %convert_element_type.18), channel_id=1, source_target_pairs={{0,1},{1,0},{2,3},{3,2},{4,5},{5,4},{6,7},{7,6},{8,9},{9,8},{10,11... | collective-permute-start | bytes 1572872 | tf_op jit(solution)/shard_map/ppermute | solution.py:576
  55.7 1.4 %copy-start.2 = (bf16[3,512,512]{2,1,0:T(8,128)(2,1)S(1)}, bf16[3,512,512]{2,1,0:T(8,128)(2,1)}, u32[]{:S(2)}) copy-start(bf16[3,512,512]{2,1,0:T(8,128)(2,1)} %get-tuple-element.17.values_hbm) | copy-start | bytes 4718596
  68.5 19.8 %copy-start.6 = (f32[1,384]{1,0:T(1,128)S(1)}, f32[1,384]{1,0:T(1,128)}, u32[]{:S(2)}) copy-start(f32[1,384]{1,0:T(1,128)} %get-tuple-element.13.placed_ref) | copy-start | bytes 4612

commit v9 on v8

--- a/solution.py
+++ b/solution.py
@@ -178,29 +178,22 @@
     table_hbm,
     w_hbm,
     w_out_hbm,
-    normed_q_hbm,
-    keys_hbm,
-    values_hbm,
-    residual_hbm,
-    bias_hbm,
+    later_q_ref,
+    keys_ref,
+    values_ref,
+    residual_ref,
+    bias_ref,
     sent_ref,
     table_ref,
     w_ref,
     gain_ref,
     w_out_ref,
     normed_ref,
-    normed_q_ref,
-    keys_ref,
-    values_ref,
-    residual_ref,
-    bias_ref,
+    next_q_ref,
     hidden_ref,
     att_ref,
     sum_ref,
     in_sems,
-    out_sems,
-    key_sems,
-    value_sems,
 ):
     loads = copies(
         (
@@ -210,18 +203,10 @@
         ),
         in_sems,
     )
-    stores = copies(
-        (
-            (normed_q_ref.at[pl.ds(1, normed_q_hbm.shape[0])], normed_q_hbm),
-            (bias_ref, bias_hbm),
-            (residual_ref, residual_hbm),
-        ),
-        out_sems,
-    )
     for load in loads:
         load.start()
     branches, slots, width = normed_ref.shape
-    heads, _, queries, _ = normed_q_ref.shape
+    queries, heads = next_q_ref.shape[1], later_q_ref.shape[0] + 1
     group = att_ref.shape[1]
     capacity = slots // senders
     share = queries // senders
@@ -234,7 +219,6 @@
     pick = ((iota((8, EXTRA), 1) == 3)).astype(F32).astype(BF16)
     live = lax.dot_general(pick, extra, NT, preferred_element_type=F32)
     bias_ref[...] = jnp.where(live > 0.5, 0.0, -1e30)
-    stores[1].start()
 
     spots = extra.astype(F32)
     lane = iota((slots, 3 * GRID), 1)
@@ -260,6 +244,7 @@
             normed_ref[b, rows, :] = (normal * stretches[b] + shifts[b]).astype(BF16)
 
     for d in range(heads):
+        normed_q_ref = next_q_ref if d == 0 else later_q_ref.at[d - 1]
         first = lax.rem(me + d + 1, heads) * share
         if share % 16 == 0:
             for s in range(senders):
@@ -268,7 +253,7 @@
                 if d == heads - 1:
                     residual_ref[target, :] = hidden_ref[source, :] * total
                 for b in range(branches):
-                    normed_q_ref[d, b, target, :] = normed_ref[b, source, :]
+                    normed_q_ref[b, target, :] = normed_ref[b, source, :]
         else:
             row = iota((queries, slots), 0)
             wanted_slot = (row // share) * capacity + first + row % share
@@ -282,19 +267,11 @@
                 )
                 residual_ref[...] = picked * total
             for b in range(branches):
-                normed_q_ref[d, b] = dot(chooser.astype(BF16), normed_ref[b]).astype(BF16)
-    stores[0].start()
-    stores[2].start()
+                normed_q_ref[b] = dot(chooser.astype(BF16), normed_ref[b]).astype(BF16)
 
     bias = bias_ref[0:1, :]
     tile = min(256, group)
     loads[1].wait()
-
-    def store(b):
-        return (
-            pltpu.make_async_copy(keys_ref.at[b], keys_hbm.at[b], key_sems.at[b]),
-            pltpu.make_async_copy(values_ref.at[b], values_hbm.at[b], value_sems.at[b]),
-        )
 
     for b in range(branches):
         made = {}
@@ -303,7 +280,7 @@
             features = slice(t * tile, (t + 1) * tile)
             if kind == "query":
                 array = project_query(
-                    normed_q_ref[0, b], w_ref[0, features, :], gain_ref[features, 0:1], head_size
+                    next_q_ref[b], w_ref[0, features, :], gain_ref[features, 0:1], head_size
                 )
             elif kind == "key":
                 array = project_keys(
@@ -338,8 +315,6 @@
             tile,
             head_size,
         )
-        for copy in store(b):
-            copy.start()
         if b == 0:
             loads[2].wait()
         term = dot(att_ref[...], w_out_ref[...]) * (scales[b] * modulation_ref[b, 2:3, :])
@@ -348,11 +323,6 @@
         else:
             sum_ref[...] += term
     sent_ref[...] = sum_ref[...] * SENT_SCALE
-    for copy in stores:
-        copy.wait()
-    for b in range(branches):
-        for copy in store(b):
-            copy.wait()
 
 
 def query_kernel(
@@ -362,76 +332,34 @@
     guidance_ref,
     modulation_ref,
     gain_rows_ref,
-    normed_q_hbm,
-    keys_hbm,
-    values_hbm,
-    bias_hbm,
-    w_hbm,
-    w_out_hbm,
-    start_hbm,
-    out_hbm,
     normed_q_ref,
     keys_ref,
     values_ref,
     bias_ref,
     w_ref,
+    w_out_ref,
+    start_ref,
+    sum_ref,
     gain_ref,
-    w_out_ref,
-    sum_ref,
     att_ref,
-    in_sems,
-    query_sems,
-    key_sems,
-    value_sems,
-    out_sem,
 ):
     branches, _, slots = keys_ref.shape
     group = att_ref.shape[1]
-    loads = copies(
-        (
-            (w_hbm.at[0], w_ref),
-            (bias_hbm, bias_ref),
-            (w_out_hbm, w_out_ref),
-            (start_hbm, sum_ref),
-        ),
-        in_sems,
-    )
-    if not last:
-        loads = loads[:-1]
-
-    def load(b):
-        return (
-            pltpu.make_async_copy(
-                normed_q_hbm.at[distance - 1, b], normed_q_ref.at[b], query_sems.at[b]
-            ),
-            pltpu.make_async_copy(keys_hbm.at[b], keys_ref.at[b], key_sems.at[b]),
-            pltpu.make_async_copy(values_hbm.at[b], values_ref.at[b], value_sems.at[b]),
-        )
-
-    for copy in load(0)[:1] + (loads[0], loads[1]) + load(0)[1:] + tuple(loads[2:]):
-        copy.start()
-    for b in range(1, branches):
-        for copy in load(b):
-            copy.start()
     scales = branch_scales(guidance_ref)
     tile = min(256, group)
-    if not last:
-        sum_ref[...] = jnp.zeros_like(sum_ref)
     gain_ref[...] = gain_columns(gain_rows_ref)
-    for copy in loads[:2]:
-        copy.wait()
     bias = bias_ref[0:1, :]
 
     for b in range(branches):
-        for copy in load(b):
-            copy.wait()
         made = {}
 
         def query(t):
             if t not in made:
                 features = slice(t * tile, (t + 1) * tile)
                 made[t] = project_query(
-                    normed_q_ref[b], w_ref[features, :], gain_ref[features, 0:1], head_size
+                    normed_q_ref[distance - 1, b],
+                    w_ref[0, features, :],
+                    gain_ref[features, 0:1], head_size
                 )
             return made[t]
 
@@ -445,17 +373,13 @@
             tile,
             head_size,
         )
+        term = dot(att_ref[...], w_out_ref[...]) * (scales[b] * modulation_ref[b, 2:3, :])
         if b == 0:
-            for copy in loads[2:]:
-                copy.wait()
-        sum_ref[...] += dot(att_ref[...], w_out_ref[...]) * (
-            scales[b] * modulation_ref[b, 2:3, :]
-        )
+            sum_ref[...] = start_ref[...] + term if last else term
+        else:
+            sum_ref[...] += term
     if not last:
         sum_ref[...] = sum_ref[...] * SENT_SCALE
-    store = pltpu.make_async_copy(sum_ref, out_hbm, out_sem)
-    store.start()
-    store.wait()
 
 
 def return_kernel(placed_ref, rows_ref, out_ref):
@@ -520,26 +444,20 @@
         functools.partial(first_kernel, senders, head_size),
         out_shape=tuple(jax.ShapeDtypeStruct(*shape) for shape in shapes.values()),
         in_specs=[SMEM, VMEM, VMEM, VMEM] + [HBM] * 3,
-        out_specs=(HBM,) * 5 + (VMEM,),
+        out_specs=(VMEM,) * 6,
         scratch_shapes=[
             vmem(table.shape, BF16),
             vmem((3, group, width), BF16),
             vmem((group, 8), F32),
             vmem((group, width), BF16),
             vmem((branches, SLOTS, width), BF16),
-        ]
-        + [vmem((heads, branches, queries, width), BF16)]
-        + [vmem(*shape) for name, shape in shapes.items() if name not in ("normed_q", "sent")]
-        + [
+            vmem((branches, queries, width), BF16),
             vmem((SLOTS, width), F32),
             vmem((queries, group), BF16),
             vmem((queries, width), F32),
             dma((3,)),
-            dma((3,)),
-            dma((branches,)),
-            dma((branches,)),
         ],
-        compiler_params=params(46),
+        compiler_params=params(43),
         name="first_queries",
     )(guidance, modulation, qk_gain, arrived, table, flat, w_out)
     normed_q, keys, values, residual, bias, partial = made
@@ -548,25 +466,10 @@
         return pl.pallas_call(
             functools.partial(query_kernel, head_size, distance, last),
             out_shape=jax.ShapeDtypeStruct((queries, width), F32),
-            in_specs=[SMEM, VMEM, VMEM] + [HBM] * 7,
-            out_specs=HBM,
-            scratch_shapes=[
-                vmem((branches, queries, width), BF16),
-                vmem(*shapes["keys"]),
-                vmem(*shapes["values"]),
-                vmem(*shapes["bias"]),
-                vmem((group, width), BF16),
-                vmem((group, 8), F32),
-                vmem((group, width), BF16),
-                vmem((queries, width), F32),
-                vmem((queries, group), BF16),
-                dma((4,)),
-                dma((branches,)),
-                dma((branches,)),
-                dma((branches,)),
-                dma(()),
-            ],
-            compiler_params=params(46),
+            in_specs=[SMEM] + [VMEM] * 9,
+            out_specs=VMEM,
+            scratch_shapes=[vmem((group, 8), F32), vmem((queries, group), BF16)],
+            compiler_params=params(28),
             name="more_queries",
         )(guidance, modulation, qk_gain, normed_q, keys, values, bias, flat, w_out, residual)
 

time: 89.9 us -> 89.5 us (level)
  waiting for transfers between devices: 23.7 us -> 26.2 us
  Pallas kernels: 29.7 us -> 27.5 us
  local copies, waits for them, and re-layouts: 6.21 us -> 4.75 us
  blocking collectives: 19.7 us -> 20.8 us
    ppermute x1, waiting for transfers between devices: 0.01 us -> 2.38 us  [on_device(): terms.append(lax.ppermute(partial.astype(jnp.float16), 'head', turn))]
    pallas_call x1, Pallas kernels: 11.1 us -> 9.07 us  [attend(): pl.pallas_call(functools.partial(query_kernel, head_size, distance, last)...]
    unnamed x15 -> x13, local copies, waits for them, and re-layouts: 6.13 us -> 4.68 us
    all_to_all x1, blocking collectives: 19.7 us -> 20.8 us  [on_device(): lax.all_to_all(rows.reshape(senders * heads, share, width // heads), ('cf...]
  transfers between devices with their start and end apart: 2 -> 2, of which waited for: 1 -> 2; matrix products, arithmetic and copies ran while one was open for 6% -> 6% of each run, Pallas kernels for 12% -> 10%
where the time goes in v9:
time: 89.5 us; the launch traced here: 89.2 us
  Pallas kernels  27.5 us (31%)
  waiting for transfers between devices  26.2 us (29%)
  blocking collectives  20.8 us (23%)
  starting transfers between devices  8.96 us (10%)
  local copies, waits for them, and re-layouts  4.75 us (5%)
  other arithmetic  0.92 us (1%)
    all_to_all x1, waiting for transfers between devices, on_device(): lax.all_to_all(outgoing.reshape(senders, capacity, width + EXTRA), ('cfg'...  23.8 us
    all_to_all x1, blocking collectives, on_device(): lax.all_to_all(rows.reshape(senders * heads, share, width // heads), ('cf...  20.8 us
    pallas_call x1, Pallas kernels, on_device(): pl.pallas_call(functools.partial(first_kernel, senders, head_size), out_s...  14.2 us
    pallas_call x1, Pallas kernels, attend(): pl.pallas_call(functools.partial(query_kernel, head_size, distance, last)...  9.07 us
    all_to_all x1, starting transfers between devices, on_device(): lax.all_to_all(outgoing.reshape(senders, capacity, width + EXTRA), ('cfg'...  7.37 us
    unnamed x13, local copies, waits for them, and re-layouts  4.68 us
    pallas_call x1, Pallas kernels, on_device(): pl.pallas_call(functools.partial(place_kernel, senders, capacity), out_sh...  3.02 us
    ppermute x1, waiting for transfers between devices, on_device(): terms.append(lax.ppermute(partial.astype(jnp.float16), 'head', turn))  2.38 us
  transfers between devices with their start and end apart: 2, of which 2 were waited for; matrix products, arithmetic and copies ran while one was open for 6% of the time, Pallas kernels for 10%

profile of v9, /device:TPU:0, one launch (start us, length us, event | category | flops | bytes accessed | tf_op | source)
XLA Modules:
  0.0 89.2 jit_solution(1559380928327695828)
XLA Ops:
  0.0 3.0 %place.1 = (bf16[512,1152]{1,0:T(8,128)(2,1)}, f32[1,384]{1,0:T(1,128)}) custom-call(s32[384]{0:T(512)} %windows_hbm.1, s32[3,384]{1,0:T(4,128)} %coords_hbm.1, bf16[384,1024]{1,0:T(8,128)(2,1)} %x_hbm.1), custom_call_target="tpu_custom_call" | custom-call | tf_op jit(solution)/shard_map/place/pallas_call | solution.py:408
  3.0 7.4 %all-to-all-start = ((bf16[16,32,1152]{2,1,0:T(8,128)(2,1)}), bf16[16,32,1152]{2,1,0:T(8,128)(2,1)S(1)}, u32[]{:S(2)}, u32[]{:S(2)}) async-start(bf16[16,32,1152]{2,1,0:T(8,128)(2,1)} %bitcast.12), calls=%async_computation | async-start | bytes 2359296 | tf_op jit(solution)/shard_map/all_to_all | solution.py:425
  10.4 4.6 %copy.9 = bf16[1024,3,512]{0,2,1:T(8,128)(2,1)} copy(bf16[1024,3,512]{2,0,1:T(8,128)(2,1)} %param.12) | data formatting | bytes 6291456 | tf_op args[4]
  15.1 0.3 fusion.3
  15.3 0.1 pad_maximum_fusion.2
  15.4 0.0 copy-start.1
  15.4 0.0 copy-start.2
  15.4 0.0 copy-start.3
  15.4 0.0 copy-start.4
  15.5 0.2 reduce-precision_convert_fusion.1
  15.7 0.1 pad_maximum_fusion.table_hbm
  15.8 23.8 %all-to-all-done = bf16[16,32,1152]{2,1,0:T(8,128)(2,1)S(1)} async-done(((bf16[16,32,1152]{2,1,0:T(8,128)(2,1)}), bf16[16,32,1152]{2,1,0:T(8,128)(2,1)S(1)}, u32[]{:S(2)}, u32[]{:S(2)}) %all-to-all-start) | async-done | bytes 1179680 | tf_op jit(solution)/shard_map/all_to_all | solution.py:425
  39.5 0.0 copy-done.1
  39.5 0.0 copy-done.2
  39.5 0.0 copy-done.3
  39.6 0.0 copy-done.4
  39.6 0.0 copy-start
  39.6 14.2 %first_queries.1 = (bf16[1,3,256,1024]{3,2,1,0:T(8,128)(2,1)S(1)}, bf16[3,512,512]{2,1,0:T(8,128)(2,1)S(1)}, bf16[3,512,512]{2,1,0:T(8,128)(2,1)S(1)}, f32[256,1...) custom-call(f32[2]{0:T(128)S(1)} %copy-done.4, f32[3,3,1024]{2,1,0:T(4,128)S(1)} %copy-done.2, ...), custom_call_target="tpu_custom_call" | custom-call | tf_op jit(solution)/shard_map/first_queries/pallas_call | solution.py:443
  53.8 0.1 convert_element_type.18
  53.9 1.6 %collective-permute-start = (f16[256,1024]{1,0:T(8,128)(2,1)S(1)}, f16[256,1024]{1,0:T(8,128)(2,1)S(1)}, u32[]{:S(2)}, u32[]{:S(2)}) collective-permute-start(f16[256,1024]{1,0:T(8,128)(2,1)S(1)} %convert_element_type.18), channel_id=1, source_target_pairs={{0,1},{1,0},{2,3},{3,2},{4,5},{5,4},{6,7},{7,6},{8,9},{9,8},{10,11... | collective-permute-start | bytes 1572872 | tf_op jit(solution)/shard_map/ppermute | solution.py:479
  55.5 0.0 copy-done
  55.5 9.1 %more_queries.1 = f32[256,1024]{1,0:T(8,128)S(1)} custom-call(f32[2]{0:T(128)S(1)} %copy-done.4, f32[3,3,1024]{2,1,0:T(4,128)S(1)} %copy-done.2, f32[2,512]{1,0:T(2,128)S(1)} %copy-done.3, bf16[1,3,256,1024]{3,2,1,0:T(8,128)(2,1)S(1)} %get-tuple-element.15.normed_q_ref, bf16[3,512,512]{2,1,0:T(8,128)(2,1)S(1)} %get-tuple-element.16.keys_ref, ...), custom_call_target="tpu_custom_call" | custom-call | tf_op jit(solution)/shard_map/more_queries/pallas_call | solution.py:466
  64.5 2.4 %collective-permute-done = f16[256,1024]{1,0:T(8,128)(2,1)S(1)} collective-permute-done((f16[256,1024]{1,0:T(8,128)(2,1)S(1)}, f16[256,1024]{1,0:T(8,128)(2,1)S(1)}, u32[]{:S(2)}, u32[]{:S(2)}) %collective-permute-start) | collective-permute-done | bytes 524320 | tf_op jit(solution)/shard_map/ppermute | solution.py:479
  66.9 0.2 add_convert_fusion
  67.1 0.0 copy-start.5
  67.1 0.1 pad_maximum_fusion.1
  67.2 20.8 %all_to_all.10 = bf16[32,16,512]{2,1,0:T(8,128)(2,1)S(1)} all-to-all(bf16[32,16,512]{2,1,0:T(8,128)(2,1)S(1)} %bitcast.11), channel_id=1, replica_groups=mesh['cfg'=2,'vox'=8,'head'=2] {'cfg','vox','head'}, dimensions={0} | all-to-all | bytes 1048576 | tf_op jit(solution)/shard_map/all_to_all | solution.py:491
  88.0 0.0 copy-done.5
  88.0 1.2 %return_rows.1 = bf16[384,512]{1,0:T(8,128)(2,1)} custom-call(f32[1,384]{1,0:T(1,128)S(1)} %copy-done.5, bf16[512,512]{1,0:T(8,128)(2,1)S(1)} %bitcast.10), custom_call_target="tpu_custom_call" | custom-call | tf_op jit(solution)/shard_map/return_rows/pallas_call | solution.py:498
  (3 shorter events, 0.1 us)
Async XLA Ops:
  3.0 36.5 %all-to-all-start = ((bf16[16,32,1152]{2,1,0:T(8,128)(2,1)}), bf16[16,32,1152]{2,1,0:T(8,128)(2,1)S(1)}, u32[]{:S(2)}, u32[]{:S(2)}) async-start(bf16[16,32,1152]{2,1,0:T(8,128)(2,1)} %bitcast.12), calls=%async_computation | async-start | bytes 2359296 | tf_op jit(solution)/shard_map/all_to_all | solution.py:425
  15.4 24.1 %copy-start.1 = (bf16[512,1024]{1,0:T(8,128)(2,1)S(1)}, bf16[512,1024]{1,0:T(8,128)(2,1)}, u32[]{:S(2)}) copy-start(bf16[512,1024]{1,0:T(8,128)(2,1)} %w_out_ref.1) | copy-start | bytes 3145732
  15.4 24.1 %copy-start.2 = (f32[3,3,1024]{2,1,0:T(4,128)S(1)}, f32[3,3,1024]{2,1,0:T(4,128)}, u32[]{:S(2)}) copy-start(f32[3,3,1024]{2,1,0:T(4,128)} %modulation_ref.3) | copy-start | bytes 110596
  15.4 24.1 %copy-start.3 = (f32[2,512]{1,0:T(2,128)S(1)}, f32[2,512]{1,0:T(2,128)}, u32[]{:S(2)}) copy-start(f32[2,512]{1,0:T(2,128)} %gain_rows_ref.3) | copy-start | bytes 12292
  15.4 24.1 %copy-start.4 = (f32[2]{0:T(128)S(1)}, f32[2]{0:T(128)}, u32[]{:S(2)}) copy-start(f32[2]{0:T(128)} %guidance_ref.3) | copy-start | bytes 28
  39.6 15.9 %copy-start = (bf16[1024,3,512]{0,2,1:T(8,128)(2,1)S(1)}, bf16[1024,3,512]{0,2,1:T(8,128)(2,1)}, u32[]{:S(2)}) copy-start(bf16[1024,3,512]{0,2,1:T(8,128)(2,1)} %copy.9) | copy-start | bytes 9437188
  53.9 13.0 %collective-permute-start = (f16[256,1024]{1,0:T(8,128)(2,1)S(1)}, f16[256,1024]{1,0:T(8,128)(2,1)S(1)}, u32[]{:S(2)}, u32[]{:S(2)}) collective-permute-start(f16[256,1024]{1,0:T(8,128)(2,1)S(1)} %convert_element_type.18), channel_id=1, source_target_pairs={{0,1},{1,0},{2,3},{3,2},{4,5},{5,4},{6,7},{7,6},{8,9},{9,8},{10,11... | collective-permute-start | bytes 1572872 | tf_op jit(solution)/shard_map/ppermute | solution.py:479
  67.1 20.9 %copy-start.5 = (f32[1,384]{1,0:T(1,128)S(1)}, f32[1,384]{1,0:T(1,128)}, u32[]{:S(2)}) copy-start(f32[1,384]{1,0:T(1,128)} %get-tuple-element.13.placed_ref) | copy-start | bytes 4612

commit v10 on v9

--- a/solution.py
+++ b/solution.py
@@ -178,6 +178,7 @@
     table_hbm,
     w_hbm,
     w_out_hbm,
+    half_q_ref,
     later_q_ref,
     keys_ref,
     values_ref,
@@ -206,7 +207,8 @@
     for load in loads:
         load.start()
     branches, slots, width = normed_ref.shape
-    queries, heads = next_q_ref.shape[1], later_q_ref.shape[0] + 1
+    queries, heads = later_q_ref.shape[2], later_q_ref.shape[0] + 1
+    half = queries // 2
     group = att_ref.shape[1]
     capacity = slots // senders
     share = queries // senders
@@ -244,7 +246,14 @@
             normed_ref[b, rows, :] = (normal * stretches[b] + shifts[b]).astype(BF16)
 
     for d in range(heads):
-        normed_q_ref = next_q_ref if d == 0 else later_q_ref.at[d - 1]
+        def put(b, start, rows):
+            if d > 0:
+                later_q_ref[d - 1, b, start : start + rows.shape[0], :] = rows
+            elif start < half:
+                next_q_ref[b, start : start + rows.shape[0], :] = rows
+            else:
+                half_q_ref[0, b, start - half : start - half + rows.shape[0], :] = rows
+
         first = lax.rem(me + d + 1, heads) * share
         if share % 16 == 0:
             for s in range(senders):
@@ -253,7 +262,7 @@
                 if d == heads - 1:
                     residual_ref[target, :] = hidden_ref[source, :] * total
                 for b in range(branches):
-                    normed_q_ref[b, target, :] = normed_ref[b, source, :]
+                    put(b, s * share, normed_ref[b, source, :])
         else:
             row = iota((queries, slots), 0)
             wanted_slot = (row // share) * capacity + first + row % share
@@ -267,7 +276,9 @@
                 )
                 residual_ref[...] = picked * total
             for b in range(branches):
-                normed_q_ref[b] = dot(chooser.astype(BF16), normed_ref[b]).astype(BF16)
+                rows = dot(chooser.astype(BF16), normed_ref[b]).astype(BF16)
+                put(b, 0, rows[:half])
+                put(b, half, rows[half:])
 
     bias = bias_ref[0:1, :]
     tile = min(256, group)
@@ -433,36 +444,38 @@
     table = position_parts(width)
     flat = jnp.transpose(w_qkv, (1, 2, 0))
     shapes = dict(
+        half_q=((1, branches, queries // 2, width), BF16),
         normed_q=((heads - 1, branches, queries, width), BF16),
         keys=((branches, group, SLOTS), BF16),
         values=((branches, SLOTS, group), BF16),
         residual=((queries, width), F32),
         bias=((8, SLOTS), F32),
-        sent=((queries, width), F32),
+        sent=((queries // 2, width), F32),
     )
     made = pl.pallas_call(
         functools.partial(first_kernel, senders, head_size),
         out_shape=tuple(jax.ShapeDtypeStruct(*shape) for shape in shapes.values()),
         in_specs=[SMEM, VMEM, VMEM, VMEM] + [HBM] * 3,
-        out_specs=(VMEM,) * 6,
+        out_specs=(VMEM,) * 7,
         scratch_shapes=[
             vmem(table.shape, BF16),
             vmem((3, group, width), BF16),
             vmem((group, 8), F32),
             vmem((group, width), BF16),
             vmem((branches, SLOTS, width), BF16),
-            vmem((branches, queries, width), BF16),
+            vmem((branches, queries // 2, width), BF16),
             vmem((SLOTS, width), F32),
-            vmem((queries, group), BF16),
-            vmem((queries, width), F32),
+            vmem((queries // 2, group), BF16),
+            vmem((queries // 2, width), F32),
             dma((3,)),
         ],
-        compiler_params=params(43),
+        compiler_params=params(42),
         name="first_queries",
     )(guidance, modulation, qk_gain, arrived, table, flat, w_out)
-    normed_q, keys, values, residual, bias, partial = made
-
-    def attend(distance, last):
+    half_q, normed_q, keys, values, residual, bias, partial = made
+
+    def attend(normed_q, distance, last):
+        queries = normed_q.shape[2]
         return pl.pallas_call(
             functools.partial(query_kernel, head_size, distance, last),
             out_shape=jax.ShapeDtypeStruct((queries, width), F32),
@@ -476,8 +489,13 @@
     terms = []
     for distance in range(1, heads):
         turn = [(h, (h + distance) % heads) for h in range(heads)]
-        terms.append(lax.ppermute(partial.astype(jnp.float16), "head", turn))
-        partial = attend(distance, distance == heads - 1)
+        term = lax.ppermute(partial.astype(jnp.float16), "head", turn)
+        if distance == 1:
+            partial = attend(half_q, 1, False)
+            other = lax.ppermute(partial.astype(jnp.float16), "head", turn)
+            term = jnp.concatenate([term, other], axis=0)
+        terms.append(term)
+        partial = attend(normed_q, distance, distance == heads - 1)
     for term in terms:
         partial = partial + term.astype(F32) * (1.0 / SENT_SCALE)
     columns = width // heads

time: 89.5 us -> 96.1 us (1.074)
  Pallas kernels: 27.5 us -> 34 us
    pallas_call x1 -> x2, Pallas kernels: 9.07 us -> 16.8 us  [attend(): pl.pallas_call(functools.partial(query_kernel, head_size, distance, last)...]
    pallas_call x1, Pallas kernels: 14.2 us -> 13.1 us  [on_device(): pl.pallas_call(functools.partial(first_kernel, senders, head_size), out_s...]
    ppermute x1 -> x2, starting transfers between devices: 1.59 us -> 2.09 us  [the longest x1 1.62 us: on_device(): term = lax.ppermute(partial.astype(jnp.float16), 'head', turn)]
    ppermute x1 -> x2, waiting for transfers between devices: 2.38 us -> 1.89 us  [the longest x1 1.88 us: on_device(): other = lax.ppermute(partial.astype(jnp.float16), 'head', turn)]
  transfers between devices with their start and end apart: 2 -> 3, of which waited for: 2 -> 2; matrix products, arithmetic and copies ran while one was open for 6% -> 6% of each run, Pallas kernels for 10% -> 9%
where the time goes in v10:
time: 96.1 us; the launch traced here: 95.8 us
  Pallas kernels  34 us (35%)
  waiting for transfers between devices  25.6 us (27%)
  blocking collectives  20.8 us (22%)
  starting transfers between devices  9.46 us (10%)
  local copies, waits for them, and re-layouts  4.8 us (5%)
    all_to_all x1, waiting for transfers between devices, on_device(): lax.all_to_all(outgoing.reshape(senders, capacity, width + EXTRA), ('cfg'...  23.7 us
    all_to_all x1, blocking collectives, on_device(): lax.all_to_all(rows.reshape(senders * heads, share, width // heads), ('cf...  20.8 us
    pallas_call x2, Pallas kernels, attend(): pl.pallas_call(functools.partial(query_kernel, head_size, distance, last)...  16.8 us
    pallas_call x1, Pallas kernels, on_device(): pl.pallas_call(functools.partial(first_kernel, senders, head_size), out_s...  13.1 us
    all_to_all x1, starting transfers between devices, on_device(): lax.all_to_all(outgoing.reshape(senders, capacity, width + EXTRA), ('cfg'...  7.37 us
    unnamed x13, local copies, waits for them, and re-layouts  4.73 us
    pallas_call x1, Pallas kernels, on_device(): pl.pallas_call(functools.partial(place_kernel, senders, capacity), out_sh...  3.01 us
  transfers between devices with their start and end apart: 3, of which 2 were waited for; matrix products, arithmetic and copies ran while one was open for 6% of the time, Pallas kernels for 9%

profile of v10, /device:TPU:0, one launch (start us, length us, event | category | flops | bytes accessed | tf_op | source)
XLA Modules:
  0.0 95.8 jit_solution(3800887313873812498)
XLA Ops:
  0.0 3.0 %place.1 = (bf16[512,1152]{1,0:T(8,128)(2,1)}, f32[1,384]{1,0:T(1,128)}) custom-call(s32[384]{0:T(512)} %windows_hbm.1, s32[3,384]{1,0:T(4,128)} %coords_hbm.1, bf16[384,1024]{1,0:T(8,128)(2,1)} %x_hbm.1), custom_call_target="tpu_custom_call" | custom-call | tf_op jit(solution)/shard_map/place/pallas_call | solution.py:419
  3.0 7.4 %all-to-all-start = ((bf16[16,32,1152]{2,1,0:T(8,128)(2,1)}), bf16[16,32,1152]{2,1,0:T(8,128)(2,1)S(1)}, u32[]{:S(2)}, u32[]{:S(2)}) async-start(bf16[16,32,1152]{2,1,0:T(8,128)(2,1)} %bitcast.13), calls=%async_computation | async-start | bytes 2359296 | tf_op jit(solution)/shard_map/all_to_all | solution.py:436
  10.4 4.7 %copy.9 = bf16[1024,3,512]{0,2,1:T(8,128)(2,1)} copy(bf16[1024,3,512]{2,0,1:T(8,128)(2,1)} %param.12) | data formatting | bytes 6291456 | tf_op args[4]
  15.1 0.3 fusion.3
  15.4 0.1 pad_maximum_fusion.2
  15.4 0.0 copy-start.1
  15.5 0.0 copy-start.2
  15.5 0.0 copy-start.3
  15.5 0.0 copy-start.4
  15.5 0.2 reduce-precision_convert_fusion.1
  15.7 0.1 pad_maximum_fusion.table_hbm
  15.8 23.7 %all-to-all-done = bf16[16,32,1152]{2,1,0:T(8,128)(2,1)S(1)} async-done(((bf16[16,32,1152]{2,1,0:T(8,128)(2,1)}), bf16[16,32,1152]{2,1,0:T(8,128)(2,1)S(1)}, u32[]{:S(2)}, u32[]{:S(2)}) %all-to-all-start) | async-done | bytes 1179680 | tf_op jit(solution)/shard_map/all_to_all | solution.py:436
  39.5 0.0 copy-done.1
  39.5 0.0 copy-done.2
  39.5 0.0 copy-done.3
  39.5 0.0 copy-done.4
  39.6 0.0 copy-start
  39.6 13.1 %first_queries.1 = (bf16[1,3,128,1024]{3,2,1,0:T(8,128)(2,1)S(1)}, bf16[1,3,256,1024]{3,2,1,0:T(8,128)(2,1)S(1)}, bf16[3,512,512]{2,1,0:T(8,128)(2,1)S(1)}, bf16...) custom-call(f32[2]{0:T(128)S(1)} %copy-done.4, ...), custom_call_target="tpu_custom_call" | custom-call | tf_op jit(solution)/shard_map/first_queries/pallas_call | solution.py:455
  52.7 0.0 copy-done
  52.7 7.7 %more_queries.3 = f32[128,1024]{1,0:T(8,128)S(1)} custom-call(f32[2]{0:T(128)S(1)} %copy-done.4, f32[3,3,1024]{2,1,0:T(4,128)S(1)} %copy-done.2, f32[2,512]{1,0:T(2,128)S(1)} %copy-done.3, bf16[1,3,128,1024]{3,2,1,0:T(8,128)(2,1)S(1)} %get-tuple-element.22.normed_q_ref, bf16[3,512,512]{2,1,0:T(8,128)(2,1)S(1)} %get-tuple-element.17.keys_ref, ...), custom_call_target="tpu_custom_call" | custom-call | tf_op jit(solution)/shard_map/more_queries/pallas_call | solution.py:479
  60.5 1.6 %collective-permute-start = (f16[128,1024]{1,0:T(8,128)(2,1)S(1)}, f16[128,1024]{1,0:T(8,128)(2,1)S(1)}, u32[]{:S(2)}, u32[]{:S(2)}) collective-permute-start(f16[128,1024]{1,0:T(8,128)(2,1)S(1)} %convert_element_type.21), channel_id=1, source_target_pairs={{0,1},{1,0},{2,3},{3,2},{4,5},{5,4},{6,7},{7,6},{8,9},{9,8},{10,11... | collective-permute-start | bytes 786440 | tf_op jit(solution)/shard_map/ppermute | solution.py:492
  62.1 0.5 collective-permute-start.1
  62.6 9.1 %more_queries.2 = f32[256,1024]{1,0:T(8,128)S(1)} custom-call(f32[2]{0:T(128)S(1)} %copy-done.4, f32[3,3,1024]{2,1,0:T(4,128)S(1)} %copy-done.2, f32[2,512]{1,0:T(2,128)S(1)} %copy-done.3, bf16[1,3,256,1024]{3,2,1,0:T(8,128)(2,1)S(1)} %get-tuple-element.16.normed_q_ref, bf16[3,512,512]{2,1,0:T(8,128)(2,1)S(1)} %get-tuple-element.17.keys_ref, ...), custom_call_target="tpu_custom_call" | custom-call | tf_op jit(solution)/shard_map/more_queries/pallas_call | solution.py:479
  71.6 0.0 collective-permute-done
  71.6 1.9 %collective-permute-done.1 = f16[128,1024]{1,0:T(8,128)(2,1)S(1)} collective-permute-done((f16[128,1024]{1,0:T(8,128)(2,1)S(1)}, f16[128,1024]{1,0:T(8,128)(2,1)S(1)}, u32[]{:S(2)}, u32[]{:S(2)}) %collective-permute-start.1) | collective-permute-done | bytes 262176 | tf_op jit(solution)/shard_map/ppermute | solution.py:495
  73.5 0.2 add_convert_fusion
  73.8 0.0 copy-start.5
  73.8 0.1 pad_maximum_fusion.1
  73.9 20.8 %all_to_all.10 = bf16[32,16,512]{2,1,0:T(8,128)(2,1)S(1)} all-to-all(bf16[32,16,512]{2,1,0:T(8,128)(2,1)S(1)} %bitcast.12), channel_id=1, replica_groups=mesh['cfg'=2,'vox'=8,'head'=2] {'cfg','vox','head'}, dimensions={0} | all-to-all | bytes 1048576 | tf_op jit(solution)/shard_map/all_to_all | solution.py:509
  94.7 0.0 copy-done.5
  94.7 1.2 %return_rows.1 = bf16[384,512]{1,0:T(8,128)(2,1)} custom-call(f32[1,384]{1,0:T(1,128)S(1)} %copy-done.5, bf16[512,512]{1,0:T(8,128)(2,1)S(1)} %bitcast.11), custom_call_target="tpu_custom_call" | custom-call | tf_op jit(solution)/shard_map/return_rows/pallas_call | solution.py:516
  (5 shorter events, 0.1 us)
Async XLA Ops:
  3.0 36.5 %all-to-all-start = ((bf16[16,32,1152]{2,1,0:T(8,128)(2,1)}), bf16[16,32,1152]{2,1,0:T(8,128)(2,1)S(1)}, u32[]{:S(2)}, u32[]{:S(2)}) async-start(bf16[16,32,1152]{2,1,0:T(8,128)(2,1)} %bitcast.13), calls=%async_computation | async-start | bytes 2359296 | tf_op jit(solution)/shard_map/all_to_all | solution.py:436
  15.4 24.1 %copy-start.1 = (bf16[512,1024]{1,0:T(8,128)(2,1)S(1)}, bf16[512,1024]{1,0:T(8,128)(2,1)}, u32[]{:S(2)}) copy-start(bf16[512,1024]{1,0:T(8,128)(2,1)} %w_out_ref.3) | copy-start | bytes 3145732
  15.5 24.1 %copy-start.2 = (f32[3,3,1024]{2,1,0:T(4,128)S(1)}, f32[3,3,1024]{2,1,0:T(4,128)}, u32[]{:S(2)}) copy-start(f32[3,3,1024]{2,1,0:T(4,128)} %modulation_ref.5) | copy-start | bytes 110596
  15.5 24.1 %copy-start.3 = (f32[2,512]{1,0:T(2,128)S(1)}, f32[2,512]{1,0:T(2,128)}, u32[]{:S(2)}) copy-start(f32[2,512]{1,0:T(2,128)} %gain_rows_ref.5) | copy-start | bytes 12292
  15.5 24.1 %copy-start.4 = (f32[2]{0:T(128)S(1)}, f32[2]{0:T(128)}, u32[]{:S(2)}) copy-start(f32[2]{0:T(128)} %guidance_ref.5) | copy-start | bytes 28
  39.6 13.1 %copy-start = (bf16[1024,3,512]{0,2,1:T(8,128)(2,1)S(1)}, bf16[1024,3,512]{0,2,1:T(8,128)(2,1)}, u32[]{:S(2)}) copy-start(bf16[1024,3,512]{0,2,1:T(8,128)(2,1)} %copy.9) | copy-start | bytes 9437188
  60.5 11.2 %collective-permute-start = (f16[128,1024]{1,0:T(8,128)(2,1)S(1)}, f16[128,1024]{1,0:T(8,128)(2,1)S(1)}, u32[]{:S(2)}, u32[]{:S(2)}) collective-permute-start(f16[128,1024]{1,0:T(8,128)(2,1)S(1)} %convert_element_type.21), channel_id=1, source_target_pairs={{0,1},{1,0},{2,3},{3,2},{4,5},{5,4},{6,7},{7,6},{8,9},{9,8},{10,11... | collective-permute-start | bytes 786440 | tf_op jit(solution)/shard_map/ppermute | solution.py:492
  62.1 11.4 %collective-permute-start.1 = (f16[128,1024]{1,0:T(8,128)(2,1)S(1)}, f16[128,1024]{1,0:T(8,128)(2,1)S(1)}, u32[]{:S(2)}, u32[]{:S(2)}) collective-permute-start(f16[128,1024]{1,0:T(8,128)(2,1)S(1)} %convert_element_type.22), channel_id=1, source_target_pairs={{0,1},{1,0},{2,3},{3,2},{4,5},{5,4},{6,7},{7,6},{8,9},{9,8},{10,11... | collective-permute-start | bytes 786440 | tf_op jit(solution)/shard_map/ppermute | solution.py:495
  73.8 20.9 %copy-start.5 = (f32[1,384]{1,0:T(1,128)S(1)}, f32[1,384]{1,0:T(1,128)}, u32[]{:S(2)}) copy-start(f32[1,384]{1,0:T(1,128)} %get-tuple-element.14.placed_ref) | copy-start | bytes 4612

commit v11 on v9

--- a/solution.py
+++ b/solution.py
@@ -320,9 +320,10 @@
         term = dot(att_ref[...], w_out_ref[...]) * (scales[b] * modulation_ref[b, 2:3, :])
         if b == 0:
             sum_ref[...] = term
+        elif b < branches - 1:
+            sum_ref[...] += term
         else:
-            sum_ref[...] += term
-    sent_ref[...] = sum_ref[...] * SENT_SCALE
+            sent_ref[...] = (sum_ref[...] + term) * SENT_SCALE
 
 
 def query_kernel(

time: 89.5 us -> 89.5 us (level)
  no operation moved by 1% of the time
where the time goes in v11:
time: 89.5 us; the launch traced here: 89.2 us
  Pallas kernels  27.5 us (31%)
  waiting for transfers between devices  26.2 us (29%)
  blocking collectives  20.8 us (23%)
  starting transfers between devices  8.96 us (10%)
  local copies, waits for them, and re-layouts  4.75 us (5%)
  other arithmetic  0.92 us (1%)
    all_to_all x1, waiting for transfers between devices, on_device(): lax.all_to_all(outgoing.reshape(senders, capacity, width + EXTRA), ('cfg'...  23.8 us
    all_to_all x1, blocking collectives, on_device(): lax.all_to_all(rows.reshape(senders * heads, share, width // heads), ('cf...  20.8 us
    pallas_call x1, Pallas kernels, on_device(): pl.pallas_call(functools.partial(first_kernel, senders, head_size), out_s...  14.2 us
    pallas_call x1, Pallas kernels, attend(): pl.pallas_call(functools.partial(query_kernel, head_size, distance, last)...  9.07 us
    all_to_all x1, starting transfers between devices, on_device(): lax.all_to_all(outgoing.reshape(senders, capacity, width + EXTRA), ('cfg'...  7.37 us
    unnamed x13, local copies, waits for them, and re-layouts  4.68 us
    pallas_call x1, Pallas kernels, on_device(): pl.pallas_call(functools.partial(place_kernel, senders, capacity), out_sh...  3.02 us
    ppermute x1, waiting for transfers between devices, on_device(): terms.append(lax.ppermute(partial.astype(jnp.float16), 'head', turn))  2.38 us
  transfers between devices with their start and end apart: 2, of which 2 were waited for; matrix products, arithmetic and copies ran while one was open for 6% of the time, Pallas kernels for 10%

profile of v11, /device:TPU:0, one launch (start us, length us, event | category | flops | bytes accessed | tf_op | source)
XLA Modules:
  0.0 89.2 jit_solution(1559380928327695828)
XLA Ops:
  0.0 3.0 %place.1 = (bf16[512,1152]{1,0:T(8,128)(2,1)}, f32[1,384]{1,0:T(1,128)}) custom-call(s32[384]{0:T(512)} %windows_hbm.1, s32[3,384]{1,0:T(4,128)} %coords_hbm.1, bf16[384,1024]{1,0:T(8,128)(2,1)} %x_hbm.1), custom_call_target="tpu_custom_call" | custom-call | tf_op jit(solution)/shard_map/place/pallas_call | solution.py:409
  3.0 7.4 %all-to-all-start = ((bf16[16,32,1152]{2,1,0:T(8,128)(2,1)}), bf16[16,32,1152]{2,1,0:T(8,128)(2,1)S(1)}, u32[]{:S(2)}, u32[]{:S(2)}) async-start(bf16[16,32,1152]{2,1,0:T(8,128)(2,1)} %bitcast.12), calls=%async_computation | async-start | bytes 2359296 | tf_op jit(solution)/shard_map/all_to_all | solution.py:426
  10.4 4.6 %copy.9 = bf16[1024,3,512]{0,2,1:T(8,128)(2,1)} copy(bf16[1024,3,512]{2,0,1:T(8,128)(2,1)} %param.12) | data formatting | bytes 6291456 | tf_op args[4]
  15.1 0.3 fusion.3
  15.3 0.1 pad_maximum_fusion.2
  15.4 0.0 copy-start.1
  15.4 0.0 copy-start.2
  15.4 0.0 copy-start.3
  15.4 0.0 copy-start.4
  15.5 0.2 reduce-precision_convert_fusion.1
  15.7 0.1 pad_maximum_fusion.table_hbm
  15.8 23.8 %all-to-all-done = bf16[16,32,1152]{2,1,0:T(8,128)(2,1)S(1)} async-done(((bf16[16,32,1152]{2,1,0:T(8,128)(2,1)}), bf16[16,32,1152]{2,1,0:T(8,128)(2,1)S(1)}, u32[]{:S(2)}, u32[]{:S(2)}) %all-to-all-start) | async-done | bytes 1179680 | tf_op jit(solution)/shard_map/all_to_all | solution.py:426
  39.5 0.0 copy-done.1
  39.5 0.0 copy-done.2
  39.5 0.0 copy-done.3
  39.6 0.0 copy-done.4
  39.6 0.0 copy-start
  39.6 14.2 %first_queries.1 = (bf16[1,3,256,1024]{3,2,1,0:T(8,128)(2,1)S(1)}, bf16[3,512,512]{2,1,0:T(8,128)(2,1)S(1)}, bf16[3,512,512]{2,1,0:T(8,128)(2,1)S(1)}, f32[256,1...) custom-call(f32[2]{0:T(128)S(1)} %copy-done.4, f32[3,3,1024]{2,1,0:T(4,128)S(1)} %copy-done.2, ...), custom_call_target="tpu_custom_call" | custom-call | tf_op jit(solution)/shard_map/first_queries/pallas_call | solution.py:444
  53.8 0.1 convert_element_type.18
  53.9 1.6 %collective-permute-start = (f16[256,1024]{1,0:T(8,128)(2,1)S(1)}, f16[256,1024]{1,0:T(8,128)(2,1)S(1)}, u32[]{:S(2)}, u32[]{:S(2)}) collective-permute-start(f16[256,1024]{1,0:T(8,128)(2,1)S(1)} %convert_element_type.18), channel_id=1, source_target_pairs={{0,1},{1,0},{2,3},{3,2},{4,5},{5,4},{6,7},{7,6},{8,9},{9,8},{10,11... | collective-permute-start | bytes 1572872 | tf_op jit(solution)/shard_map/ppermute | solution.py:480
  55.5 0.0 copy-done
  55.5 9.1 %more_queries.1 = f32[256,1024]{1,0:T(8,128)S(1)} custom-call(f32[2]{0:T(128)S(1)} %copy-done.4, f32[3,3,1024]{2,1,0:T(4,128)S(1)} %copy-done.2, f32[2,512]{1,0:T(2,128)S(1)} %copy-done.3, bf16[1,3,256,1024]{3,2,1,0:T(8,128)(2,1)S(1)} %get-tuple-element.15.normed_q_ref, bf16[3,512,512]{2,1,0:T(8,128)(2,1)S(1)} %get-tuple-element.16.keys_ref, ...), custom_call_target="tpu_custom_call" | custom-call | tf_op jit(solution)/shard_map/more_queries/pallas_call | solution.py:467
  64.5 2.4 %collective-permute-done = f16[256,1024]{1,0:T(8,128)(2,1)S(1)} collective-permute-done((f16[256,1024]{1,0:T(8,128)(2,1)S(1)}, f16[256,1024]{1,0:T(8,128)(2,1)S(1)}, u32[]{:S(2)}, u32[]{:S(2)}) %collective-permute-start) | collective-permute-done | bytes 524320 | tf_op jit(solution)/shard_map/ppermute | solution.py:480
  66.9 0.2 add_convert_fusion
  67.1 0.0 copy-start.5
  67.1 0.1 pad_maximum_fusion.1
  67.2 20.8 %all_to_all.10 = bf16[32,16,512]{2,1,0:T(8,128)(2,1)S(1)} all-to-all(bf16[32,16,512]{2,1,0:T(8,128)(2,1)S(1)} %bitcast.11), channel_id=1, replica_groups=mesh['cfg'=2,'vox'=8,'head'=2] {'cfg','vox','head'}, dimensions={0} | all-to-all | bytes 1048576 | tf_op jit(solution)/shard_map/all_to_all | solution.py:492
  88.0 0.0 copy-done.5
  88.0 1.2 %return_rows.1 = bf16[384,512]{1,0:T(8,128)(2,1)} custom-call(f32[1,384]{1,0:T(1,128)S(1)} %copy-done.5, bf16[512,512]{1,0:T(8,128)(2,1)S(1)} %bitcast.10), custom_call_target="tpu_custom_call" | custom-call | tf_op jit(solution)/shard_map/return_rows/pallas_call | solution.py:499
  (3 shorter events, 0.1 us)
Async XLA Ops:
  3.0 36.5 %all-to-all-start = ((bf16[16,32,1152]{2,1,0:T(8,128)(2,1)}), bf16[16,32,1152]{2,1,0:T(8,128)(2,1)S(1)}, u32[]{:S(2)}, u32[]{:S(2)}) async-start(bf16[16,32,1152]{2,1,0:T(8,128)(2,1)} %bitcast.12), calls=%async_computation | async-start | bytes 2359296 | tf_op jit(solution)/shard_map/all_to_all | solution.py:426
  15.4 24.1 %copy-start.1 = (bf16[512,1024]{1,0:T(8,128)(2,1)S(1)}, bf16[512,1024]{1,0:T(8,128)(2,1)}, u32[]{:S(2)}) copy-start(bf16[512,1024]{1,0:T(8,128)(2,1)} %w_out_ref.1) | copy-start | bytes 3145732
  15.4 24.1 %copy-start.2 = (f32[3,3,1024]{2,1,0:T(4,128)S(1)}, f32[3,3,1024]{2,1,0:T(4,128)}, u32[]{:S(2)}) copy-start(f32[3,3,1024]{2,1,0:T(4,128)} %modulation_ref.3) | copy-start | bytes 110596
  15.4 24.1 %copy-start.3 = (f32[2,512]{1,0:T(2,128)S(1)}, f32[2,512]{1,0:T(2,128)}, u32[]{:S(2)}) copy-start(f32[2,512]{1,0:T(2,128)} %gain_rows_ref.3) | copy-start | bytes 12292
  15.4 24.1 %copy-start.4 = (f32[2]{0:T(128)S(1)}, f32[2]{0:T(128)}, u32[]{:S(2)}) copy-start(f32[2]{0:T(128)} %guidance_ref.3) | copy-start | bytes 28
  39.6 15.9 %copy-start = (bf16[1024,3,512]{0,2,1:T(8,128)(2,1)S(1)}, bf16[1024,3,512]{0,2,1:T(8,128)(2,1)}, u32[]{:S(2)}) copy-start(bf16[1024,3,512]{0,2,1:T(8,128)(2,1)} %copy.9) | copy-start | bytes 9437188
  53.9 13.0 %collective-permute-start = (f16[256,1024]{1,0:T(8,128)(2,1)S(1)}, f16[256,1024]{1,0:T(8,128)(2,1)S(1)}, u32[]{:S(2)}, u32[]{:S(2)}) collective-permute-start(f16[256,1024]{1,0:T(8,128)(2,1)S(1)} %convert_element_type.18), channel_id=1, source_target_pairs={{0,1},{1,0},{2,3},{3,2},{4,5},{5,4},{6,7},{7,6},{8,9},{9,8},{10,11... | collective-permute-start | bytes 1572872 | tf_op jit(solution)/shard_map/ppermute | solution.py:480
  67.1 20.9 %copy-start.5 = (f32[1,384]{1,0:T(1,128)S(1)}, f32[1,384]{1,0:T(1,128)}, u32[]{:S(2)}) copy-start(f32[1,384]{1,0:T(1,128)} %get-tuple-element.13.placed_ref) | copy-start | bytes 4612
